TPU v7x, 512 devices: a whole 4x8x8 slice. The times are simulated.
512 devices in a mesh: dp: 32 (over x, z), group: 16 (over y, core).
Axes of the slice: x: 4, y: 8, z: 8, core: 2. Of those that a mesh axis runs over, the one named last changes fastest.
Arguments:
- queries: bfloat16 [24576, 4096], P('dp', 'group'), may hold values from -120 to 120
- passages: bfloat16 [24576, 4096], P('dp', 'group'), may hold values from -120 to 120
- neg_owner: int32 [24576, 8], P('dp'), may hold values from 0 to 31, all different within a row; in each aligned block of 768 rows (0 to 767, 768 to 1535, ...) at most 240 rows name the same one
- neg_row: int32 [24576, 8], P('dp'), may hold values from 0 to 767
- gain: float32 [4096], replicated, may hold values from 0.5 to 1.5
Outputs:
- grad_queries: bfloat16 [24576, 4096], P('dp', 'group')
- grad_passages: bfloat16 [24576, 4096], P('dp', 'group')
- grad_gain: float32 [4096], replicated
- loss: float32 [], replicated
Inputs may be any that keep to these rules, and one draw needn't show every extreme that they name: `neg_owner`: the 8 owners of one query are distinct; among the 768 queries of one data group no owner is named more than 240 times, and that many in every draw.
All inputs are finite; a program needn't handle non-finite values.
Results may differ from a plain program's by a relative error of at most 0.00305.
The roundings to bfloat16 on the way count: a program that leaves them out, or rounds other values in their place, can miss the bound.
Values may be sent and summed in bfloat16 or wider, within the bound.
No kernel may reach another device: no remote copies, remote signals or barrier semaphores. Data moves between devices by JAX's collectives and lax.ppermute only.
A program may use at most 64 MiB of HBM per device.

v0:
```python
import math

import jax
import jax.numpy as jnp
from jax import lax
from jax.sharding import PartitionSpec as P

EPSILON = 1e-06
SOFTNESS_DIVISOR = 0.25


def softmax_rows(scores, near, positive):
    top = jnp.maximum(jnp.max(scores, axis=1), jnp.max(near, axis=1))[:, None]
    total = jnp.sum(jnp.exp(scores - top), axis=1, keepdims=True) + jnp.sum(
        jnp.exp(near - top), axis=1, keepdims=True
    )
    lse = top + jnp.log(total)
    losses = lse[:, 0] - jnp.sum(jnp.where(positive, scores, 0.0), axis=1)
    weights = (jnp.exp(scores - lse) - positive.astype(jnp.float32)).astype(jnp.bfloat16)
    hard_weights = jnp.exp(near - lse).astype(jnp.bfloat16)
    return (weights, hard_weights, losses)


def local(queries, passages, neg_owner, neg_row, gain):
    rows, piece = queries.shape
    negs = neg_owner.shape[1]
    n_data = lax.axis_size("dp")
    n_members = lax.axis_size("group")
    member = lax.axis_index("group")
    hidden_dimension = piece * n_members
    slot_capacity = min(rows, 5 * rows * negs // (4 * n_data))
    multiplier_coefficient = 1.0 / (SOFTNESS_DIVISOR * math.sqrt(hidden_dimension))
    my_gain = lax.dynamic_slice_in_dim(gain, member * piece, piece, 0)
    q_values = queries.astype(jnp.float32)
    p_values = passages.astype(jnp.float32)
    q_square, passage_squares = lax.psum(
        (jnp.sum(q_values * q_values, axis=1), jnp.sum(p_values * p_values, axis=1)), "group"
    )
    q_inverse = lax.rsqrt(q_square / hidden_dimension + EPSILON)[:, None]
    document_reciprocal_norm = lax.rsqrt(passage_squares / hidden_dimension + EPSILON)[:, None]
    q_normed = q_values * q_inverse
    p_normed = p_values * document_reciprocal_norm
    q_emb = (q_normed * my_gain).astype(jnp.bfloat16)
    p_emb = (p_normed * my_gain).astype(jnp.bfloat16)
    owners = neg_owner.reshape(-1)
    owner_hits = (owners[:, None] == jnp.arange(n_data, dtype=jnp.int32)[None, :]).astype(jnp.int32)
    earlier = jnp.cumsum(owner_hits, axis=0) - owner_hits
    slot_of = jnp.sum(earlier * owner_hits, axis=1)
    target = owners * slot_capacity + slot_of
    requested_rows = (
        jnp.zeros((n_data * slot_capacity,), jnp.int32)
        .at[target]
        .set(neg_row.reshape(-1))
        .reshape(n_data, slot_capacity)
    )
    asked = lax.all_to_all(requested_rows, "dp", split_axis=0, concat_axis=0, tiled=True)
    found = jnp.take(p_emb, asked.reshape(-1), axis=0).reshape(asked.shape + (piece,))
    received_block = lax.all_to_all(found, "dp", split_axis=0, concat_axis=0, tiled=True)
    hard = jnp.take(received_block.reshape(-1, piece), target, axis=0).reshape(rows, negs, piece)
    partial_value = (
        jnp.dot(q_emb, p_emb.T, preferred_element_type=jnp.float32) * multiplier_coefficient
    )
    near_part = (
        jnp.einsum("qd,qkd->qk", q_emb, hard, preferred_element_type=jnp.float32)
        * multiplier_coefficient
    )
    share = rows // n_members
    first_row = member * share
    scores, near = lax.psum((partial_value, near_part), "group")
    positive = (
        jnp.arange(rows, dtype=jnp.int32)[None, :] == jnp.arange(rows, dtype=jnp.int32)[:, None]
    )
    weights, hard_weights, losses = softmax_rows(scores, near, positive)
    loss_part = jnp.sum(lax.dynamic_slice_in_dim(losses, first_row, share, 0))
    grad_q = (
        jnp.dot(weights, p_emb, preferred_element_type=jnp.float32)
        + jnp.einsum("qk,qkd->qd", hard_weights, hard, preferred_element_type=jnp.float32)
    ) * multiplier_coefficient
    grad_p = (
        jnp.einsum("qg,qd->gd", weights, q_emb, preferred_element_type=jnp.float32)
        * multiplier_coefficient
    )
    couple_derivatives = (
        (
            (hard_weights.astype(jnp.float32) * multiplier_coefficient)[:, :, None]
            * q_emb.astype(jnp.float32)[:, None, :]
        )
        .astype(jnp.bfloat16)
        .reshape(-1, piece)
    )
    departing_block = (
        jnp.zeros((n_data * slot_capacity, piece), jnp.bfloat16).at[target].set(couple_derivatives)
    )
    returned = lax.all_to_all(
        departing_block.reshape(n_data, slot_capacity, piece),
        "dp",
        split_axis=0,
        concat_axis=0,
        tiled=True,
    )
    select = (asked.reshape(-1)[None, :] == jnp.arange(rows, dtype=jnp.int32)[:, None]).astype(
        jnp.bfloat16
    )
    grad_p = grad_p + jnp.dot(
        select, returned.reshape(-1, piece), preferred_element_type=jnp.float32
    )
    q_inner = grad_q * my_gain
    p_inner = grad_p * my_gain
    q_mean, p_mean = lax.psum(
        (jnp.sum(q_inner * q_normed, axis=1), jnp.sum(p_inner * p_normed, axis=1)), "group"
    )
    grad_queries = (q_inverse * (q_inner - q_normed * (q_mean / hidden_dimension)[:, None])).astype(
        jnp.bfloat16
    )
    grad_passages = (
        document_reciprocal_norm * (p_inner - p_normed * (p_mean / hidden_dimension)[:, None])
    ).astype(jnp.bfloat16)
    gain_part = jnp.sum(grad_q * q_normed, axis=0) + jnp.sum(grad_p * p_normed, axis=0)
    gain_full = lax.dynamic_update_slice_in_dim(
        jnp.zeros((hidden_dimension,), jnp.float32), gain_part, member * piece, 0
    )
    loss_total, gain_total = lax.psum((loss_part, gain_full), ("dp", "group"))
    count = rows * n_data
    return (grad_queries, grad_passages, gain_total / math.sqrt(count), loss_total / count)


def solution(mesh):
    return jax.shard_map(
        local,
        mesh=mesh,
        in_specs=(P("dp", "group"), P("dp", "group"), P("dp", None), P("dp", None), P()),
        out_specs=(P("dp", "group"), P("dp", "group"), P(), P()),
        check_vma=False,
    )
```

profile of v0, /device:TPU:1, one launch (start us, length us, event | category | flops | bytes accessed | tf_op | source)
XLA Modules:
  0.0 616.7 jit_solution(1964288203037721149)
XLA Ops:
  7.2 0.7 broadcast_multiply_fusion.1
  7.9 0.9 copy.18
  8.8 0.2 eq.58
  9.0 0.2 reshape.168
  9.4 0.2 mul.174
  9.7 9.4 %reduce-window.6 = s32[32,48,128]{2,1,0:T(8,128)S(1)} reduce-window(s32[32,48,128]{2,1,0:T(8,128)S(1)} %fusion.39, s32[]{:T(128)} %constant.28.clone.1), window={size=1x1x128 pad=0_0x0_0x127_0}, to_apply=%region_6.7 | reduce-window | flops 24969216 | bytes 1572868 | tf_op jit(solution)/shard_map/reduce-window
  19.1 0.8 slice_reduce_fusion
  20.0 0.2 reduce-window.9
  20.2 0.3 broadcast_add_fusion
  20.6 0.2 reshape.197
  20.8 0.4 fusion.37
  21.3 23.0 %scatter_custom_fusion = s32[7680]{0:T(1024)S(1)} fusion(s32[6144]{0:T(1024)S(1)} %bitcast.53, s32[6144]{0:T(1024)S(1)} %reshape.197, s32[]{:T(128)} %constant.28.clone.1), kind=kCustom, calls=%fused_computation.76 | custom fusion | bytes 30724 | tf_op jit(solution)/shard_map/scatter | solution.py:53
  44.3 0.7 all_to_all.12
  45.0 13.7 %all-to-all-start = ((s32[32,1,240]{2,1,0:T(1,128)}), s32[32,1,240]{2,1,0:T(1,128)S(1)}, u32[]{:S(2)}, u32[]{:S(2)}) async-start(s32[32,1,240]{2,1,0:T(1,128)} %all_to_all.12), calls=%async_computation | async-start | bytes 65536 | tf_op jit(solution)/shard_map/all_to_all | solution.py:56
  59.1 25.3 %all-reduce.2 = (f32[768]{0:T(1024)S(1)}, f32[768]{0:T(1024)S(1)}) all-reduce(f32[768]{0:T(1024)S(1)} %fusion.34, f32[768]{0:T(1024)S(1)} %fusion.27), channel_id=1, replica_groups=mesh['dp'=32,'group'=16] {'group'}, use_global_device_ids=true, to_apply=%region_3.0 | all-reduce | flops 1536 | bytes 12288 | tf_op jit(solution)/shard_map/psum | solution.py:36
  84.4 1.4 broadcast_multiply_fusion.5
  85.8 1.2 fusion.47
  87.3 22.1 %gather_fusion = bf16[7680,256]{1,0:T(8,128)(2,1)} fusion(bf16[768,256]{1,0:T(8,128)(2,1)S(1)} %get-tuple-element.24, s32[8192]{0:T(1024)S(1)} %pad_clamp_fusion), kind=kCustom, calls=%fused_computation | custom fusion | bytes 7895040 | tf_op jit(solution)/shard_map/jit(_take)/gather | solution.py:57
  109.3 5.2 broadcast_select_fusion
  114.5 9.3 %all-to-all-start.1 = ((bf16[32,240,256]{2,1,0:T(8,128)(2,1)}), bf16[32,240,256]{2,1,0:T(8,128)(2,1)}, u32[]{:S(2)}, u32[]{:S(2)}) async-start(bf16[32,240,256]{2,1,0:T(8,128)(2,1)} %broadcast_select_fusion), calls=%async_computation.1 | async-start | bytes 7864320 | tf_op jit(solution)/shard_map/all_to_all | solution.py:58
  123.9 2.0 convolution_multiply_fusion
  126.0 0.2 reduce_sum.106
  126.4 0.2 copy.21
  126.7 124.8 %all-reduce.5.cloned.1.call-done = f32[768,768]{1,0:T(8,128)} async-done(((f32[768,768]{1,0:T(8,128)}), f32[768,768]{1,0:T(8,128)}) %all-reduce.5.cloned.1.call-update) | async-done | bytes 2359312 | tf_op jit(solution)/shard_map/psum | solution.py:69
  251.4 2.4 reduce_max.18
  253.8 26.1 %gather_fusion.1 = bf16[6144,256]{1,0:T(8,128)(2,1)} fusion(bf16[7680,256]{1,0:T(8,128)(2,1)} %bitcast.5, s32[6144]{0:T(1024)S(1)} %broadcast_clamp_fusion), kind=kCustom, calls=%fused_computation.1 | custom fusion | bytes 6316032 | tf_op jit(solution)/shard_map/jit(_take)/gather | solution.py:59
  280.0 4.8 fusion.8
  284.8 0.8 broadcast_multiply_fusion
  285.5 50.3 %psum.59 = f32[768,8]{1,0:T(8,128)S(1)} all-reduce(f32[768,8]{1,0:T(8,128)} %broadcast_multiply_fusion), channel_id=1, replica_groups=mesh['dp'=32,'group'=16] {'group'}, use_global_device_ids=true, to_apply=%region_10.11 | all-reduce | flops 6144 | bytes 49152 | tf_op jit(solution)/shard_map/psum | solution.py:69
  336.0 0.7 max.11
  336.7 0.3 exponential_reduce_fusion.1
  337.0 0.7 select_reduce_fusion
  337.8 0.6 fusion.51
  338.4 1.0 convert_multiply_fusion.4
  339.4 1.2 mul.186
  340.5 32.0 %scatter_custom_fusion.1 = bf16[7680,256]{1,0:T(8,128)(2,1)} fusion(s32[6144]{0:T(1024)} %bitcast.55, f32[768,256]{1,0:T(8,128)} %get-tuple-element.20, f32[6144]{0:T(1024)S(1)} %mul.186, bf16[]{:T(256)} %constant.72.clone.1), kind=kCustom, calls=%fused_computation.10 | custom fusion | flops 3145728 | bytes 4743680 | tf_op jit(solution)/shard_map/scatter | solution.py:92
  372.6 10.1 %all-to-all-start.2 = ((bf16[32,240,256]{2,1,0:T(8,128)(2,1)}), bf16[32,240,256]{2,1,0:T(8,128)(2,1)}, u32[]{:S(2)}, u32[]{:S(2)}) async-start(bf16[32,240,256]{2,1,0:T(8,128)(2,1)} %bitcast.49), calls=%async_computation.2 | async-start | bytes 7864320 | tf_op jit(solution)/shard_map/all_to_all | solution.py:94
  382.7 1.4 dynamic-slice_reduce_fusion
  384.1 4.8 fusion.7
  388.9 1.6 fusion.26
  390.6 77.3 %all-to-all-done.2 = bf16[32,240,256]{2,1,0:T(8,128)(2,1)} async-done(((bf16[32,240,256]{2,1,0:T(8,128)(2,1)}), bf16[32,240,256]{2,1,0:T(8,128)(2,1)}, u32[]{:S(2)}, u32[]{:S(2)}) %all-to-all-start.2) | async-done | bytes 3932192 | tf_op jit(solution)/shard_map/all_to_all | solution.py:94
  467.8 5.9 fusion
  473.7 1.9 fusion.33
  475.6 30.4 %all-reduce.1 = (f32[768]{0:T(1024)S(1)}, f32[768]{0:T(1024)S(1)}) all-reduce(f32[768]{0:T(1024)S(1)} %get-tuple-element.9, f32[768]{0:T(1024)S(1)} %get-tuple-element.7), channel_id=1, replica_groups=mesh['dp'=32,'group'=16] {'group'}, use_global_device_ids=true, to_apply=%region_15.16 | all-reduce | flops 1536 | bytes 12288 | tf_op jit(solution)/shard_map/psum | solution.py:109
  506.1 97.1 %all-reduce = (f32[4096]{0:T(1024)S(1)}, f32[]{:T(128)}) all-reduce(f32[4096]{0:T(1024)S(1)} %add_dynamic-update-slice_fusion, f32[]{:T(128)} %dynamic-slice_reduce_fusion), channel_id=1, replica_groups=mesh['dp'=32,'group'=16] {'dp','group'}, use_global_device_ids=true, to_apply=%region_21.22 | all-reduce | flops 4097 | bytes 32776 | tf_op jit(solution)/shard_map/psum | solution.py:122
  603.2 0.6 broadcast_multiply_fusion.2
  603.8 2.2 fusion.25
  606.0 2.2 fusion.32
  (51 shorter events, 1.7 us)
Async XLA Ops:
  8.8 11.7 %copy-start.11 = (s32[768,8]{0,1:T(8,128)S(1)}, s32[768,8]{0,1:T(8,128)}, u32[]{:S(2)}) copy-start(s32[768,8]{0,1:T(8,128)} %param.8) | copy-start | bytes 73732
  9.7 49.0 %copy-start.2 = (bf16[768,256]{1,0:T(8,128)(2,1)S(1)}, bf16[768,256]{1,0:T(8,128)(2,1)}, u32[]{:S(2)}) copy-start(bf16[768,256]{1,0:T(8,128)(2,1)} %param.6) | copy-start | bytes 1179652
  9.7 49.2 %copy-start.1 = (bf16[768,256]{1,0:T(8,128)(2,1)S(1)}, bf16[768,256]{1,0:T(8,128)(2,1)}, u32[]{:S(2)}) copy-start(bf16[768,256]{1,0:T(8,128)(2,1)} %param.5) | copy-start | bytes 1179652
  21.3 105.4 %copy-start.10 = (s32[6144,1]{0,1:T(1,128)}, s32[6144,1]{0,1:T(1,128)S(1)}, u32[]{:S(2)}) copy-start(s32[6144,1]{0,1:T(1,128)S(1)} %compare_select_fusion.1) | copy-start | bytes 73732
  45.0 41.9 %all-to-all-start = ((s32[32,1,240]{2,1,0:T(1,128)}), s32[32,1,240]{2,1,0:T(1,128)S(1)}, u32[]{:S(2)}, u32[]{:S(2)}) async-start(s32[32,1,240]{2,1,0:T(1,128)} %all_to_all.12), calls=%async_computation | async-start | bytes 65536 | tf_op jit(solution)/shard_map/all_to_all | solution.py:56
  87.0 22.3 %copy-start.4 = (s32[32,240]{1,0:T(8,128)}, s32[32,240]{1,0:T(8,128)S(1)}, u32[]{:S(2)}) copy-start(s32[32,240]{1,0:T(8,128)S(1)} %reduce.1) | copy-start | bytes 92164
  114.5 139.3 %all-to-all-start.1 = ((bf16[32,240,256]{2,1,0:T(8,128)(2,1)}), bf16[32,240,256]{2,1,0:T(8,128)(2,1)}, u32[]{:S(2)}, u32[]{:S(2)}) async-start(bf16[32,240,256]{2,1,0:T(8,128)(2,1)} %broadcast_select_fusion), calls=%async_computation.1 | async-start | bytes 7864320 | tf_op jit(solution)/shard_map/all_to_all | solution.py:58
  123.9 2.5 copy-start.6
  123.9 127.5 %all-reduce.5.cloned.1.call-start = ((), (), s32[]{:S(2)}) async-start(), calls=%async_computation.3 | async-start | bytes 4718592 | tf_op jit(solution)/shard_map/psum | solution.py:69
  126.6 153.4 %copy-start.8 = (pred[768,8]{1,0:T(8,128)(4,1)}, pred[768,8]{1,0:T(8,128)(4,1)S(1)}, u32[]{:S(2)}) copy-start(pred[768,8]{1,0:T(8,128)(4,1)S(1)} %copy.21) | copy-start | bytes 18436
  284.7 52.3 %copy-start = (f32[768,768]{1,0:T(8,128)S(1)}, f32[768,768]{1,0:T(8,128)}, u32[]{:S(2)}) copy-start(f32[768,768]{1,0:T(8,128)} %all-reduce.5.cloned.1.call-done) | copy-start | bytes 7077892
  372.5 10.1 %copy-start.5 = (s32[32,240]{1,0:T(8,128)S(1)}, s32[32,240]{1,0:T(8,128)}, u32[]{:S(2)}) copy-start(s32[32,240]{1,0:T(8,128)} %copy-done.4) | copy-start | bytes 92164
  372.5 11.6 %copy-start.7 = (bf16[768,8,1]{1,0,2:T(8,128)(2,1)S(1)}, bf16[768,8,1]{1,0,2:T(8,128)(2,1)}, u32[]{:S(2)}) copy-start(bf16[768,8,1]{1,0,2:T(8,128)(2,1)} %get-tuple-element.23) | copy-start | bytes 36868
  372.5 11.6 %copy-start.9 = (pred[768,8]{1,0:T(8,128)(4,1)S(1)}, pred[768,8]{1,0:T(8,128)(4,1)}, u32[]{:S(2)}) copy-start(pred[768,8]{1,0:T(8,128)(4,1)} %copy-done.8) | copy-start | bytes 18436
  372.6 95.3 %all-to-all-start.2 = ((bf16[32,240,256]{2,1,0:T(8,128)(2,1)}), bf16[32,240,256]{2,1,0:T(8,128)(2,1)}, u32[]{:S(2)}, u32[]{:S(2)}) async-start(bf16[32,240,256]{2,1,0:T(8,128)(2,1)} %bitcast.49), calls=%async_computation.2 | async-start | bytes 7864320 | tf_op jit(solution)/shard_map/all_to_all | solution.py:94
  384.1 4.8 copy-start.12
  467.8 5.9 copy-start.3
Sparse Core Ops, SparseCore 0:
  127.1 124.2 all-reduce.4
where the time goes:
time: 618 us; the launch traced here: 617 us
  blocking collectives  203 us (33%)
  waiting for transfers between devices  202 us (33%)
  local copies, waits for them, and re-layouts  76.9 us (12%)
  other arithmetic  64.5 us (10%)
  starting transfers between devices  33.2 us (5%)
  matrix products  20.9 us (3%)
  between operations  16.2 us (3%)
    psum x1, waiting for transfers between devices, local(): scores, near = lax.psum((partial_value, near_part), 'group')  125 us
    psum x1, blocking collectives, local(): loss_total, gain_total = lax.psum((loss_part, gain_full), ('dp', 'group'))  97.1 us
    all_to_all x1, waiting for transfers between devices, local(): lax.all_to_all(departing_block.reshape(n_data, slot_capacity, piece), 'dp...  77.3 us
    psum x1, blocking collectives, local(): scores, near = lax.psum((partial_value, near_part), 'group')  50.3 us
    scatter x1, other arithmetic, local(): jnp.zeros((n_data * slot_capacity, piece), jnp.bfloat16).at[target]  32 us
    psum x1, blocking collectives, local(): lax.psum((jnp.sum(q_inner * q_normed, axis=1), jnp.sum(p_inner * p_normed...  30.4 us
    gather x1, local copies, waits for them, and re-layouts, local(): jnp.take(received_block.reshape(-1, piece), target, axis=0)  26.1 us
    psum x1, blocking collectives, local(): lax.psum((jnp.sum(q_values * q_values, axis=1), jnp.sum(p_values * p_valu...  25.3 us
  transfers between devices with their start and end apart: 4, of which 2 were waited for; matrix products, arithmetic and copies ran while one was open for 3% of the time, Pallas kernels for 0%

commit v1 on v0

v1 whole, which is shorter than its diff:
```python
import functools
import math

import jax
import jax.numpy as jnp
from jax import lax
from jax.experimental import pallas as pl
from jax.experimental.pallas import tpu as pltpu
from jax.sharding import PartitionSpec as P

EPSILON = 1e-06
SOFTNESS_DIVISOR = 0.25
ABSENT = -1e30
F32 = jnp.float32
BF16 = jnp.bfloat16


def iota(shape, axis):
    return lax.broadcasted_iota(jnp.int32, shape, axis)


def contract(a, b, da, db):
    return lax.dot_general(a, b, (((da,), (db,)), ((), ())), preferred_element_type=F32)


def call(kernel, grid, in_specs, out_specs, out_shape, flops, bytes_accessed, scratch=()):
    return pl.pallas_call(
        kernel,
        grid=(grid,),
        in_specs=in_specs,
        out_specs=out_specs,
        out_shape=out_shape,
        scratch_shapes=list(scratch),
        compiler_params=pltpu.CompilerParams(vmem_limit_bytes=24 * 1024 * 1024),
        cost_estimate=pl.CostEstimate(flops=flops, bytes_accessed=bytes_accessed, transcendentals=0),
    )


def whole(shape):
    return pl.BlockSpec(shape, lambda i: (0,) * len(shape))


def slab(cap, piece):
    return pl.BlockSpec((1, cap, piece), lambda i: (i, 0, 0))


def slots_kernel(cap, owner_ref, row_ref, q_ref, pos_ref, rows_ref, column_ref, slot_ref, asked_ref):
    step = pl.program_id(0)
    negs, rows = owner_ref.shape
    n_data = pos_ref.shape[0]

    @pl.when(step == 0)
    def _():
        ids = iota((n_data, rows), 0)
        asked = jnp.full((n_data, rows), -1, jnp.int32)
        for k in range(negs):
            asked = jnp.where(owner_ref[k : k + 1, :] == ids, row_ref[k : k + 1, :], asked)
        hit = jnp.where(asked >= 0, 1.0, 0.0).astype(BF16)
        before = jnp.where(iota((rows, rows), 0) < iota((rows, rows), 1), 1.0, 0.0).astype(BF16)
        count = contract(hit, before, 1, 0)
        pos_ref[...] = jnp.where(asked >= 0, count.astype(jnp.int32), -1)
        asked_ref[...] = asked
        column_ref[...] = jnp.zeros_like(column_ref)

    pick = jnp.where(iota((cap, rows), 0) == pos_ref[pl.ds(step, 1), :], 1.0, 0.0).astype(BF16)
    slot_ref[0] = contract(pick, q_ref[...], 1, 0).astype(BF16)
    code = asked_ref[pl.ds(step, 1), :] + 1
    part = iota((8, rows), 0)
    digits = jnp.where(part == 0, code >> 5, jnp.where(part == 1, code & 31, 0))
    digits = digits.astype(F32).astype(BF16)
    found = contract(digits, pick, 1, 1)
    rows_ref[0] = found[0:1, :] * 32.0 + found[1:2, :] - 1.0
    column = contract(pick, digits, 1, 1)
    column = column[:, 0:1] * 32.0 + column[:, 1:2] - 1.0
    column_ref[...] += jnp.where(iota(column_ref.shape, 1) == step, column, 0.0)


def make_slots(owner_t, row_t, q_emb, n_data, cap):
    negs, rows = owner_t.shape
    piece = q_emb.shape[1]
    return call(
        functools.partial(slots_kernel, cap),
        n_data,
        [whole((negs, rows)), whole((negs, rows)), whole((rows, piece))],
        [
            whole((n_data, rows)),
            pl.BlockSpec((1, 1, cap), lambda i: (i, 0, 0)),
            whole((cap, n_data)),
            slab(cap, piece),
        ],
        [
            jax.ShapeDtypeStruct((n_data, rows), jnp.int32),
            jax.ShapeDtypeStruct((n_data, 1, cap), F32),
            jax.ShapeDtypeStruct((cap, n_data), F32),
            jax.ShapeDtypeStruct((n_data, cap, piece), BF16),
        ],
        2 * n_data * cap * rows * piece,
        n_data * cap * piece * 2,
        [pltpu.VMEM((n_data, rows), jnp.int32)],
    )(owner_t, row_t, q_emb)


def near_kernel(scale, pos_ref, column_ref, inverse_ref, gain_ref, q_ref, p_ref, slot_ref, near_ref):
    step = pl.program_id(0)
    cap = q_ref.shape[1]
    rows = p_ref.shape[0]
    column = jnp.sum(
        jnp.where(iota(column_ref.shape, 1) == step, column_ref[...], 0.0), axis=1, keepdims=True
    ).astype(jnp.int32)
    match = iota((cap, rows), 1) == column
    raw = contract(jnp.where(match, 1.0, 0.0).astype(BF16), p_ref[...], 1, 0)
    inverse = jnp.sum(jnp.where(match, inverse_ref[pl.ds(step, 1), :], 0.0), axis=1, keepdims=True)
    emb = ((raw * inverse) * gain_ref[...]).astype(BF16)
    slot_ref[0] = emb
    score = jnp.sum(q_ref[0].astype(F32) * emb.astype(F32), axis=1, keepdims=True) * scale
    pos = pos_ref[pl.ds(step, 1), :]
    spread = jnp.sum(jnp.where(iota((cap, rows), 0) == pos, score, 0.0), axis=0, keepdims=True)
    near_ref[pl.ds(step, 1), :] = jnp.where(pos >= 0, spread, ABSENT)


def near_scores(scale, pos, column, inverse_all, gain, q_slots, p_all):
    n_data, cap, piece = q_slots.shape
    rows = pos.shape[1]
    return call(
        functools.partial(near_kernel, scale),
        n_data,
        [
            whole((n_data, rows)),
            whole((cap, n_data)),
            whole((n_data, rows)),
            whole((1, piece)),
            slab(cap, piece),
            pl.BlockSpec((rows, piece), lambda i: (i, 0)),
        ],
        [slab(cap, piece), whole((n_data, rows))],
        [
            jax.ShapeDtypeStruct((n_data, cap, piece), BF16),
            jax.ShapeDtypeStruct((n_data, rows), F32),
        ],
        2 * n_data * cap * rows * piece,
        n_data * rows * piece * 2,
    )(pos, column, inverse_all, gain, q_slots, p_all)


def softmax_kernel(first_ref, scores_ref, near_ref, weights_ref, hard_ref, loss_ref):
    scores = jnp.sum(scores_ref[...], axis=0)
    near = near_ref[...]
    top = jnp.maximum(jnp.max(scores, axis=1, keepdims=True), jnp.max(near, axis=1, keepdims=True))
    total = jnp.sum(jnp.exp(scores - top), axis=1, keepdims=True) + jnp.sum(
        jnp.exp(near - top), axis=1, keepdims=True
    )
    lse = top + jnp.log(total)
    positive = iota(scores.shape, 1) == iota(scores.shape, 0) + first_ref[0]
    diagonal = jnp.sum(jnp.where(positive, scores, 0.0), axis=1, keepdims=True)
    weights_ref[...] = (jnp.exp(scores - lse) - jnp.where(positive, 1.0, 0.0)).astype(BF16)
    hard_ref[...] = jnp.exp(near - lse).astype(BF16)
    loss_ref[...] = jnp.sum(lse - diagonal, axis=0, keepdims=True)


def softmax_share(first, scores, near):
    parts, share, rows = scores.shape
    n_data = near.shape[1]
    return call(
        softmax_kernel,
        1,
        [pl.BlockSpec(memory_space=pltpu.SMEM), whole((parts, share, rows)), whole((share, n_data))],
        [whole((share, rows)), whole((share, n_data)), whole((1, 1))],
        [
            jax.ShapeDtypeStruct((share, rows), BF16),
            jax.ShapeDtypeStruct((share, n_data), BF16),
            jax.ShapeDtypeStruct((1, 1), F32),
        ],
        8 * share * rows,
        parts * share * rows * 4,
    )(first, scores, near)


def weigh_kernel(pos_ref, hard_ref, table_ref):
    step = pl.program_id(0)
    cap = table_ref.shape[0]
    rows = pos_ref.shape[1]

    @pl.when(step == 0)
    def _():
        table_ref[...] = jnp.zeros_like(table_ref)

    match = iota((cap, rows), 0) == pos_ref[pl.ds(step, 1), :]
    column = jnp.sum(jnp.where(match, hard_ref[pl.ds(step, 1), :], 0.0), axis=1, keepdims=True)
    table_ref[...] += jnp.where(iota(table_ref.shape, 1) == step, column, 0.0)


def weigh_slots(pos, hard, cap):
    n_data, rows = pos.shape
    return call(
        weigh_kernel,
        n_data,
        [whole((n_data, rows)), whole((n_data, rows))],
        whole((cap, n_data)),
        jax.ShapeDtypeStruct((cap, n_data), F32),
        4 * n_data * cap * rows,
        n_data * rows * 8,
    )(pos, hard)


def hard_grad_kernel(pos_ref, hard_ref, slot_ref, total_ref):
    step = pl.program_id(0)
    cap = slot_ref.shape[1]
    rows = pos_ref.shape[1]

    @pl.when(step == 0)
    def _():
        total_ref[...] = jnp.zeros_like(total_ref)

    match = iota((cap, rows), 0) == pos_ref[pl.ds(step, 1), :]
    spread = jnp.where(match, hard_ref[pl.ds(step, 1), :], 0.0).astype(BF16)
    total_ref[...] += contract(slot_ref[0], spread, 0, 0)


def hard_grad(pos, hard, p_slots):
    n_data, cap, piece = p_slots.shape
    rows = pos.shape[1]
    return call(
        hard_grad_kernel,
        n_data,
        [whole((n_data, rows)), whole((n_data, rows)), slab(cap, piece)],
        whole((piece, rows)),
        jax.ShapeDtypeStruct((piece, rows), F32),
        2 * n_data * cap * rows * piece,
        n_data * cap * piece * 2,
    )(pos, hard, p_slots)


def pair_kernel(scale, rows_ref, table_ref, q_ref, base_ref, total_ref):
    step = pl.program_id(0)
    cap = q_ref.shape[1]
    rows = total_ref.shape[0]

    @pl.when(step == 0)
    def _():
        total_ref[...] = base_ref[...] * scale

    weight = jnp.sum(
        jnp.where(iota(table_ref.shape, 1) == step, table_ref[...], 0.0), axis=1, keepdims=True
    )
    pairs = ((weight * scale) * q_ref[0].astype(F32)).astype(BF16)
    wanted = rows_ref[pl.ds(step, 1), :].astype(jnp.int32)
    match = jnp.where(iota((rows, cap), 0) == wanted, 1.0, 0.0).astype(BF16)
    total_ref[...] += contract(match, pairs, 1, 0)


def pair_grad(scale, wanted, table, q_received, base):
    n_data, cap, piece = q_received.shape
    rows = base.shape[0]
    return call(
        functools.partial(pair_kernel, scale),
        n_data,
        [whole((n_data, cap)), whole((cap, n_data)), slab(cap, piece), whole((rows, piece))],
        whole((rows, piece)),
        jax.ShapeDtypeStruct((rows, piece), F32),
        2 * n_data * cap * rows * piece,
        n_data * cap * piece * 2,
    )(wanted, table, q_received, base)


def swap(x, axis):
    return lax.all_to_all(x, axis, split_axis=0, concat_axis=0, tiled=True)


def group_total(x, n_members):
    return jnp.sum(lax.all_gather(x, "group", axis=0), axis=0)


def scatter_scores(scores, member, n_members):
    rows = scores.shape[0]
    share = rows // n_members
    half = n_members // 2
    split = scores.reshape(half, 2, share, rows)
    odd = (member % 2) == 1
    keep = jnp.where(odd, split[:, 1], split[:, 0])
    send = jnp.where(odd, split[:, 0], split[:, 1])
    pairs = [(i, i ^ 1) for i in range(n_members)]
    both = keep + lax.ppermute(send, "group", pairs)
    lanes = [[2 * y + core for y in range(half)] for core in range(2)]
    return lax.all_to_all(
        both, "group", split_axis=0, concat_axis=0, tiled=True, axis_index_groups=lanes
    )


def local(queries, passages, neg_owner, neg_row, gain):
    rows, piece = queries.shape
    negs = neg_owner.shape[1]
    n_data = lax.axis_size("dp")
    n_members = lax.axis_size("group")
    member = lax.axis_index("group")
    width = piece * n_members
    cap = min(rows, 5 * rows * negs // (4 * n_data))
    scale = 1.0 / (SOFTNESS_DIVISOR * math.sqrt(width))
    share = rows // n_members
    my_gain = lax.dynamic_slice_in_dim(gain, member * piece, piece, 0)

    p_all = lax.all_gather(passages, "dp", axis=0, tiled=True)

    q_values = queries.astype(F32)
    p_values = passages.astype(F32)
    squares = group_total(
        jnp.stack([jnp.sum(q_values * q_values, axis=1), jnp.sum(p_values * p_values, axis=1)]),
        n_members,
    )
    inverses = lax.rsqrt(squares / width + EPSILON)
    q_inverse, p_inverse = inverses[0][:, None], inverses[1][:, None]
    q_normed = q_values * q_inverse
    p_normed = p_values * p_inverse
    q_emb = (q_normed * my_gain).astype(BF16)
    p_emb = (p_normed * my_gain).astype(BF16)

    inverse_all = swap(jnp.broadcast_to(inverses[1][None, :], (n_data, rows)), "dp")
    pos, row_slots, column, q_slots = make_slots(neg_owner.T, neg_row.T, q_emb, n_data, cap)
    scores_part = contract(q_emb, p_emb, 1, 1) * scale
    scores = scatter_scores(scores_part, member, n_members)

    q_slots_late, p_all = lax.optimization_barrier((q_slots, p_all))
    q_received = swap(q_slots_late, "dp")

    p_slots, near_part = near_scores(
        scale, pos, column, inverse_all, my_gain[None, :], q_slots, p_all
    )
    near = swap(near_part.reshape(n_data, n_members, share).transpose(1, 0, 2), "group")
    near = jnp.maximum(jnp.sum(near, axis=0), ABSENT).T
    first = jnp.full((1,), member * share, jnp.int32)
    weights, hard, loss_part = softmax_share(first, scores, near)

    hard = lax.all_gather(hard, "group", axis=0, tiled=True).T.astype(F32)
    weights = lax.all_gather(weights, "group", axis=0, tiled=True)
    table = weigh_slots(pos, hard, cap)
    sent = jnp.stack([table.T, row_slots[:, 0, :]], axis=1)
    got = swap(sent, "dp")

    grad_q = (
        contract(weights, p_emb, 1, 0) + hard_grad(pos, hard, p_slots).T
    ) * scale
    batch_grad = contract(weights, q_emb, 0, 0)
    grad_p = pair_grad(scale, got[:, 1, :], got[:, 0, :].T, q_received, batch_grad)

    q_inner = grad_q * my_gain
    p_inner = grad_p * my_gain
    q_mean = group_total(jnp.sum(q_inner * q_normed, axis=1), n_members) / width
    p_mean = group_total(jnp.sum(p_inner * p_normed, axis=1), n_members) / width
    grad_queries = (q_inverse * (q_inner - q_normed * q_mean[:, None])).astype(BF16)
    grad_passages = (p_inverse * (p_inner - p_normed * p_mean[:, None])).astype(BF16)

    gain_part = jnp.sum(grad_q * q_normed, axis=0) + jnp.sum(grad_p * p_normed, axis=0)
    last = jnp.concatenate([gain_part, jnp.broadcast_to(loss_part[0], (128,))])
    last = jnp.sum(swap(jnp.broadcast_to(last[None, :], (n_data, piece + 128)), "dp"), axis=0)
    last = lax.all_gather(last, "group", axis=0)
    count = rows * n_data
    return (
        grad_queries,
        grad_passages,
        last[:, :piece].reshape(-1) / math.sqrt(count),
        jnp.sum(last[:, piece]) / count,
    )


def solution(mesh):
    return jax.shard_map(
        local,
        mesh=mesh,
        in_specs=(P("dp", "group"), P("dp", "group"), P("dp", None), P("dp", None), P()),
        out_specs=(P("dp", "group"), P("dp", "group"), P(), P()),
        check_vma=False,
    )
```

time: 618 us -> 425 us (0.69)
  blocking collectives: 203 us -> 98.2 us
  Pallas kernels: 0 us -> 71.6 us
  local copies, waits for them, and re-layouts: 76.9 us -> 18 us
  other arithmetic: 64.5 us -> 11.3 us
  waiting for transfers between devices: 202 us -> 168 us
  matrix products: 20.9 us -> 4.35 us
    psum x4 -> x0, blocking collectives: 203 us -> none  [the longest x1 97.1 us: local(): loss_total, gain_total = lax.psum((loss_part, gain_full), ('dp', 'group'))]
    psum x1 -> x0, waiting for transfers between devices: 125 us -> none  [local(): scores, near = lax.psum((partial_value, near_part), 'group')]
    all_gather x0 -> x2, waiting for transfers between devices: none -> 104 us  [the longest x1 75.4 us: local(): p_all = lax.all_gather(passages, 'dp', axis=0, tiled=True)]
    all_gather x0 -> x5, blocking collectives: none -> 84.4 us  [the longest x3 54.4 us: group_total(): return jnp.sum(lax.all_gather(x, 'group', axis=0), axis=0)]
    pallas_call x0 -> x6, Pallas kernels: none -> 71.6 us  [the longest x1 20.7 us: pair_grad(): call(functools.partial(pair_kernel, scale), n_data, [whole((n_data, cap))...]
    gather x2 -> x0, local copies, waits for them, and re-layouts: 48.2 us -> none  [the longest x1 26.1 us: local(): jnp.take(received_block.reshape(-1, piece), target, axis=0)]
    scatter x1 -> x0, other arithmetic: 32 us -> none  [local(): jnp.zeros((n_data * slot_capacity, piece), jnp.bfloat16).at[target]]
    scatter x1 -> x0, local copies, waits for them, and re-layouts: 23 us -> none  [local(): requested_rows = jnp.zeros((n_data * slot_capacity,), jnp.int32).at[targe...]
  transfers between devices with their start and end apart: 4 -> 8, of which waited for: 2 -> 5; matrix products, arithmetic and copies ran while one was open for 3% -> 4% of each run, Pallas kernels for 0% -> 11%
where the time goes in v1:
time: 425 us; the launch traced here: 424 us
  waiting for transfers between devices  168 us (40%)
  blocking collectives  98.2 us (23%)
  Pallas kernels  71.6 us (17%)
  starting transfers between devices  35.7 us (8%)
  local copies, waits for them, and re-layouts  18 us (4%)
  between operations  16.2 us (4%)
  other arithmetic  11.3 us (3%)
  matrix products  4.35 us (1%)
    all_gather x1, waiting for transfers between devices, local(): p_all = lax.all_gather(passages, 'dp', axis=0, tiled=True)  75.4 us
    all_gather x3, blocking collectives, group_total(): return jnp.sum(lax.all_gather(x, 'group', axis=0), axis=0)  54.4 us
    all_to_all x4, waiting for transfers between devices, swap(): return lax.all_to_all(x, axis, split_axis=0, concat_axis=0, tiled=True)  32.5 us
    all_to_all x1, waiting for transfers between devices, scatter_scores(): lax.all_to_all(both, 'group', split_axis=0, concat_axis=0, tiled=True, ax...  30.3 us
    all_to_all x4, starting transfers between devices, swap(): return lax.all_to_all(x, axis, split_axis=0, concat_axis=0, tiled=True)  29.9 us
    all_gather x1, waiting for transfers between devices, local(): weights = lax.all_gather(weights, 'group', axis=0, tiled=True)  28.9 us
    pallas_call x1, Pallas kernels, pair_grad(): call(functools.partial(pair_kernel, scale), n_data, [whole((n_data, cap))...  20.7 us
    pallas_call x1, Pallas kernels, make_slots(): call(functools.partial(slots_kernel, cap), n_data, [whole((negs, rows)),...  17.8 us
  transfers between devices with their start and end apart: 8, of which 5 were waited for; matrix products, arithmetic and copies ran while one was open for 4% of the time, Pallas kernels for 11%

profile of v1, /device:TPU:1, one launch (start us, length us, event | category | flops | bytes accessed | tf_op | source)
XLA Modules:
  0.0 423.6 jit_solution(1195239920734493513)
XLA Ops:
  7.2 0.7 all-gather.12.cloned.1.call-update
  7.9 1.2 fusion.14
  9.1 1.2 fusion.21
  10.3 21.1 %all-gather.4 = f32[16,2,768]{2,1,0:T(2,128)S(1)} all-gather(f32[1,2,768]{2,1,0:T(2,128)S(1)} %maximum_bitcast_fusion.1), channel_id=2, replica_groups=mesh['dp'=32,'group'=16] {'group'}, dimensions={0}, use_global_device_ids=true | all-gather | bytes 104448 | tf_op jit(solution)/shard_map/all_gather | solution.py:270
  31.5 0.8 broadcast_multiply_fusion.2
  32.5 0.6 convolution_multiply_fusion
  33.1 1.2 select_bitcast_fusion
  34.4 2.1 collective-permute-start
  36.4 0.7 broadcast_in_dim.11
  37.1 10.9 %all-to-all-start.1 = ((f32[32,1,768]{2,1,0:T(1,128)}), f32[32,1,768]{2,1,0:T(1,128)S(1)}, u32[]{:S(2)}, u32[]{:S(2)}) async-start(f32[32,1,768]{2,1,0:T(1,128)} %broadcast_in_dim.11), calls=%async_computation.1 | async-start | bytes 196608 | tf_op jit(solution)/shard_map/all_to_all | solution.py:266
  48.1 17.8 %shard_map.84 = (s32[32,768]{1,0:T(8,128)S(1)}, f32[32,1,240]{2,1,0:T(1,128)S(1)}, f32[240,32]{1,0:T(8,128)S(1)}, bf16[32,240,256]{2,1,0:T(8,128)(2,1)S(1)}) custom-call(s32[8,768]{1,0:T(8,128)S(1)} %bitcast.65, s32[8,768]{1,0:T(8,128)S(1)} %bitcast.66, bf16[768,256]{1,0:T(8,128)(2,1)S(1)} %fusion.8.q_ref), custom_call_target="tpu_custom_call" | custom-call | flops 3019898880 | bytes 3932160 | tf_op jit(solution)/shard_map/pallas_call | solution.py:81
  65.9 1.9 copy-done
  67.8 75.4 %all-gather.12.cloned.1.call-done.p_ref = bf16[24576,256]{1,0:T(8,128)(2,1)} async-done(((bf16[768,256]{1,0:T(8,128)(2,1)}), bf16[24576,256]{1,0:T(8,128)(2,1)}) %all-gather.12.cloned.1.call-update) | async-done | bytes 12582928 | tf_op jit(solution)/shard_map/all_gather | solution.py:301
  143.2 2.1 copy-done.1
  145.3 4.6 %copy-done.2 = bf16[24576,256]{1,0:T(8,128)(2,1)S(1)} copy-done((bf16[24576,256]{1,0:T(8,128)(2,1)S(1)}, bf16[24576,256]{1,0:T(8,128)(2,1)}, u32[]{:S(2)}) %copy-start.2) | copy-done | bytes 12582936
  149.9 15.5 %shard_map.85 = (bf16[32,240,256]{2,1,0:T(8,128)(2,1)S(1)}, f32[32,768]{1,0:T(8,128)S(1)}) custom-call(s32[32,768]{1,0:T(8,128)S(1)} %get-tuple-element.15.pos_ref, f32[240,32]{1,0:T(8,128)S(1)} %get-tuple-element.16.column_ref, f32[32,768]{1,0:T(8,128)S(1)} %bitcast.58, f32[1,256]{1,0:T(1,128)S(1)} %bitcast.62, bf16[32,240,256]{2,1,0:T(8,128)(2,1)S(1)} %copy-done.1, ...), custom_call_target="tpu_custom_call" | custom-call | flops 3019898880 | bytes 12582912 | tf_op jit(solution)/shard_map/pallas_call | solution.py:124
  165.3 1.9 copy-done.3
  167.4 0.9 reshape.66
  168.3 7.8 %all-to-all-start.2 = ((f32[16,1,1536]{2,1,0:T(1,128)}), f32[16,1,1536]{2,1,0:T(1,128)S(1)}, u32[]{:S(2)}, u32[]{:S(2)}) async-start(f32[16,1,1536]{2,1,0:T(1,128)} %reshape.66), calls=%async_computation.2 | async-start | bytes 196608 | tf_op jit(solution)/shard_map/all_to_all | solution.py:266
  176.1 2.5 bitcast_add_fusion
  178.6 6.0 %all-to-all-done.2 = f32[16,1,1536]{2,1,0:T(1,128)S(1)} async-done(((f32[16,1,1536]{2,1,0:T(1,128)}), f32[16,1,1536]{2,1,0:T(1,128)S(1)}, u32[]{:S(2)}, u32[]{:S(2)}) %all-to-all-start.2) | async-done | bytes 98336 | tf_op jit(solution)/shard_map/all_to_all | solution.py:266
  184.6 3.6 all-to-all-start
  188.3 0.5 broadcast.41
  188.8 0.9 reduce.9
  190.0 30.3 %all-to-all-done.scores_ref = f32[8,48,768]{2,1,0:T(8,128)S(1)} async-done(((f32[8,48,768]{2,1,0:T(8,128)}), f32[8,48,768]{2,1,0:T(8,128)S(1)}, u32[]{:S(2)}, u32[]{:S(2)}) %all-to-all-start) | async-done | bytes 1179680 | tf_op jit(solution)/shard_map/all_to_all | solution.py:284
  220.2 0.9 shard_map.86
  221.2 15.3 %all-gather.5 = bf16[16,48,32]{1,2,0:T(8,128)(2,1)S(1)} all-gather(bf16[1,48,32]{1,2,0:T(8,128)(2,1)S(1)} %copy.63), channel_id=1, replica_groups=mesh['dp'=32,'group'=16] {'group'}, dimensions={0}, use_global_device_ids=true | all-gather | bytes 52224 | tf_op jit(solution)/shard_map/all_gather | solution.py:332
  236.6 5.2 %shard_map.88 = f32[240,32]{1,0:T(8,128)S(1)} custom-call(s32[32,768]{1,0:T(8,128)S(1)} %get-tuple-element.15.pos_ref, f32[32,768]{1,0:T(8,128)S(1)} %bitcast.59), custom_call_target="tpu_custom_call" | custom-call | flops 23592960 | bytes 196608 | tf_op jit(solution)/shard_map/pallas_call | solution.py:194
  242.0 13.8 %all_to_all.34 = f32[32,2,240]{2,1,0:T(2,128)S(1)} all-to-all(f32[32,2,240]{2,1,0:T(2,128)S(1)} %copy.67), channel_id=1, replica_groups=mesh['dp'=32,'group'=16] {'dp'}, dimensions={0} | all-to-all | bytes 122880 | tf_op jit(solution)/shard_map/all_to_all | solution.py:266
  255.8 4.8 %all-to-all-start.4 = ((bf16[32,240,256]{2,1,0:T(8,128)(2,1)}), bf16[32,240,256]{2,1,0:T(8,128)(2,1)}, u32[]{:S(2)}, u32[]{:S(2)}) async-start(bf16[32,240,256]{2,1,0:T(8,128)(2,1)} %copy-done), calls=%async_computation.4 | async-start | bytes 7864320 | tf_op jit(solution)/shard_map/all_to_all | solution.py:266
  260.7 0.7 all-gather.14.cloned.1.call-update
  261.4 2.1 copy-done.4
  263.5 11.5 %shard_map.87 = f32[256,768]{1,0:T(8,128)S(1)} custom-call(s32[32,768]{1,0:T(8,128)S(1)} %get-tuple-element.15.pos_ref, f32[32,768]{1,0:T(8,128)S(1)} %bitcast.60, bf16[32,240,256]{2,1,0:T(8,128)(2,1)S(1)} %copy-done.4), custom_call_target="tpu_custom_call" | custom-call | flops 3019898880 | bytes 3932160 | tf_op jit(solution)/shard_map/pallas_call | solution.py:222
  275.5 28.9 %all-gather.14.cloned.1.call-done = bf16[768,768]{1,0:T(8,128)(2,1)} async-done(((bf16[48,768]{1,0:T(8,128)(2,1)}), bf16[768,768]{1,0:T(8,128)(2,1)}) %all-gather.14.cloned.1.call-update) | async-done | bytes 1179664 | tf_op jit(solution)/shard_map/all_gather | solution.py:333
  304.4 2.0 fusion.13
  306.3 16.0 %all-gather.6 = f32[16,1,768]{2,1,0:T(1,128)S(1)} all-gather(f32[1,1,768]{2,1,0:T(1,128)S(1)} %reshape.53), channel_id=3, replica_groups=mesh['dp'=32,'group'=16] {'group'}, dimensions={0}, use_global_device_ids=true | all-gather | bytes 52224 | tf_op jit(solution)/shard_map/all_gather | solution.py:270
  322.4 1.0 fusion.12
  323.4 1.8 fusion.26.base_ref
  325.2 26.5 %all-to-all-done.4.q_ref = bf16[32,240,256]{2,1,0:T(8,128)(2,1)} async-done(((bf16[32,240,256]{2,1,0:T(8,128)(2,1)}), bf16[32,240,256]{2,1,0:T(8,128)(2,1)}, u32[]{:S(2)}, u32[]{:S(2)}) %all-to-all-start.4) | async-done | bytes 3932192 | tf_op jit(solution)/shard_map/all_to_all | solution.py:266
  351.7 20.7 %shard_map.89 = f32[768,256]{1,0:T(8,128)S(1)} custom-call(f32[32,240]{1,0:T(8,128)S(1)} %bitcast.63, f32[240,32]{1,0:T(8,128)S(1)} %bitcast.61, bf16[32,240,256]{2,1,0:T(8,128)(2,1)} %all-to-all-done.4.q_ref, f32[768,256]{1,0:T(8,128)S(1)} %fusion.26.base_ref), custom_call_target="tpu_custom_call" | custom-call | flops 3019898880 | bytes 3932160 | tf_op jit(solution)/shard_map/pallas_call | solution.py:254
  372.9 0.7 concatenate.3
  373.6 0.6 broadcast_in_dim.14
  374.2 6.4 %all-to-all-start.5 = ((f32[32,1,384]{2,1,0:T(1,128)}), f32[32,1,384]{2,1,0:T(1,128)S(1)}, u32[]{:S(2)}, u32[]{:S(2)}) async-start(f32[32,1,384]{2,1,0:T(1,128)} %broadcast_in_dim.14), calls=%async_computation.5 | async-start | bytes 98304 | tf_op jit(solution)/shard_map/all_to_all | solution.py:266
  380.6 17.3 %all-gather.7 = f32[16,1,768]{2,1,0:T(1,128)S(1)} all-gather(f32[1,1,768]{2,1,0:T(1,128)S(1)} %reshape.55), channel_id=4, replica_groups=mesh['dp'=32,'group'=16] {'group'}, dimensions={0}, use_global_device_ids=true | all-gather | bytes 52224 | tf_op jit(solution)/shard_map/all_gather | solution.py:270
  398.0 1.0 fusion.19
  399.1 14.7 %all-gather.8 = f32[16,1,384]{2,1,0:T(1,128)S(1)} all-gather(f32[1,1,384]{2,1,0:T(1,128)S(1)} %reshape.57), channel_id=5, replica_groups=mesh['dp'=32,'group'=16] {'group'}, dimensions={0}, use_global_device_ids=true | all-gather | bytes 26112 | tf_op jit(solution)/shard_map/all_gather | solution.py:354
  413.8 0.6 slice_reduce_fusion
  414.4 0.6 copy.79
  (58 shorter events, 2.4 us)
Async XLA Ops:
  7.2 25.4 %copy-start.7 = (bf16[768,256]{1,0:T(8,128)(2,1)S(1)}, bf16[768,256]{1,0:T(8,128)(2,1)}, u32[]{:S(2)}) copy-start(bf16[768,256]{1,0:T(8,128)(2,1)} %param.6) | copy-start | bytes 1179652
  7.2 25.2 %copy-start.9 = (bf16[768,256]{1,0:T(8,128)(2,1)S(1)}, bf16[768,256]{1,0:T(8,128)(2,1)}, u32[]{:S(2)}) copy-start(bf16[768,256]{1,0:T(8,128)(2,1)} %param.5) | copy-start | bytes 1179652
  7.2 136.0 %all-gather.12.cloned.1.call-start = ((), (), s32[]{:S(2)}) async-start(), calls=%async_computation.6 | async-start | bytes 12976128 | tf_op jit(solution)/shard_map/all_gather | solution.py:301
  33.1 14.9 %copy-start.5 = (s32[768,8]{0,1:T(8,128)S(1)}, s32[768,8]{0,1:T(8,128)}, u32[]{:S(2)}) copy-start(s32[768,8]{0,1:T(8,128)} %param.7) | copy-start | bytes 73732
  33.1 14.9 %copy-start.6 = (s32[768,8]{0,1:T(8,128)S(1)}, s32[768,8]{0,1:T(8,128)}, u32[]{:S(2)}) copy-start(s32[768,8]{0,1:T(8,128)} %param.8) | copy-start | bytes 73732
  34.4 141.8 %collective-permute-start = (f32[8,48,768]{2,1,0:T(8,128)}, f32[8,48,768]{2,1,0:T(8,128)}, u32[]{:S(2)}, u32[]{:S(2)}) collective-permute-start(f32[8,48,768]{2,1,0:T(8,128)} %select_bitcast_fusion), channel_id=1, source_target_pairs={{0,1},{1,0},{2,3},{3,2},{4,5},{5,4},{6,7},{7,6},{8,9},{9,8},{10,11... | collective-permute-start | bytes 3538952 | tf_op jit(solution)/shard_map/ppermute | solution.py:282
  37.1 30.7 %all-to-all-start.1 = ((f32[32,1,768]{2,1,0:T(1,128)}), f32[32,1,768]{2,1,0:T(1,128)S(1)}, u32[]{:S(2)}, u32[]{:S(2)}) async-start(f32[32,1,768]{2,1,0:T(1,128)} %broadcast_in_dim.11), calls=%async_computation.1 | async-start | bytes 196608 | tf_op jit(solution)/shard_map/all_to_all | solution.py:266
  65.9 1.9 copy-start
  143.2 2.1 copy-start.1
  145.3 4.6 %copy-start.2 = (bf16[24576,256]{1,0:T(8,128)(2,1)S(1)}, bf16[24576,256]{1,0:T(8,128)(2,1)}, u32[]{:S(2)}) copy-start(bf16[24576,256]{1,0:T(8,128)(2,1)} %all-gather.12.cloned.1.call-done.p_ref) | copy-start | bytes 37748740
  165.3 1.9 copy-start.3
  168.3 16.3 %all-to-all-start.2 = ((f32[16,1,1536]{2,1,0:T(1,128)}), f32[16,1,1536]{2,1,0:T(1,128)S(1)}, u32[]{:S(2)}, u32[]{:S(2)}) async-start(f32[16,1,1536]{2,1,0:T(1,128)} %reshape.66), calls=%async_computation.2 | async-start | bytes 196608 | tf_op jit(solution)/shard_map/all_to_all | solution.py:266
  184.6 35.6 %all-to-all-start = ((f32[8,48,768]{2,1,0:T(8,128)}), f32[8,48,768]{2,1,0:T(8,128)S(1)}, u32[]{:S(2)}, u32[]{:S(2)}) async-start(f32[8,48,768]{2,1,0:T(8,128)} %bitcast_add_fusion), calls=%async_computation | async-start | bytes 2359296 | tf_op jit(solution)/shard_map/all_to_all | solution.py:284
  255.8 95.9 %all-to-all-start.4 = ((bf16[32,240,256]{2,1,0:T(8,128)(2,1)}), bf16[32,240,256]{2,1,0:T(8,128)(2,1)}, u32[]{:S(2)}, u32[]{:S(2)}) async-start(bf16[32,240,256]{2,1,0:T(8,128)(2,1)} %copy-done), calls=%async_computation.4 | async-start | bytes 7864320 | tf_op jit(solution)/shard_map/all_to_all | solution.py:266
  260.6 43.7 %all-gather.14.cloned.1.call-start = ((), (), s32[]{:S(2)}) async-start(), calls=%async_computation.7 | async-start | bytes 1253376 | tf_op jit(solution)/shard_map/all_gather | solution.py:333
  261.4 2.1 copy-start.4
  275.0 29.3 %copy-start.8 = (bf16[768,256]{1,0:T(8,128)(2,1)S(1)}, bf16[768,256]{1,0:T(8,128)(2,1)}, u32[]{:S(2)}) copy-start(bf16[768,256]{1,0:T(8,128)(2,1)} %param.6) | copy-start | bytes 1179652
  275.0 29.3 %copy-start.10 = (bf16[768,256]{1,0:T(8,128)(2,1)S(1)}, bf16[768,256]{1,0:T(8,128)(2,1)}, u32[]{:S(2)}) copy-start(bf16[768,256]{1,0:T(8,128)(2,1)} %param.5) | copy-start | bytes 1179652
  374.2 24.8 %all-to-all-start.5 = ((f32[32,1,384]{2,1,0:T(1,128)}), f32[32,1,384]{2,1,0:T(1,128)S(1)}, u32[]{:S(2)}, u32[]{:S(2)}) async-start(f32[32,1,384]{2,1,0:T(1,128)} %broadcast_in_dim.14), calls=%async_computation.5 | async-start | bytes 98304 | tf_op jit(solution)/shard_map/all_to_all | solution.py:266
Sparse Core Ops, SparseCore 0:
  11.2 131.9 all-gather.11
  264.2 40.1 all-gather.13

commit v2 on v0

v2 whole, which is shorter than its diff:
```python
import functools
import math

import jax
import jax.numpy as jnp
from jax import lax
from jax.experimental import pallas as pl
from jax.experimental.pallas import tpu as pltpu
from jax.sharding import PartitionSpec as P

EPSILON = 1e-06
SOFTNESS_DIVISOR = 0.25
F32 = jnp.float32
BF16 = jnp.bfloat16
VMEM_LIMIT = 52 * 1024 * 1024
MANY = 4


def iota(shape, axis):
    return lax.broadcasted_iota(jnp.int32, shape, axis)


def contract(a, b, da, db):
    return lax.dot_general(a, b, (((da,), (db,)), ((), ())), preferred_element_type=F32)


def cost(micros):
    return pl.CostEstimate(flops=0, bytes_accessed=int(micros * 3.5e6), transcendentals=0)


def call(kernel, grid, in_specs, out_specs, out_shape, micros, scratch=()):
    return pl.pallas_call(
        kernel,
        grid=(grid,),
        in_specs=in_specs,
        out_specs=out_specs,
        out_shape=out_shape,
        scratch_shapes=list(scratch),
        compiler_params=pltpu.CompilerParams(vmem_limit_bytes=VMEM_LIMIT),
        cost_estimate=cost(micros),
    )


def whole(shape):
    return pl.BlockSpec(shape, lambda i: (0,) * len(shape))


def slab(cap, piece, many=1):
    return pl.BlockSpec((many, cap, piece), lambda i: (i, 0, 0))


def table_column(table_ref, index):
    lanes = iota(table_ref.shape, 1)
    return jnp.sum(jnp.where(lanes == index, table_ref[...], 0.0), axis=1, keepdims=True)


def add_column(table_ref, index, column):
    table_ref[...] += jnp.where(iota(table_ref.shape, 1) == index, column, 0.0)


def slot_value(pos, values, cap):
    match = iota((cap, pos.shape[1]), 0) == pos
    return jnp.sum(jnp.where(match, values, 0.0), axis=1, keepdims=True)


def slot_pick(pos, values, cap):
    slots = iota((cap, pos.shape[1]), 0).astype(F32).astype(BF16)
    return jnp.where(slots == pos.astype(F32).astype(BF16), values, jnp.zeros((), BF16))


def one_hot(match):
    return jnp.where(match, 1.0, 0.0).astype(BF16)


def tables_kernel(owner_ref, row_ref, pos_ref, code_ref):
    negs, rows = owner_ref.shape
    n_data = pos_ref.shape[0]
    ids = iota((n_data, rows), 0)
    asked = jnp.full((n_data, rows), -1, jnp.int32)
    for k in range(negs):
        asked = jnp.where(owner_ref[k : k + 1, :] == ids, row_ref[k : k + 1, :], asked)
    hit = one_hot(asked >= 0)
    before = one_hot(iota((rows, rows), 0) < iota((rows, rows), 1))
    count = contract(hit, before, 1, 0).astype(jnp.int32)
    pos_ref[...] = jnp.where(asked >= 0, count, -1)
    code_ref[...] = jnp.where(asked >= 0, asked * 1024 + count, -1).astype(F32)


def make_tables(owner_t, row_t, n_data):
    negs, rows = owner_t.shape
    return call(
        tables_kernel,
        1,
        [whole((negs, rows)), whole((negs, rows))],
        [whole((n_data, rows)), whole((n_data, rows))],
        [
            jax.ShapeDtypeStruct((n_data, rows), jnp.int32),
            jax.ShapeDtypeStruct((n_data, rows), F32),
        ],
        1,
    )(owner_t, row_t)


def decode(code_ref, index):
    code = code_ref[pl.ds(index, 1), :].astype(jnp.int32)
    return code & 1023, code >> 10


def serve_kernel(code_ref, p_ref, slot_ref, pick_ref):
    many, cap, piece = slot_ref.shape
    rows = p_ref.shape[0]
    for t in range(many):
        pos, asked = decode(code_ref, pl.program_id(0) * many + t)
        wanted = slot_value(pos, (asked + 1).astype(F32), cap).astype(jnp.int32) - 1
        pick_ref[t * cap : (t + 1) * cap, :] = one_hot(iota((cap, rows), 1) == wanted)
    found = contract(pick_ref[...], p_ref[...], 1, 0).astype(BF16)
    slot_ref[...] = found.reshape(many, cap, piece)


def serve(code, passages, cap):
    n_data, rows = code.shape
    piece = passages.shape[1]
    return call(
        serve_kernel,
        n_data // MANY,
        [whole((n_data, rows)), whole((rows, piece))],
        slab(cap, piece, MANY),
        jax.ShapeDtypeStruct((n_data, cap, piece), BF16),
        8,
        [pltpu.VMEM((MANY * cap, rows), BF16)],
    )(code, passages)


def match_kernel(code_ref, match_ref):
    step = pl.program_id(0)
    rows, wide = match_ref.shape[1:]
    many = 4
    each = wide // many
    part = iota((8, rows), 0)
    for t in range(many):
        pos, asked = decode(code_ref, step * many + t)
        asked = asked + 1
        digits = jnp.where(part == 0, asked >> 5, jnp.where(part == 1, asked & 31, 0))
        pick = one_hot(iota((each, rows), 0) == pos)
        found = contract(digits.astype(F32).astype(BF16), pick, 1, 1)
        wanted = (found[0:1, :] * 32.0 + found[1:2, :]).astype(jnp.int32) - 1
        match_ref[0, :, t * each : (t + 1) * each] = one_hot(iota((rows, each), 0) == wanted)


def make_match(code, many, each):
    n_data, rows = code.shape
    wide = many * each
    steps = n_data // many
    return call(
        match_kernel,
        steps,
        [whole((n_data, rows))],
        slab(rows, wide),
        jax.ShapeDtypeStruct((steps, rows, wide), BF16),
        10,
    )(code)


def slots_kernel(pos_ref, q_ref, inverse_ref, slot_ref, table_ref, pick_ref):
    step = pl.program_id(0)
    many, cap, piece = slot_ref.shape

    @pl.when(step == 0)
    def _():
        table_ref[...] = jnp.zeros_like(table_ref)

    for t in range(many):
        pos = pos_ref[pl.ds(step * many + t, 1), :]
        pick_ref[t * cap : (t + 1) * cap, :] = slot_pick(pos, jnp.ones((), BF16), cap)
        add_column(table_ref, step * many + t, slot_value(pos, inverse_ref[...], cap))
    found = contract(pick_ref[...], q_ref[...], 1, 0).astype(BF16)
    slot_ref[...] = found.reshape(many, cap, piece)


def make_slots(pos, q_emb, inverse, cap):
    n_data, rows = pos.shape
    piece = q_emb.shape[1]
    return call(
        slots_kernel,
        n_data // MANY,
        [whole((n_data, rows)), whole((rows, piece)), whole((1, rows))],
        [slab(cap, piece, MANY), whole((cap, n_data))],
        [
            jax.ShapeDtypeStruct((n_data, cap, piece), BF16),
            jax.ShapeDtypeStruct((cap, n_data), F32),
        ],
        9,
        [pltpu.VMEM((MANY * cap, rows), BF16)],
    )(pos, q_emb, inverse)


def collect_kernel(base_ref, code_ref, q_ref, slot_ref):
    many, cap, _ = slot_ref.shape
    rows = code_ref.shape[1]
    for t in range(many):
        pos, _ = decode(code_ref, base_ref[0] + pl.program_id(0) * many + t)
        pick = slot_pick(pos, jnp.ones((), BF16), cap)
        found = contract(pick, q_ref[t * rows : (t + 1) * rows, :], 1, 0)
        slot_ref[t] = found.astype(BF16)


def collect(base, code, part, cap):
    n_data, rows = code.shape
    piece = part.shape[1]
    count = part.shape[0] // rows
    many = 2
    return call(
        collect_kernel,
        count // many,
        [
            pl.BlockSpec(memory_space=pltpu.SMEM),
            whole((n_data, rows)),
            pl.BlockSpec((many * rows, piece), lambda i: (i, 0)),
        ],
        slab(cap, piece, many),
        jax.ShapeDtypeStruct((count, cap, piece), BF16),
        0.5 * count,
    )(base, code, part)


def near_kernel(scale, pos_ref, owner_ref, q_ref, p_ref, near_ref):
    step = pl.program_id(0)
    many, cap, _ = q_ref.shape
    rows = pos_ref.shape[1]
    chunk = 48

    @pl.when(step == 0)
    def _():
        near_ref[...] = jnp.zeros_like(near_ref)

    for t in range(many):
        owner = step * many + t
        pos = pos_ref[pl.ds(owner, 1), :]
        spread = jnp.zeros((8, rows), F32)
        for start in range(0, cap, chunk):
            span = slice(start, start + chunk)
            product = q_ref[t, span, :].astype(F32) * p_ref[t, span, :].astype(F32)
            score = jnp.sum(product, axis=1, keepdims=True) * scale
            match = iota((chunk, rows), 0) + start == pos
            spread += jnp.sum(jnp.where(match, score, 0.0).reshape(chunk // 8, 8, rows), axis=0)
        spread = jnp.sum(spread, axis=0, keepdims=True)
        near_ref[...] += jnp.where(owner_ref[...] == owner, spread, 0.0)


def near_scores(scale, pos, owner_t, q_slots, p_slots):
    n_data, cap, piece = q_slots.shape
    negs, rows = owner_t.shape
    return call(
        functools.partial(near_kernel, scale),
        n_data // MANY,
        [whole((n_data, rows)), whole((negs, rows)), slab(cap, piece, MANY), slab(cap, piece, MANY)],
        whole((negs, rows)),
        jax.ShapeDtypeStruct((negs, rows), F32),
        9,
    )(pos, owner_t, q_slots, p_slots)


def batch_kernel(scores_ref, stats_ref):
    scores = scores_ref[...]
    top = jnp.max(scores, axis=1, keepdims=True)
    total = jnp.sum(jnp.exp(scores - top), axis=1, keepdims=True)
    stats_ref[...] = jnp.where(iota(stats_ref.shape, 1) == 0, top, total)


def batch_stats(scores):
    share, rows = scores.shape
    return call(
        batch_kernel,
        1,
        [whole((share, rows))],
        whole((share, 2)),
        jax.ShapeDtypeStruct((share, 2), F32),
        1,
    )(scores)


def softmax_kernel(owner_ref, near_ref, stats_ref, hard_ref, lse_ref):
    near = jnp.sum(near_ref[...], axis=0)
    batch_top = stats_ref[0:1, :]
    top = jnp.maximum(batch_top, jnp.max(near, axis=0, keepdims=True))
    total = stats_ref[1:2, :] * jnp.exp(batch_top - top) + jnp.sum(
        jnp.exp(near - top), axis=0, keepdims=True
    )
    lse = top + jnp.log(total)
    lse_ref[...] = lse
    hard = jnp.exp(near - lse).astype(BF16).astype(F32)
    ids = iota(hard_ref.shape, 0)
    spread = jnp.zeros(hard_ref.shape, F32)
    for k in range(hard.shape[0]):
        spread += jnp.where(owner_ref[k : k + 1, :] == ids, hard[k : k + 1, :], 0.0)
    hard_ref[...] = spread


def softmax_all(owner_t, near, stats, n_data):
    n_members, negs, rows = near.shape
    return call(
        softmax_kernel,
        1,
        [whole((negs, rows)), whole((n_members, negs, rows)), whole((2, rows))],
        [whole((n_data, rows)), whole((1, rows))],
        [jax.ShapeDtypeStruct((n_data, rows), F32), jax.ShapeDtypeStruct((1, rows), F32)],
        2,
    )(owner_t, near, stats)


def weigh_kernel(pos_ref, hard_ref, table_ref):
    step = pl.program_id(0)
    many = 8

    @pl.when(step == 0)
    def _():
        table_ref[...] = jnp.zeros_like(table_ref)

    lanes = iota(table_ref.shape, 1)
    total = table_ref[...]
    for t in range(many):
        at = step * many + t
        weight = slot_value(pos_ref[pl.ds(at, 1), :], hard_ref[pl.ds(at, 1), :], total.shape[0])
        total = jnp.where(lanes == at, weight, total)
    table_ref[...] = total


def weigh_slots(pos, hard, cap):
    n_data, rows = pos.shape
    return call(
        weigh_kernel,
        n_data // 8,
        [whole((n_data, rows)), whole((n_data, rows))],
        whole((cap, n_data)),
        jax.ShapeDtypeStruct((cap, n_data), F32),
        5,
    )(pos, hard)


def hard_grad_kernel(scale, pos_ref, hard_ref, table_ref, q_ref, p_ref, total_ref, sum_ref, spread_ref):
    step = pl.program_id(0)
    many, cap, piece = p_ref.shape

    @pl.when(step == 0)
    def _():
        total_ref[...] = jnp.zeros_like(total_ref)
        sum_ref[...] = jnp.zeros_like(sum_ref)

    gain = jnp.zeros((8, piece), F32)
    for t in range(many):
        at = step * many + t
        hard = hard_ref[pl.ds(at, 1), :].astype(BF16)
        spread_ref[t * cap : (t + 1) * cap, :] = slot_pick(pos_ref[pl.ds(at, 1), :], hard, cap)
        weight = table_column(table_ref, at) * scale
        pairs = (weight * q_ref[t].astype(F32)).astype(BF16).astype(F32)
        gain += jnp.sum((pairs * p_ref[t].astype(F32)).reshape(cap // 8, 8, piece), axis=0)
    sum_ref[...] += jnp.sum(gain, axis=0, keepdims=True)
    total_ref[...] += contract(p_ref[...].reshape(many * cap, piece), spread_ref[...], 0, 0)


def hard_grad(scale, pos, hard, table, q_slots, p_slots):
    n_data, cap, piece = p_slots.shape
    rows = pos.shape[1]
    return call(
        functools.partial(hard_grad_kernel, scale),
        n_data // MANY,
        [
            whole((n_data, rows)),
            whole((n_data, rows)),
            whole((cap, n_data)),
            slab(cap, piece, MANY),
            slab(cap, piece, MANY),
        ],
        [whole((piece, rows)), whole((1, piece))],
        [jax.ShapeDtypeStruct((piece, rows), F32), jax.ShapeDtypeStruct((1, piece), F32)],
        12,
        [pltpu.VMEM((MANY * cap, rows), BF16)],
    )(pos, hard, table, q_slots, p_slots)


def pair_kernel(scale, nz, x_ref, table_ref, inverse_ref, gain_ref, match_ref, *refs):
    q_refs, (total_ref, pairs_ref) = refs[:7], refs[7:]
    step = pl.program_id(0)
    many, cap, _ = q_refs[0].shape
    each = pairs_ref.shape[0] // many
    nx = pl.num_programs(0) * many // nz
    first = lax.rem(x_ref[0] * nz + step * many, nx * nz)

    @pl.when(step == 0)
    def _():
        total_ref[...] = jnp.zeros_like(total_ref)
        pairs_ref[...] = jnp.zeros_like(pairs_ref)

    def fill(q_ref):
        for t in range(many):
            weight = table_column(table_ref, first + t)
            inverse = table_column(inverse_ref, first + t)
            emb = ((q_ref[t].astype(F32) * inverse) * gain_ref[...]).astype(BF16)
            pairs = ((weight * scale) * emb.astype(F32)).astype(BF16)
            pairs_ref[t * each : t * each + cap, :] = pairs

    half = nz // many
    for place, (low, high) in enumerate(pair_spans(half)):
        pl.when((step >= low) & (step < high))(functools.partial(fill, q_refs[place]))
    total_ref[...] += contract(match_ref[0], pairs_ref[...], 1, 0)


def pair_spans(half):
    quarter = half // 2
    return [(0, half)] + [(half + i * quarter, half + (i + 1) * quarter) for i in range(6)]


def pair_grad(scale, nz, x, table, inverse, gain, match, parts):
    cap, n_data = table.shape
    steps, rows, wide = match.shape
    piece = parts[0].shape[2]
    many = n_data // steps

    def part_spec(span):
        low, high = span
        return pl.BlockSpec(
            (many, cap, piece), lambda i, x_ref: (jnp.clip(i, low, high - 1) - low, 0, 0)
        )

    def match_block(i, x_ref):
        return (lax.rem(x_ref[0] * (nz // many) + i, steps), 0, 0)

    return pl.pallas_call(
        functools.partial(pair_kernel, scale, nz),
        grid_spec=pltpu.PrefetchScalarGridSpec(
            num_scalar_prefetch=1,
            grid=(steps,),
            in_specs=[
                pl.BlockSpec((cap, n_data), lambda i, x_ref: (0, 0)),
                pl.BlockSpec((cap, n_data), lambda i, x_ref: (0, 0)),
                pl.BlockSpec((1, piece), lambda i, x_ref: (0, 0)),
                pl.BlockSpec((1, rows, wide), match_block),
                *[part_spec(span) for span in pair_spans(nz // many)],
            ],
            out_specs=pl.BlockSpec((rows, piece), lambda i, x_ref: (0, 0)),
            scratch_shapes=[pltpu.VMEM((wide, piece), BF16)],
        ),
        out_shape=jax.ShapeDtypeStruct((rows, piece), F32),
        compiler_params=pltpu.CompilerParams(vmem_limit_bytes=VMEM_LIMIT),
        cost_estimate=cost(7),
    )(x, table, inverse, gain, match, *parts)


def swap(x, axis):
    return lax.all_to_all(x, axis, split_axis=0, concat_axis=0, tiled=True)


def tied(*values):
    return lax.optimization_barrier(values)


class Torus:
    def __init__(self, n_data, nx):
        self.nx, self.nz = nx, n_data // nx
        self.along_z = [[x * self.nz + z for z in range(self.nz)] for x in range(nx)]

    def shift(self, value, by):
        nx, nz = self.nx, self.nz
        pairs = [
            (x * nz + z, (x + by) % nx * nz + z) for x in range(nx) for z in range(nz)
        ]
        return lax.ppermute(value, "dp", pairs)

    def gather_z(self, value):
        return lax.all_gather(value, "dp", axis=0, tiled=True, axis_index_groups=self.along_z)


def local(nx, queries, passages, neg_owner, neg_row, gain):
    rows, piece = queries.shape
    negs = neg_owner.shape[1]
    n_data = lax.axis_size("dp")
    n_members = lax.axis_size("group")
    member = lax.axis_index("group")
    width = piece * n_members
    cap = min(rows, 5 * rows * negs // (4 * n_data))
    scale = 1.0 / (SOFTNESS_DIVISOR * math.sqrt(width))
    torus = Torus(n_data, nx)
    nz = torus.nz
    my_x = (lax.axis_index("dp") // nz).astype(jnp.int32)
    my_gain = lax.dynamic_slice_in_dim(gain, member * piece, piece, 0)
    gain_row = my_gain[None, :]
    owner_t = neg_owner.T

    def base(away, more=0):
        return jnp.full((1,), (my_x + away) % nx * nz + more, jnp.int32)

    q_zero = torus.gather_z(queries)
    half = q_zero.shape[0] // 2

    pos, code = make_tables(owner_t, neg_row.T, n_data)
    code_got = swap(code, "dp")

    q_values = queries.astype(F32)
    p_values = passages.astype(F32)
    squares = jnp.stack(
        [jnp.sum(q_values * q_values, axis=1), jnp.sum(p_values * p_values, axis=1)]
    )
    squares = jnp.sum(lax.all_gather(squares, "group", axis=0), axis=0)
    squares, code_got = tied(squares, code_got)
    inverses = lax.rsqrt(squares / width + EPSILON)
    q_inverse, p_inverse = inverses[0][:, None], inverses[1][:, None]
    q_normed = q_values * q_inverse
    p_normed = p_values * p_inverse
    q_emb = (q_normed * my_gain).astype(BF16)
    p_emb = (p_normed * my_gain).astype(BF16)
    p_slots = swap(serve(code_got, p_emb, cap), "dp")

    scores = contract(q_emb, p_emb, 1, 1) * scale
    scores = lax.psum_scatter(scores, "group", scatter_dimension=0, tiled=True)
    q_slots, inverse = make_slots(pos, q_emb, inverses[:1], cap)
    each = -(-cap // 128) * 128
    match = make_match(code_got, 4, each)
    q_three_low, q_one_high = torus.shift(q_zero[:half], 1), torus.shift(q_zero[half:], -1)
    part_zero = collect(base(0), code_got, q_zero, cap)
    scores, q_slots, match, q_three_low, q_one_high, q_zero, part_zero = tied(
        scores, q_slots, match, q_three_low, q_one_high, q_zero, part_zero
    )
    stats = batch_stats(scores)
    scores = lax.all_gather(scores, "group", axis=0, tiled=True)
    q_one_low, q_three_high = torus.shift(q_zero[:half], -1), torus.shift(q_zero[half:], 1)
    q_low, q_high = torus.shift(q_three_low, 1), torus.shift(q_one_high, -1)
    p_slots, stats = tied(p_slots, stats)

    near = near_scores(scale, pos, owner_t, q_slots, p_slots)
    share = rows // n_members
    per = 2 * share // negs
    stats = jnp.pad(stats.T.reshape(negs, per), ((0, 0), (0, -per % 128)))
    mixed = lax.all_gather(jnp.concatenate([near, stats], axis=1), "group", axis=0)
    near = mixed[:, :, :rows]
    stats = mixed[:, :, rows : rows + per].reshape(n_members, 2, share)
    stats = stats.transpose(1, 0, 2).reshape(2, rows)
    hard, lse = softmax_all(owner_t, near, stats, n_data)
    table = weigh_slots(pos, hard, cap)
    _, q_one_low, q_one_high, q_low, q_high, q_three_low, q_three_high = tied(
        hard, q_one_low, q_one_high, q_low, q_high, q_three_low, q_three_high
    )
    got = swap(jnp.concatenate([table, inverse], axis=0).T, "dp").T

    parts = [part_zero] + [
        collect(at, code_got, part, cap)
        for at, part in (
            (base(1), q_one_low),
            (base(1, nz // 2), q_one_high),
            (base(2), q_low),
            (base(2, nz // 2), q_high),
            (base(3), q_three_low),
            (base(3, nz // 2), q_three_high),
        )
    ]

    hard_q, pair_gain = hard_grad(scale, pos, hard, table, q_slots, p_slots)
    lse = lse[0][:, None]
    positive = iota((rows, rows), 0) == iota((rows, rows), 1)
    weights = (jnp.exp(scores - lse) - positive.astype(F32)).astype(BF16)
    losses = jnp.sum(lse) - jnp.sum(jnp.where(positive, scores, 0.0))
    grad_q = (contract(weights, p_emb, 1, 0) + hard_q.T) * scale
    batch_grad = contract(weights, q_emb, 0, 0) * scale
    gain_part = (
        jnp.sum(grad_q * q_normed, axis=0)
        + jnp.sum(batch_grad * p_normed, axis=0)
        + pair_gain[0] / my_gain
    )
    last = jnp.concatenate([gain_part, jnp.broadcast_to(losses, (128,))])
    last, got = tied(last, got)
    last = jnp.sum(swap(jnp.broadcast_to(last[None, :], (n_data, piece + 128)), "dp"), axis=0)

    grad_p = batch_grad + pair_grad(
        scale, nz, jnp.full((1,), my_x), got[:cap], got[cap:], gain_row, match, parts
    )
    q_inner = grad_q * my_gain
    p_inner = grad_p * my_gain
    final = jnp.concatenate(
        [jnp.sum(q_inner * q_normed, axis=1), jnp.sum(p_inner * p_normed, axis=1), last]
    )
    final = lax.all_gather(final, "group", axis=0)
    means = jnp.sum(final[:, : 2 * rows], axis=0) / width
    q_mean, p_mean = means[:rows, None], means[rows:, None]
    grad_queries = (q_inverse * (q_inner - q_normed * q_mean)).astype(BF16)
    grad_passages = (p_inverse * (p_inner - p_normed * p_mean)).astype(BF16)
    count = rows * n_data
    grad_gain = final[:, 2 * rows : 2 * rows + piece].reshape(-1) / math.sqrt(count)
    loss = final[0, 2 * rows + piece] / count
    return grad_queries, grad_passages, grad_gain, loss


def solution(mesh):
    nx = 4
    return jax.shard_map(
        functools.partial(local, nx),
        mesh=mesh,
        in_specs=(P("dp", "group"), P("dp", "group"), P("dp", None), P("dp", None), P()),
        out_specs=(P("dp", "group"), P("dp", "group"), P(), P()),
        check_vma=False,
    )
```

time: 618 us -> 299 us (0.48)
  waiting for transfers between devices: 202 us -> 51.6 us
  blocking collectives: 203 us -> 53.7 us
  Pallas kernels: 0 us -> 72.1 us
  local copies, waits for them, and re-layouts: 76.9 us -> 17.1 us
  other arithmetic: 64.5 us -> 10.7 us
  starting transfers between devices: 33.2 us -> 65.9 us
  matrix products: 20.9 us -> 7.09 us
    psum x4 -> x0, blocking collectives: 203 us -> none  [the longest x1 97.1 us: local(): loss_total, gain_total = lax.psum((loss_part, gain_full), ('dp', 'group'))]
    psum x1 -> x0, waiting for transfers between devices: 125 us -> none  [local(): scores, near = lax.psum((partial_value, near_part), 'group')]
    pallas_call x0 -> x17, Pallas kernels: none -> 72.1 us  [the longest x7 14.9 us: collect(): call(collect_kernel, count // many, [pl.BlockSpec(memory_space=pltpu.SMEM...]
    all_to_all x3 -> x4, waiting for transfers between devices: 77.3 us -> 11.2 us  [swap(): return lax.all_to_all(x, axis, split_axis=0, concat_axis=0, tiled=True)]
    all_gather x0 -> x3, blocking collectives: none -> 53.7 us  [the longest x1 18.6 us: local(): squares = jnp.sum(lax.all_gather(squares, 'group', axis=0), axis=0)]
    gather x2 -> x0, local copies, waits for them, and re-layouts: 48.2 us -> none  [the longest x1 26.1 us: local(): jnp.take(received_block.reshape(-1, piece), target, axis=0)]
    scatter x1 -> x0, other arithmetic: 32 us -> none  [local(): jnp.zeros((n_data * slot_capacity, piece), jnp.bfloat16).at[target]]
    ppermute x0 -> x6, waiting for transfers between devices: none -> 29 us  [shift(): return lax.ppermute(value, 'dp', pairs)]
  transfers between devices with their start and end apart: 4 -> 13, of which waited for: 2 -> 4; matrix products, arithmetic and copies ran while one was open for 3% -> 6% of each run, Pallas kernels for 0% -> 24%
where the time goes in v2:
time: 299 us; the launch traced here: 297 us
  Pallas kernels  72.1 us (24%)
  starting transfers between devices  65.9 us (22%)
  blocking collectives  53.7 us (18%)
  waiting for transfers between devices  51.6 us (17%)
  between operations  19.2 us (6%)
  local copies, waits for them, and re-layouts  17.1 us (6%)
  other arithmetic  10.7 us (4%)
  matrix products  7.09 us (2%)
    all_to_all x4, starting transfers between devices, swap(): return lax.all_to_all(x, axis, split_axis=0, concat_axis=0, tiled=True)  48.8 us
    ppermute x6, waiting for transfers between devices, shift(): return lax.ppermute(value, 'dp', pairs)  29 us
    all_gather x1, blocking collectives, local(): squares = jnp.sum(lax.all_gather(squares, 'group', axis=0), axis=0)  18.6 us
    all_gather x1, blocking collectives, local(): lax.all_gather(jnp.concatenate([near, stats], axis=1), 'group', axis=0)  17.9 us
    all_gather x1, blocking collectives, local(): final = lax.all_gather(final, 'group', axis=0)  17.2 us
    ppermute x6, starting transfers between devices, shift(): return lax.ppermute(value, 'dp', pairs)  17 us
    pallas_call x7, Pallas kernels, collect(): call(collect_kernel, count // many, [pl.BlockSpec(memory_space=pltpu.SMEM...  14.9 us
    pallas_call x1, Pallas kernels, pair_grad(): pl.pallas_call(functools.partial(pair_kernel, scale, nz), grid_spec=pltpu...  12.5 us
  transfers between devices with their start and end apart: 13, of which 4 were waited for; matrix products, arithmetic and copies ran while one was open for 6% of the time, Pallas kernels for 24%

profile of v2, /device:TPU:1, one launch (start us, length us, event | category | flops | bytes accessed | tf_op | source)
XLA Modules:
  0.0 297.3 jit_solution(7740457331138409419)
XLA Ops:
  11.3 13.7 %all-to-all-start = ((f32[32,1,768]{2,1,0:T(1,128)}), f32[32,1,768]{2,1,0:T(1,128)S(1)}, u32[]{:S(2)}, u32[]{:S(2)}) async-start(f32[32,1,768]{2,1,0:T(1,128)} %copy.29), calls=%async_computation | async-start | bytes 196608 | tf_op jit(solution)/shard_map/all_to_all | solution.py:450
  25.1 1.2 fusion.21
  26.2 1.2 fusion.14
  27.5 18.6 %all-gather.3 = f32[16,2,768]{2,1,0:T(2,128)S(1)} all-gather(f32[1,2,768]{2,1,0:T(2,128)S(1)} %maximum_bitcast_fusion.1), channel_id=2, replica_groups=mesh['dp'=32,'group'=16] {'group'}, dimensions={0}, use_global_device_ids=true | all-gather | bytes 104448 | tf_op jit(solution)/shard_map/all_gather | solution.py:503
  46.1 0.8 broadcast_multiply_fusion.1
  47.0 1.3 fusion.8
  48.3 2.0 convolution_multiply_fusion
  50.3 7.5 %shard_map.88 = bf16[32,240,256]{2,1,0:T(8,128)(2,1)} custom-call(f32[32,768]{1,0:T(8,128)S(1)} %bitcast.39, bf16[768,256]{1,0:T(8,128)(2,1)S(1)} %get-tuple-element.76.p_ref), custom_call_target="tpu_custom_call" | custom-call | bytes 28000000 | tf_op jit(solution)/shard_map/pallas_call | solution.py:123
  57.7 9.6 %all-to-all-start.1 = ((bf16[32,240,256]{2,1,0:T(8,128)(2,1)}), bf16[32,240,256]{2,1,0:T(8,128)(2,1)}, u32[]{:S(2)}, u32[]{:S(2)}) async-start(bf16[32,240,256]{2,1,0:T(8,128)(2,1)} %shard_map.88), calls=%async_computation.2 | async-start | bytes 7864320 | tf_op jit(solution)/shard_map/all_to_all | solution.py:450
  67.4 3.3 %fusion.25 = (bf16[3072,256]{1,0:T(8,128)(2,1)S(1)}, bf16[3072,256]{1,0:T(8,128)(2,1)}) fusion(bf16[6144,256]{1,0:T(8,128)(2,1)} %all-gather.8.cloned.1.call-done.q_ref), kind=kLoop, calls=%fused_computation.51 | loop fusion | bytes 6291456 | tf_op jit(solution)/shard_map/slice | solution.py:518
  70.7 3.1 %collective-permute-start = (bf16[3072,256]{1,0:T(8,128)(2,1)}, bf16[3072,256]{1,0:T(8,128)(2,1)}, u32[]{:S(2)}, u32[]{:S(2)}) collective-permute-start(bf16[3072,256]{1,0:T(8,128)(2,1)} %get-tuple-element.69), channel_id=1, source_target_pairs={{0,128},{16,144},{32,160},{48,176},{64,192},{80,208},{96,224},{112... | collective-permute-start | bytes 4718600 | tf_op jit(solution)/shard_map/ppermute | solution.py:467
  73.8 3.4 %collective-permute-start.1 = (bf16[3072,256]{1,0:T(8,128)(2,1)S(1)}, bf16[3072,256]{1,0:T(8,128)(2,1)}, u32[]{:S(2)}, u32[]{:S(2)}) collective-permute-start(bf16[3072,256]{1,0:T(8,128)(2,1)S(1)} %get-tuple-element.68), channel_id=1, source_target_pairs={{0,384},{16,400},{32,416},{48,432},{64,448},{80,464},{96,480},{112... | collective-permute-start | bytes 4718600 | tf_op jit(solution)/shard_map/ppermute | solution.py:467
  77.2 10.4 %shard_map.86.match_ref = bf16[8,768,1024]{2,1,0:T(8,128)(2,1)} custom-call(f32[32,768]{1,0:T(8,128)S(1)} %bitcast.40), custom_call_target="tpu_custom_call" | custom-call | bytes 35000000 | tf_op jit(solution)/shard_map/pallas_call | solution.py:154
  87.7 7.5 %shard_map.85 = (bf16[32,240,256]{2,1,0:T(8,128)(2,1)}, f32[240,32]{1,0:T(8,128)S(1)}) custom-call(s32[32,768]{1,0:T(8,128)S(1)} %get-tuple-element.33.pos_ref, bf16[768,256]{1,0:T(8,128)(2,1)S(1)} %get-tuple-element.75.q_ref, f32[1,768]{1,0:T(1,128)S(1)} %get-tuple-element.74.inverse_ref), custom_call_target="tpu_custom_call" | custom-call | bytes 31500000 | tf_op jit(solution)/shard_map/pallas_call | solution.py:183
  95.2 3.5 %shard_map.87.refs_0_ = bf16[8,240,256]{2,1,0:T(8,128)(2,1)S(1)} custom-call(s32[1]{0:T(128)} %bitcast.4.base_ref, f32[32,768]{1,0:T(8,128)S(1)} %bitcast.41, bf16[6144,256]{1,0:T(8,128)(2,1)} %all-gather.8.cloned.1.call-done.q_ref), custom_call_target="tpu_custom_call" | custom-call | bytes 14000000 | tf_op jit(solution)/shard_map/pallas_call | solution.py:212
  98.7 0.9 copy-done
  99.6 10.7 %reduce-scatter.2.cloned.1.call-done.scores_ref = f32[48,768]{1,0:T(8,128)} async-done(((f32[768,768]{1,0:T(8,128)}), f32[48,768]{1,0:T(8,128)}) %reduce-scatter.2.cloned.1.call-update) | async-done | bytes 147472 | tf_op jit(solution)/shard_map/reduce_scatter | solution.py:514
  110.3 29.0 %collective-permute-done.q_ref = bf16[3072,256]{1,0:T(8,128)(2,1)} collective-permute-done((bf16[3072,256]{1,0:T(8,128)(2,1)}, bf16[3072,256]{1,0:T(8,128)(2,1)}, u32[]{:S(2)}, u32[]{:S(2)}) %collective-permute-start) | collective-permute-done | bytes 1572896 | tf_op jit(solution)/shard_map/ppermute | solution.py:467
  139.3 3.9 %fusion.24 = (bf16[3072,256]{1,0:T(8,128)(2,1)}, bf16[3072,256]{1,0:T(8,128)(2,1)}) fusion(bf16[6144,256]{1,0:T(8,128)(2,1)} %all-gather.8.cloned.1.call-done.q_ref), kind=kLoop, calls=%fused_computation.50 | loop fusion | bytes 6291456 | tf_op jit(solution)/shard_map/slice | solution.py:525
  143.2 2.0 collective-permute-start.2
  145.2 3.3 %collective-permute-start.3 = (bf16[3072,256]{1,0:T(8,128)(2,1)}, bf16[3072,256]{1,0:T(8,128)(2,1)}, u32[]{:S(2)}, u32[]{:S(2)}) collective-permute-start(bf16[3072,256]{1,0:T(8,128)(2,1)} %collective-permute-done.q_ref), channel_id=1, source_target_pairs={{0,128},{16,144},{32,160},{48,176},{64,192},{80,208},{96,224},{112... | collective-permute-start | bytes 4718600 | tf_op jit(solution)/shard_map/ppermute | solution.py:467
  148.5 3.2 %collective-permute-start.4 = (bf16[3072,256]{1,0:T(8,128)(2,1)}, bf16[3072,256]{1,0:T(8,128)(2,1)}, u32[]{:S(2)}, u32[]{:S(2)}) collective-permute-start(bf16[3072,256]{1,0:T(8,128)(2,1)} %collective-permute-done.1.q_ref), channel_id=1, source_target_pairs={{0,384},{16,400},{32,416},{48,432},{64,448},{80,464},{96,480},{112... | collective-permute-start | bytes 4718600 | tf_op jit(solution)/shard_map/ppermute | solution.py:467
  151.7 2.1 collective-permute-start.5
  154.0 1.9 all-to-all-done.1.p_ref
  156.1 7.4 %shard_map.90 = f32[8,768]{1,0:T(8,128)S(1)} custom-call(s32[32,768]{1,0:T(8,128)S(1)} %get-tuple-element.33.pos_ref, s32[8,768]{1,0:T(8,128)S(1)} %bitcast.49, bf16[32,240,256]{2,1,0:T(8,128)(2,1)} %get-tuple-element.37.q_ref, bf16[32,240,256]{2,1,0:T(8,128)(2,1)} %all-to-all-done.1.p_ref), custom_call_target="tpu_custom_call" | custom-call | bytes 31500000 | tf_op jit(solution)/shard_map/pallas_call | solution.py:253
  163.5 17.9 %all-gather.1 = f32[128,896]{1,0:T(8,128)S(1)} all-gather(f32[8,896]{1,0:T(8,128)S(1)} %select_maximum_fusion), channel_id=3, replica_groups=mesh['dp'=32,'group'=16] {'group'}, dimensions={0}, use_global_device_ids=true | all-gather | bytes 487424 | tf_op jit(solution)/shard_map/all_gather | solution.py:533
  181.8 3.0 %shard_map.92.table_ref = f32[240,32]{1,0:T(8,128)S(1)} custom-call(s32[32,768]{1,0:T(8,128)S(1)} %get-tuple-element.33.pos_ref, f32[32,768]{1,0:T(8,128)S(1)} %get-tuple-element.41.hard_ref), custom_call_target="tpu_custom_call" | custom-call | bytes 17500000 | tf_op jit(solution)/shard_map/pallas_call | solution.py:330
  185.7 14.1 %all-to-all-start.2 = ((f32[32,1,480]{2,1,0:T(1,128)}), f32[32,1,480]{2,1,0:T(1,128)S(1)}, u32[]{:S(2)}, u32[]{:S(2)}) async-start(f32[32,1,480]{2,1,0:T(1,128)} %all_to_all.27), calls=%async_computation.3 | async-start | bytes 131072 | tf_op jit(solution)/shard_map/all_to_all | solution.py:450
  199.8 8.2 %shard_map.93 = (f32[256,768]{1,0:T(8,128)S(1)}, f32[1,256]{1,0:T(1,128)S(1)}) custom-call(s32[32,768]{1,0:T(8,128)S(1)} %get-tuple-element.33.pos_ref, f32[32,768]{1,0:T(8,128)S(1)} %get-tuple-element.41.hard_ref, f32[240,32]{1,0:T(8,128)S(1)} %shard_map.92.table_ref, bf16[32,240,256]{2,1,0:T(8,128)(2,1)} %get-tuple-element.37.q_ref, ...), custom_call_target="tpu_custom_call" | custom-call | bytes 42000000 | tf_op jit(solution)/shard_map/pallas_call | solution.py:364
  208.0 1.2 copy.32
  209.8 9.3 %all-to-all-done.2 = f32[32,1,480]{2,1,0:T(1,128)S(1)} async-done(((f32[32,1,480]{2,1,0:T(1,128)}), f32[32,1,480]{2,1,0:T(1,128)S(1)}, u32[]{:S(2)}, u32[]{:S(2)}) %all-to-all-start.2) | async-done | bytes 61472 | tf_op jit(solution)/shard_map/all_to_all | solution.py:450
  219.3 1.9 shard_map.94.refs_1_
  221.2 1.9 shard_map.95.refs_2_
  223.1 1.9 shard_map.96.refs_3_
  225.0 1.9 shard_map.97.refs_4_
  226.9 0.8 copy-done.1
  227.7 1.9 shard_map.98.refs_5_
  229.6 0.8 copy-done.2
  230.4 1.9 shard_map.99.refs_6_
  232.4 0.8 copy-done.3
  233.1 2.4 select_reduce_fusion
  236.8 3.5 %fusion.16 = (f32[256]{0:T(256)S(1)}, f32[768,256]{1,0:T(8,128)}) fusion(bf16[768,256]{1,0:T(8,128)(2,1)S(1)} %copy-done.10, f32[768]{0:T(1024)S(1)} %get-tuple-element.61, bf16[768,256]{1,0:T(8,128)(2,1)S(1)} %get-tuple-element.75.q_ref, f32[768,768]{1,0:T(8,128)} %all-gather.10.cloned.1.call-done, f32[768]{0:T(1024)S(1)} %get-tuple-element.63), kind=kOutput, calls=%fused_computation.26 | convolution fusion | flops 305921792 | bytes 3939328 | tf_op jit(solution)/shard_map/dot_general | solution.py:24
  240.4 1.6 fusion.9
  242.6 11.4 %all-to-all-start.3 = ((f32[32,1,384]{2,1,0:T(1,128)}), f32[32,1,384]{2,1,0:T(1,128)S(1)}, u32[]{:S(2)}, u32[]{:S(2)}) async-start(f32[32,1,384]{2,1,0:T(1,128)} %broadcast_in_dim.54), calls=%async_computation.4 | async-start | bytes 98304 | tf_op jit(solution)/shard_map/all_to_all | solution.py:450
  254.1 12.5 %shard_map.100 = f32[768,256]{1,0:T(8,128)} custom-call(s32[1]{0:T(128)} %bitcast.9.x_ref, f32[240,32]{1,0:T(8,128)S(1)} %get-tuple-element.71.table_ref, f32[240,32]{1,0:T(8,128)S(1)} %get-tuple-element.70.inverse_ref, f32[1,256]{1,0:T(1,128)S(1)} %bitcast.53, bf16[8,768,1024]{2,1,0:T(8,128)(2,1)} %shard_map.86.match_ref, bf16[8,240,256]{2,1,0:T(8,128)(2,1)} %copy-done, ...), custom_call_target="tpu_custom_call" | custom-call | bytes 24500000 | tf_op jit(solution)/shard_map/pallas_call | solution.py:428
  266.6 1.7 fusion.17
  268.3 17.2 %all-gather.4 = f32[16,1,1920]{2,1,0:T(1,128)S(1)} all-gather(f32[1,1,1920]{2,1,0:T(1,128)S(1)} %reshape.46), channel_id=4, replica_groups=mesh['dp'=32,'group'=16] {'group'}, dimensions={0}, use_global_device_ids=true | all-gather | bytes 130560 | tf_op jit(solution)/shard_map/all_gather | solution.py:580
  287.4 1.4 fusion.13
  (82 shorter events, 7.9 us)
Async XLA Ops:
  8.0 39.0 %copy-start.9 = (bf16[768,256]{1,0:T(8,128)(2,1)S(1)}, bf16[768,256]{1,0:T(8,128)(2,1)}, u32[]{:S(2)}) copy-start(bf16[768,256]{1,0:T(8,128)(2,1)} %param.5) | copy-start | bytes 1179652
  8.0 59.4 %all-gather.8.cloned.1.call-start = ((), (), s32[]{:S(2)}) async-start(), calls=%async_computation.6 | async-start | bytes 3538944 | tf_op jit(solution)/shard_map/all_gather | solution.py:470
  8.7 0.7 copy-start.5
  9.5 0.7 copy-start.7
  11.3 35.6 %all-to-all-start = ((f32[32,1,768]{2,1,0:T(1,128)}), f32[32,1,768]{2,1,0:T(1,128)S(1)}, u32[]{:S(2)}, u32[]{:S(2)}) async-start(f32[32,1,768]{2,1,0:T(1,128)} %copy.29), calls=%async_computation | async-start | bytes 196608 | tf_op jit(solution)/shard_map/all_to_all | solution.py:450
  25.0 85.3 %reduce-scatter.2.cloned.1.call-start = ((), (), s32[]{:S(2)}) async-start(), calls=%async_computation.5 | async-start | bytes 2506752 | tf_op jit(solution)/shard_map/reduce_scatter | solution.py:514
  57.7 98.2 %all-to-all-start.1 = ((bf16[32,240,256]{2,1,0:T(8,128)(2,1)}), bf16[32,240,256]{2,1,0:T(8,128)(2,1)}, u32[]{:S(2)}, u32[]{:S(2)}) async-start(bf16[32,240,256]{2,1,0:T(8,128)(2,1)} %shard_map.88), calls=%async_computation.2 | async-start | bytes 7864320 | tf_op jit(solution)/shard_map/all_to_all | solution.py:450
  67.3 165.8 %all-gather.10.cloned.1.call-start = ((), (), s32[]{:S(2)}) async-start(), calls=%async_computation.7 | async-start | bytes 2506752 | tf_op jit(solution)/shard_map/all_gather | solution.py:524
  70.7 68.5 %collective-permute-start = (bf16[3072,256]{1,0:T(8,128)(2,1)}, bf16[3072,256]{1,0:T(8,128)(2,1)}, u32[]{:S(2)}, u32[]{:S(2)}) collective-permute-start(bf16[3072,256]{1,0:T(8,128)(2,1)} %get-tuple-element.69), channel_id=1, source_target_pairs={{0,128},{16,144},{32,160},{48,176},{64,192},{80,208},{96,224},{112... | collective-permute-start | bytes 4718600 | tf_op jit(solution)/shard_map/ppermute | solution.py:467
  73.8 65.5 %collective-permute-start.1 = (bf16[3072,256]{1,0:T(8,128)(2,1)S(1)}, bf16[3072,256]{1,0:T(8,128)(2,1)}, u32[]{:S(2)}, u32[]{:S(2)}) collective-permute-start(bf16[3072,256]{1,0:T(8,128)(2,1)S(1)} %get-tuple-element.68), channel_id=1, source_target_pairs={{0,384},{16,400},{32,416},{48,432},{64,448},{80,464},{96,480},{112... | collective-permute-start | bytes 4718600 | tf_op jit(solution)/shard_map/ppermute | solution.py:467
  98.7 1.0 copy-start
  139.3 14.6 %copy-start.4 = (f32[48,768]{1,0:T(8,128)S(1)}, f32[48,768]{1,0:T(8,128)}, u32[]{:S(2)}) copy-start(f32[48,768]{1,0:T(8,128)} %reduce-scatter.2.cloned.1.call-done.scores_ref) | copy-start | bytes 442372
  139.3 16.8 %copy-start.6 = (s32[768,8]{0,1:T(8,128)S(1)}, s32[768,8]{0,1:T(8,128)}, u32[]{:S(2)}) copy-start(s32[768,8]{0,1:T(8,128)} %param.7) | copy-start | bytes 73732
  143.2 76.1 %collective-permute-start.2 = (bf16[3072,256]{1,0:T(8,128)(2,1)}, bf16[3072,256]{1,0:T(8,128)(2,1)}, u32[]{:S(2)}, u32[]{:S(2)}) collective-permute-start(bf16[3072,256]{1,0:T(8,128)(2,1)} %get-tuple-element.67), channel_id=1, source_target_pairs={{0,384},{16,400},{32,416},{48,432},{64,448},{80,464},{96,480},{112... | collective-permute-start | bytes 4718600 | tf_op jit(solution)/shard_map/ppermute | solution.py:467
  145.2 74.1 %collective-permute-start.3 = (bf16[3072,256]{1,0:T(8,128)(2,1)}, bf16[3072,256]{1,0:T(8,128)(2,1)}, u32[]{:S(2)}, u32[]{:S(2)}) collective-permute-start(bf16[3072,256]{1,0:T(8,128)(2,1)} %collective-permute-done.q_ref), channel_id=1, source_target_pairs={{0,128},{16,144},{32,160},{48,176},{64,192},{80,208},{96,224},{112... | collective-permute-start | bytes 4718600 | tf_op jit(solution)/shard_map/ppermute | solution.py:467
  148.5 70.8 %collective-permute-start.4 = (bf16[3072,256]{1,0:T(8,128)(2,1)}, bf16[3072,256]{1,0:T(8,128)(2,1)}, u32[]{:S(2)}, u32[]{:S(2)}) collective-permute-start(bf16[3072,256]{1,0:T(8,128)(2,1)} %collective-permute-done.1.q_ref), channel_id=1, source_target_pairs={{0,384},{16,400},{32,416},{48,432},{64,448},{80,464},{96,480},{112... | collective-permute-start | bytes 4718600 | tf_op jit(solution)/shard_map/ppermute | solution.py:467
  151.7 67.6 %collective-permute-start.5 = (bf16[3072,256]{1,0:T(8,128)(2,1)}, bf16[3072,256]{1,0:T(8,128)(2,1)}, u32[]{:S(2)}, u32[]{:S(2)}) collective-permute-start(bf16[3072,256]{1,0:T(8,128)(2,1)} %get-tuple-element.66), channel_id=1, source_target_pairs={{0,128},{16,144},{32,160},{48,176},{64,192},{80,208},{96,224},{112... | collective-permute-start | bytes 4718600 | tf_op jit(solution)/shard_map/ppermute | solution.py:467
  185.7 33.5 %all-to-all-start.2 = ((f32[32,1,480]{2,1,0:T(1,128)}), f32[32,1,480]{2,1,0:T(1,128)S(1)}, u32[]{:S(2)}, u32[]{:S(2)}) async-start(f32[32,1,480]{2,1,0:T(1,128)} %all_to_all.27), calls=%async_computation.3 | async-start | bytes 131072 | tf_op jit(solution)/shard_map/all_to_all | solution.py:450
  226.9 0.8 copy-start.1
  229.6 0.8 copy-start.2
  230.4 6.4 %copy-start.10 = (bf16[768,256]{1,0:T(8,128)(2,1)S(1)}, bf16[768,256]{1,0:T(8,128)(2,1)}, u32[]{:S(2)}) copy-start(bf16[768,256]{1,0:T(8,128)(2,1)} %param.6) | copy-start | bytes 1179652
  232.3 0.8 copy-start.3
  236.8 3.5 %copy-start.13 = (f32[768,768]{1,0:T(8,128)S(1)}, f32[768,768]{1,0:T(8,128)}, u32[]{:S(2)}) copy-start(f32[768,768]{1,0:T(8,128)} %all-gather.10.cloned.1.call-done) | copy-start | bytes 7077892
  236.8 3.5 %copy-start.15 = (f32[256,768]{0,1:T(8,128)S(1)}, f32[256,768]{0,1:T(8,128)}, u32[]{:S(2)}) copy-start(f32[256,768]{0,1:T(8,128)} %copy.32) | copy-start | bytes 2359300
  242.6 25.6 %all-to-all-start.3 = ((f32[32,1,384]{2,1,0:T(1,128)}), f32[32,1,384]{2,1,0:T(1,128)S(1)}, u32[]{:S(2)}, u32[]{:S(2)}) async-start(f32[32,1,384]{2,1,0:T(1,128)} %broadcast_in_dim.54), calls=%async_computation.4 | async-start | bytes 98304 | tf_op jit(solution)/shard_map/all_to_all | solution.py:450
  254.1 12.5 %copy-start.11 = (f32[768,256]{1,0:T(8,128)S(1)}, f32[768,256]{1,0:T(8,128)}, u32[]{:S(2)}) copy-start(f32[768,256]{1,0:T(8,128)} %get-tuple-element.79) | copy-start | bytes 2359300
  266.5 20.8 %copy-start.8 = (f32[768,256]{1,0:T(8,128)S(1)}, f32[768,256]{1,0:T(8,128)}, u32[]{:S(2)}) copy-start(f32[768,256]{1,0:T(8,128)} %shard_map.100) | copy-start | bytes 2359300
  266.5 20.8 %copy-start.12 = (f32[768,256]{1,0:T(8,128)S(1)}, f32[768,256]{1,0:T(8,128)}, u32[]{:S(2)}) copy-start(f32[768,256]{1,0:T(8,128)} %get-tuple-element.79) | copy-start | bytes 2359300
  266.5 20.8 %copy-start.14 = (f32[768,256]{1,0:T(8,128)S(1)}, f32[768,256]{1,0:T(8,128)}, u32[]{:S(2)}) copy-start(f32[768,256]{1,0:T(8,128)} %get-tuple-element.77) | copy-start | bytes 2359300
Sparse Core Ops, SparseCore 0:
  10.9 53.9 all-gather.7
Sparse Core Ops, SparseCore 1:
  50.3 59.9 reduce-scatter.1
  139.4 45.0 all-gather.9

commit v3 on v2

--- a/solution.py
+++ b/solution.py
@@ -132,32 +132,24 @@
 
 
 def match_kernel(code_ref, match_ref):
-    step = pl.program_id(0)
-    rows, wide = match_ref.shape[1:]
-    many = 4
-    each = wide // many
-    part = iota((8, rows), 0)
-    for t in range(many):
-        pos, asked = decode(code_ref, step * many + t)
-        asked = asked + 1
-        digits = jnp.where(part == 0, asked >> 5, jnp.where(part == 1, asked & 31, 0))
-        pick = one_hot(iota((each, rows), 0) == pos)
-        found = contract(digits.astype(F32).astype(BF16), pick, 1, 1)
-        wanted = (found[0:1, :] * 32.0 + found[1:2, :]).astype(jnp.int32) - 1
-        match_ref[0, :, t * each : (t + 1) * each] = one_hot(iota((rows, each), 0) == wanted)
-
-
-def make_match(code, many, each):
+    rows = match_ref.shape[2]
+    cap = match_ref.shape[1] // MANY
+    for t in range(MANY):
+        pos, asked = decode(code_ref, pl.program_id(0) * MANY + t)
+        wanted = slot_value(pos, (asked + 1).astype(F32), cap).astype(jnp.int32) - 1
+        match_ref[0, t * cap : (t + 1) * cap, :] = one_hot(iota((cap, rows), 1) == wanted)
+
+
+def make_match(code, cap):
     n_data, rows = code.shape
-    wide = many * each
-    steps = n_data // many
+    steps = n_data // MANY
     return call(
         match_kernel,
         steps,
         [whole((n_data, rows))],
-        slab(rows, wide),
-        jax.ShapeDtypeStruct((steps, rows, wide), BF16),
-        10,
+        slab(MANY * cap, rows),
+        jax.ShapeDtypeStruct((steps, MANY * cap, rows), BF16),
+        8,
     )(code)
 
 
@@ -194,33 +186,53 @@
     )(pos, q_emb, inverse)
 
 
-def collect_kernel(base_ref, code_ref, q_ref, slot_ref):
+def collect_kernel(first, counts, base_ref, code_ref, *refs):
+    q_refs, slot_ref = refs[:-1], refs[-1]
+    step = pl.program_id(0)
     many, cap, _ = slot_ref.shape
     rows = code_ref.shape[1]
-    for t in range(many):
-        pos, _ = decode(code_ref, base_ref[0] + pl.program_id(0) * many + t)
-        pick = slot_pick(pos, jnp.ones((), BF16), cap)
-        found = contract(pick, q_ref[t * rows : (t + 1) * rows, :], 1, 0)
-        slot_ref[t] = found.astype(BF16)
-
-
-def collect(base, code, part, cap):
+
+    def fill(q_ref, source):
+        for t in range(many):
+            pos, _ = decode(code_ref, source + t)
+            pick = slot_pick(pos, jnp.ones((), BF16), cap)
+            found = contract(pick, q_ref[t * rows : (t + 1) * rows, :], 1, 0)
+            slot_ref[t] = found.astype(BF16)
+
+    start = 0
+    for place, count in enumerate(counts):
+        source = base_ref[first + place] + (step - start) * many
+        pl.when((step >= start) & (step < start + count))(
+            functools.partial(fill, q_refs[place], source)
+        )
+        start += count
+
+
+def collect(base, first, code, cap, parts):
     n_data, rows = code.shape
-    piece = part.shape[1]
-    count = part.shape[0] // rows
+    piece = parts[0].shape[1]
     many = 2
-    return call(
-        collect_kernel,
-        count // many,
+    counts = [part.shape[0] // (rows * many) for part in parts]
+    starts = [sum(counts[:i]) for i in range(len(counts))]
+
+    def spec(start, count):
+        return pl.BlockSpec(
+            (many * rows, piece), lambda i: (jnp.clip(i - start, 0, count - 1), 0)
+        )
+
+    steps = sum(counts)
+    return call(
+        functools.partial(collect_kernel, first, counts),
+        steps,
         [
             pl.BlockSpec(memory_space=pltpu.SMEM),
             whole((n_data, rows)),
-            pl.BlockSpec((many * rows, piece), lambda i: (i, 0)),
+            *[spec(start, count) for start, count in zip(starts, counts)],
         ],
         slab(cap, piece, many),
-        jax.ShapeDtypeStruct((count, cap, piece), BF16),
-        0.5 * count,
-    )(base, code, part)
+        jax.ShapeDtypeStruct((steps * many, cap, piece), BF16),
+        0.3 * steps * many,
+    )(base, code, *parts)
 
 
 def near_kernel(scale, pos_ref, owner_ref, q_ref, p_ref, near_ref):
@@ -378,72 +390,77 @@
     )(pos, hard, table, q_slots, p_slots)
 
 
-def pair_kernel(scale, nz, x_ref, table_ref, inverse_ref, gain_ref, match_ref, *refs):
-    q_refs, (total_ref, pairs_ref) = refs[:7], refs[7:]
+def pair_kernel(scale, spans, base_ref, table_ref, gain_ref, match_ref, *refs):
+    q_refs, (total_ref, pairs_ref, split_ref) = refs[: len(spans)], refs[len(spans) :]
     step = pl.program_id(0)
-    many, cap, _ = q_refs[0].shape
-    each = pairs_ref.shape[0] // many
-    nx = pl.num_programs(0) * many // nz
-    first = lax.rem(x_ref[0] * nz + step * many, nx * nz)
+    many, cap, piece = q_refs[0].shape
+    wide = table_ref.shape[1]
+    n_data = wide // 4
 
     @pl.when(step == 0)
     def _():
         total_ref[...] = jnp.zeros_like(total_ref)
-        pairs_ref[...] = jnp.zeros_like(pairs_ref)
+        table = table_ref[...]
+        high = table.astype(BF16).astype(F32)
+        middle = (table - high).astype(BF16).astype(F32)
+        low = table - high - middle
+        place = iota(table.shape, 1) // n_data
+        split = jnp.where(place == 3, low, jnp.where(place == 2, middle, high))
+        split_ref[...] = split.astype(BF16)
+
+    lane = iota((wide, many * 128), 0)
+    wanted = base_ref[step] + iota((wide, many * 128), 1) // 128
+    weights = contract(split_ref[...], one_hot(lane == wanted), 1, 0) * scale
+    spread = (lane >= n_data) & (lane % n_data == wanted)
+    inverses = contract(split_ref[...], one_hot(spread), 1, 0)
 
     def fill(q_ref):
         for t in range(many):
-            weight = table_column(table_ref, first + t)
-            inverse = table_column(inverse_ref, first + t)
-            emb = ((q_ref[t].astype(F32) * inverse) * gain_ref[...]).astype(BF16)
-            pairs = ((weight * scale) * emb.astype(F32)).astype(BF16)
-            pairs_ref[t * each : t * each + cap, :] = pairs
-
-    half = nz // many
-    for place, (low, high) in enumerate(pair_spans(half)):
+            for lanes in range(0, piece, 128):
+                span = slice(lanes, lanes + 128)
+                raw = q_ref[t, :, span].astype(F32)
+                column = slice(t * 128, (t + 1) * 128)
+                emb = ((raw * inverses[:, column]) * gain_ref[:, span]).astype(BF16)
+                pairs = (weights[:, column] * emb.astype(F32)).astype(BF16)
+                pairs_ref[t * cap : (t + 1) * cap, span] = pairs
+
+    for place, (low, high) in enumerate(spans):
         pl.when((step >= low) & (step < high))(functools.partial(fill, q_refs[place]))
-    total_ref[...] += contract(match_ref[0], pairs_ref[...], 1, 0)
-
-
-def pair_spans(half):
-    quarter = half // 2
-    return [(0, half)] + [(half + i * quarter, half + (i + 1) * quarter) for i in range(6)]
-
-
-def pair_grad(scale, nz, x, table, inverse, gain, match, parts):
-    cap, n_data = table.shape
-    steps, rows, wide = match.shape
+    total_ref[...] += contract(pairs_ref[...], match_ref[0], 0, 0)
+
+
+def pair_grad(scale, base, table, gain, match, parts):
+    cap, wide = table.shape
+    steps, deep, rows = match.shape
     piece = parts[0].shape[2]
-    many = n_data // steps
+    many = wide // 4 // steps
+    ends = [sum(part.shape[0] for part in parts[: i + 1]) // many for i in range(len(parts))]
+    spans = list(zip([0] + ends[:-1], ends))
 
     def part_spec(span):
         low, high = span
         return pl.BlockSpec(
-            (many, cap, piece), lambda i, x_ref: (jnp.clip(i, low, high - 1) - low, 0, 0)
+            (many, cap, piece), lambda i, base_ref: (jnp.clip(i, low, high - 1) - low, 0, 0)
         )
 
-    def match_block(i, x_ref):
-        return (lax.rem(x_ref[0] * (nz // many) + i, steps), 0, 0)
-
     return pl.pallas_call(
-        functools.partial(pair_kernel, scale, nz),
+        functools.partial(pair_kernel, scale, spans),
         grid_spec=pltpu.PrefetchScalarGridSpec(
             num_scalar_prefetch=1,
             grid=(steps,),
             in_specs=[
-                pl.BlockSpec((cap, n_data), lambda i, x_ref: (0, 0)),
-                pl.BlockSpec((cap, n_data), lambda i, x_ref: (0, 0)),
-                pl.BlockSpec((1, piece), lambda i, x_ref: (0, 0)),
-                pl.BlockSpec((1, rows, wide), match_block),
-                *[part_spec(span) for span in pair_spans(nz // many)],
+                pl.BlockSpec((cap, wide), lambda i, base_ref: (0, 0)),
+                pl.BlockSpec((1, piece), lambda i, base_ref: (0, 0)),
+                pl.BlockSpec((1, deep, rows), lambda i, base_ref: (base_ref[i] // many, 0, 0)),
+                *[part_spec(span) for span in spans],
             ],
-            out_specs=pl.BlockSpec((rows, piece), lambda i, x_ref: (0, 0)),
-            scratch_shapes=[pltpu.VMEM((wide, piece), BF16)],
+            out_specs=pl.BlockSpec((piece, rows), lambda i, base_ref: (0, 0)),
+            scratch_shapes=[pltpu.VMEM((deep, piece), BF16), pltpu.VMEM((cap, wide), BF16)],
         ),
-        out_shape=jax.ShapeDtypeStruct((rows, piece), F32),
+        out_shape=jax.ShapeDtypeStruct((piece, rows), F32),
         compiler_params=pltpu.CompilerParams(vmem_limit_bytes=VMEM_LIMIT),
-        cost_estimate=cost(7),
-    )(x, table, inverse, gain, match, *parts)
+        cost_estimate=cost(10),
+    )(base, table, gain, match, *parts)
 
 
 def swap(x, axis):
@@ -486,8 +503,9 @@
     gain_row = my_gain[None, :]
     owner_t = neg_owner.T
 
-    def base(away, more=0):
-        return jnp.full((1,), (my_x + away) % nx * nz + more, jnp.int32)
+    away = jnp.array([0, 0, 3, 1, 1, 3, 2, 2], jnp.int32)
+    upper = jnp.array([0, 1, 0, 1, 0, 1, 0, 1], jnp.int32)
+    base = (my_x + away) % nx * nz + upper * (nz // 2)
 
     q_zero = torus.gather_z(queries)
     half = q_zero.shape[0] // 2
@@ -513,18 +531,19 @@
     scores = contract(q_emb, p_emb, 1, 1) * scale
     scores = lax.psum_scatter(scores, "group", scatter_dimension=0, tiled=True)
     q_slots, inverse = make_slots(pos, q_emb, inverses[:1], cap)
-    each = -(-cap // 128) * 128
-    match = make_match(code_got, 4, each)
-    q_three_low, q_one_high = torus.shift(q_zero[:half], 1), torus.shift(q_zero[half:], -1)
-    part_zero = collect(base(0), code_got, q_zero, cap)
-    scores, q_slots, match, q_three_low, q_one_high, q_zero, part_zero = tied(
-        scores, q_slots, match, q_three_low, q_one_high, q_zero, part_zero
+    match = make_match(code_got, cap)
+    q_lower, q_upper = q_zero[:half], q_zero[half:]
+    q_three_low, q_one_high = torus.shift(q_lower, 1), torus.shift(q_upper, -1)
+    part_zero = collect(base, 0, code_got, cap, [q_zero])
+    scores, q_slots, match, q_three_low, q_one_high, q_lower, q_upper, part_zero = tied(
+        scores, q_slots, match, q_three_low, q_one_high, q_lower, q_upper, part_zero
     )
     stats = batch_stats(scores)
     scores = lax.all_gather(scores, "group", axis=0, tiled=True)
-    q_one_low, q_three_high = torus.shift(q_zero[:half], -1), torus.shift(q_zero[half:], 1)
+    q_one_low, q_three_high = torus.shift(q_lower, -1), torus.shift(q_upper, 1)
     q_low, q_high = torus.shift(q_three_low, 1), torus.shift(q_one_high, -1)
-    p_slots, stats = tied(p_slots, stats)
+    part_first = collect(base, 2, code_got, cap, [q_three_low, q_one_high])
+    p_slots, stats, part_first = tied(p_slots, stats, part_first)
 
     near = near_scores(scale, pos, owner_t, q_slots, p_slots)
     share = rows // n_members
@@ -536,23 +555,6 @@
     stats = stats.transpose(1, 0, 2).reshape(2, rows)
     hard, lse = softmax_all(owner_t, near, stats, n_data)
     table = weigh_slots(pos, hard, cap)
-    _, q_one_low, q_one_high, q_low, q_high, q_three_low, q_three_high = tied(
-        hard, q_one_low, q_one_high, q_low, q_high, q_three_low, q_three_high
-    )
-    got = swap(jnp.concatenate([table, inverse], axis=0).T, "dp").T
-
-    parts = [part_zero] + [
-        collect(at, code_got, part, cap)
-        for at, part in (
-            (base(1), q_one_low),
-            (base(1, nz // 2), q_one_high),
-            (base(2), q_low),
-            (base(2, nz // 2), q_high),
-            (base(3), q_three_low),
-            (base(3, nz // 2), q_three_high),
-        )
-    ]
-
     hard_q, pair_gain = hard_grad(scale, pos, hard, table, q_slots, p_slots)
     lse = lse[0][:, None]
     positive = iota((rows, rows), 0) == iota((rows, rows), 1)
@@ -566,12 +568,18 @@
         + pair_gain[0] / my_gain
     )
     last = jnp.concatenate([gain_part, jnp.broadcast_to(losses, (128,))])
-    last, got = tied(last, got)
-    last = jnp.sum(swap(jnp.broadcast_to(last[None, :], (n_data, piece + 128)), "dp"), axis=0)
-
-    grad_p = batch_grad + pair_grad(
-        scale, nz, jnp.full((1,), my_x), got[:cap], got[cap:], gain_row, match, parts
-    )
+    _, q_one_low, q_three_high, q_low, q_high = tied(last, q_one_low, q_three_high, q_low, q_high)
+    sent = jnp.concatenate([table, inverse, jnp.zeros((-2 * cap % 128, n_data), F32)], axis=0).T
+    edge = sent.shape[1]
+    sent = jnp.concatenate([sent, jnp.broadcast_to(last[None, :], (n_data, piece + 128))], axis=1)
+    got = swap(sent, "dp")
+    last = jnp.sum(got[:, edge:], axis=0)
+    got_weights, got_inverses = got[:, :cap].T, got[:, cap : 2 * cap].T
+    table = jnp.concatenate([got_weights] + [got_inverses] * 3, axis=1)
+
+    part_last = collect(base, 4, code_got, cap, [q_one_low, q_three_high, q_low, q_high])
+    parts = [part_zero, part_first, part_last]
+    grad_p = batch_grad + pair_grad(scale, base, table, gain_row, match, parts).T
     q_inner = grad_q * my_gain
     p_inner = grad_p * my_gain
     final = jnp.concatenate(

time: 299 us -> 278 us (0.930)
  starting transfers between devices: 65.9 us -> 54.2 us
  waiting for transfers between devices: 51.6 us -> 44 us
  other arithmetic: 10.7 us -> 6.6 us
    all_to_all x4 -> x3, starting transfers between devices: 48.8 us -> 35.8 us  [swap(): return lax.all_to_all(x, axis, split_axis=0, concat_axis=0, tiled=True)]
    all_to_all x4 -> x3, waiting for transfers between devices: 11.2 us -> 0.79 us  [swap(): return lax.all_to_all(x, axis, split_axis=0, concat_axis=0, tiled=True)]
    unnamed x36 -> x64, local copies, waits for them, and re-layouts: 5.45 us -> 10.4 us
    slice x3 -> x1, local copies, waits for them, and re-layouts: 7.17 us -> 3.78 us  [local(): q_lower, q_upper = (q_zero[:half], q_zero[half:])]
    pallas_call x9 -> x5, Pallas kernels: 37.8 us -> 35.8 us  [the longest x3 15.4 us: collect(): call(functools.partial(collect_kernel, first, counts), steps, [pl.BlockSp...]
  transfers between devices with their start and end apart: 13 -> 12, of which waited for: 4 -> 4; matrix products, arithmetic and copies ran while one was open for 6% -> 8% of each run, Pallas kernels for 24% -> 21%
where the time goes in v3:
time: 278 us; the launch traced here: 274 us
  Pallas kernels  70.2 us (25%)
  blocking collectives  55.1 us (20%)
  starting transfers between devices  54.2 us (19%)
  waiting for transfers between devices  44 us (16%)
  between operations  19.3 us (7%)
  local copies, waits for them, and re-layouts  17.4 us (6%)
  matrix products  7.29 us (3%)
  other arithmetic  6.6 us (2%)
    all_to_all x3, starting transfers between devices, swap(): return lax.all_to_all(x, axis, split_axis=0, concat_axis=0, tiled=True)  35.8 us
    ppermute x6, waiting for transfers between devices, shift(): return lax.ppermute(value, 'dp', pairs)  28.8 us
    all_gather x1, blocking collectives, local(): lax.all_gather(jnp.concatenate([near, stats], axis=1), 'group', axis=0)  19.1 us
    all_gather x1, blocking collectives, local(): squares = jnp.sum(lax.all_gather(squares, 'group', axis=0), axis=0)  18.6 us
    ppermute x6, starting transfers between devices, shift(): return lax.ppermute(value, 'dp', pairs)  18.2 us
    all_gather x1, blocking collectives, local(): final = lax.all_gather(final, 'group', axis=0)  17.4 us
    pallas_call x3, Pallas kernels, collect(): call(functools.partial(collect_kernel, first, counts), steps, [pl.BlockSp...  15.4 us
    reduce_scatter x1, waiting for transfers between devices, local(): scores = lax.psum_scatter(scores, 'group', scatter_dimension=0, tiled=True)  13.6 us
  transfers between devices with their start and end apart: 12, of which 4 were waited for; matrix products, arithmetic and copies ran while one was open for 8% of the time, Pallas kernels for 21%

profile of v3, /device:TPU:1, one launch (start us, length us, event | category | flops | bytes accessed | tf_op | source)
XLA Modules:
  0.0 274.0 jit_solution(1294657590514600112)
XLA Ops:
  8.0 0.7 all-gather.8.cloned.1.call-update
  8.7 0.7 copy-done.2
  9.5 0.7 copy-done.4
  10.5 0.7 copy.33
  11.3 13.7 %all-to-all-start = ((f32[32,1,768]{2,1,0:T(1,128)}), f32[32,1,768]{2,1,0:T(1,128)S(1)}, u32[]{:S(2)}, u32[]{:S(2)}) async-start(f32[32,1,768]{2,1,0:T(1,128)} %copy.33), calls=%async_computation | async-start | bytes 196608 | tf_op jit(solution)/shard_map/all_to_all | solution.py:467
  25.0 1.2 copy.31
  26.2 1.3 copy.32
  27.8 18.6 %all-gather.3 = f32[16,2,768]{2,1,0:T(2,128)S(1)} all-gather(f32[1,2,768]{2,1,0:T(2,128)S(1)} %maximum_bitcast_fusion.1), channel_id=2, replica_groups=mesh['dp'=32,'group'=16] {'group'}, dimensions={0}, use_global_device_ids=true | all-gather | bytes 104448 | tf_op jit(solution)/shard_map/all_gather | solution.py:521
  46.5 1.3 broadcast_multiply_fusion.1
  48.1 1.9 convolution_multiply_fusion
  50.2 7.5 %shard_map.106 = bf16[32,240,256]{2,1,0:T(8,128)(2,1)} custom-call(f32[32,768]{1,0:T(8,128)S(1)} %bitcast.41, bf16[768,256]{1,0:T(8,128)(2,1)S(1)} %copy.35.p_ref), custom_call_target="tpu_custom_call" | custom-call | bytes 28000000 | tf_op jit(solution)/shard_map/pallas_call | solution.py:123
  57.7 9.6 %all-to-all-start.1 = ((bf16[32,240,256]{2,1,0:T(8,128)(2,1)}), bf16[32,240,256]{2,1,0:T(8,128)(2,1)}, u32[]{:S(2)}, u32[]{:S(2)}) async-start(bf16[32,240,256]{2,1,0:T(8,128)(2,1)} %shard_map.106), calls=%async_computation.2 | async-start | bytes 7864320 | tf_op jit(solution)/shard_map/all_to_all | solution.py:467
  67.4 3.8 %fusion.28 = (bf16[3072,256]{1,0:T(8,128)(2,1)}, bf16[3072,256]{1,0:T(8,128)(2,1)}) fusion(bf16[6144,256]{1,0:T(8,128)(2,1)} %all-gather.8.cloned.1.call-done.refs_0_), kind=kLoop, calls=%fused_computation.62 | loop fusion | bytes 6291456 | tf_op jit(solution)/shard_map/slice | solution.py:535
  71.2 3.1 %collective-permute-start = (bf16[3072,256]{1,0:T(8,128)(2,1)}, bf16[3072,256]{1,0:T(8,128)(2,1)S(1)}, u32[]{:S(2)}, u32[]{:S(2)}) collective-permute-start(bf16[3072,256]{1,0:T(8,128)(2,1)} %get-tuple-element.48), channel_id=1, source_target_pairs={{0,128},{16,144},{32,160},{48,176},{64,192},{80,208},{96,224},{112... | collective-permute-start | bytes 4718600 | tf_op jit(solution)/shard_map/ppermute | solution.py:484
  74.3 3.4 %collective-permute-start.1 = (bf16[3072,256]{1,0:T(8,128)(2,1)}, bf16[3072,256]{1,0:T(8,128)(2,1)}, u32[]{:S(2)}, u32[]{:S(2)}) collective-permute-start(bf16[3072,256]{1,0:T(8,128)(2,1)} %get-tuple-element.49), channel_id=1, source_target_pairs={{0,384},{16,400},{32,416},{48,432},{64,448},{80,464},{96,480},{112... | collective-permute-start | bytes 4718600 | tf_op jit(solution)/shard_map/ppermute | solution.py:484
  78.0 7.6 %shard_map.104.match_ref = bf16[8,960,768]{2,1,0:T(8,128)(2,1)} custom-call(f32[32,768]{1,0:T(8,128)S(1)} %bitcast.42), custom_call_target="tpu_custom_call" | custom-call | bytes 28000000 | tf_op jit(solution)/shard_map/pallas_call | solution.py:146
  85.5 7.6 %shard_map.103 = (bf16[32,240,256]{2,1,0:T(8,128)(2,1)}, f32[240,32]{1,0:T(8,128)S(1)}) custom-call(s32[32,768]{1,0:T(8,128)S(1)} %get-tuple-element.31.pos_ref, bf16[768,256]{1,0:T(8,128)(2,1)S(1)} %copy.34.q_ref, f32[1,768]{1,0:T(1,128)S(1)} %get-tuple-element.80.inverse_ref), custom_call_target="tpu_custom_call" | custom-call | bytes 31500000 | tf_op jit(solution)/shard_map/pallas_call | solution.py:175
  93.2 3.5 %shard_map.105.refs_0_ = bf16[8,240,256]{2,1,0:T(8,128)(2,1)S(1)} custom-call(s32[8]{0:T(128)S(1)} %fusion.26.base_ref, f32[32,768]{1,0:T(8,128)S(1)} %bitcast.43, bf16[6144,256]{1,0:T(8,128)(2,1)} %all-gather.8.cloned.1.call-done.refs_0_), custom_call_target="tpu_custom_call" | custom-call | bytes 8400000 | tf_op jit(solution)/shard_map/pallas_call | solution.py:224
  96.7 13.6 %reduce-scatter.2.cloned.1.call-done.scores_ref = f32[48,768]{1,0:T(8,128)} async-done(((f32[768,768]{1,0:T(8,128)}), f32[48,768]{1,0:T(8,128)}) %reduce-scatter.2.cloned.1.call-update) | async-done | bytes 147472 | tf_op jit(solution)/shard_map/reduce_scatter | solution.py:532
  110.3 28.7 %collective-permute-done.refs_0_ = bf16[3072,256]{1,0:T(8,128)(2,1)S(1)} collective-permute-done((bf16[3072,256]{1,0:T(8,128)(2,1)}, bf16[3072,256]{1,0:T(8,128)(2,1)S(1)}, u32[]{:S(2)}, u32[]{:S(2)}) %collective-permute-start) | collective-permute-done | bytes 1572896 | tf_op jit(solution)/shard_map/ppermute | solution.py:484
  139.0 1.1 copy-done.17
  140.3 0.9 copy-done.1
  141.4 3.0 %collective-permute-start.4 = (bf16[3072,256]{1,0:T(8,128)(2,1)}, bf16[3072,256]{1,0:T(8,128)(2,1)}, u32[]{:S(2)}, u32[]{:S(2)}) collective-permute-start(bf16[3072,256]{1,0:T(8,128)(2,1)} %copy-done.17), channel_id=1, source_target_pairs={{0,128},{16,144},{32,160},{48,176},{64,192},{80,208},{96,224},{112... | collective-permute-start | bytes 4718600 | tf_op jit(solution)/shard_map/ppermute | solution.py:484
  144.4 3.7 %shard_map.108.refs_1_ = bf16[8,240,256]{2,1,0:T(8,128)(2,1)S(1)} custom-call(s32[8]{0:T(128)S(1)} %fusion.26.base_ref, f32[32,768]{1,0:T(8,128)S(1)} %bitcast.44, bf16[3072,256]{1,0:T(8,128)(2,1)} %copy-done.17, bf16[3072,256]{1,0:T(8,128)(2,1)} %collective-permute-done.1.refs_1_), custom_call_target="tpu_custom_call" | custom-call | bytes 8400000 | tf_op jit(solution)/shard_map/pallas_call | solution.py:224
  148.2 1.0 copy-done
  149.1 3.5 %collective-permute-start.5 = (bf16[3072,256]{1,0:T(8,128)(2,1)}, bf16[3072,256]{1,0:T(8,128)(2,1)}, u32[]{:S(2)}, u32[]{:S(2)}) collective-permute-start(bf16[3072,256]{1,0:T(8,128)(2,1)} %collective-permute-done.1.refs_1_), channel_id=1, source_target_pairs={{0,384},{16,400},{32,416},{48,432},{64,448},{80,464},{96,480},{112... | collective-permute-start | bytes 4718600 | tf_op jit(solution)/shard_map/ppermute | solution.py:484
  152.6 2.0 collective-permute-start.2
  154.6 3.3 %collective-permute-start.3 = (bf16[3072,256]{1,0:T(8,128)(2,1)}, bf16[3072,256]{1,0:T(8,128)(2,1)}, u32[]{:S(2)}, u32[]{:S(2)}) collective-permute-start(bf16[3072,256]{1,0:T(8,128)(2,1)} %get-tuple-element.49), channel_id=1, source_target_pairs={{0,128},{16,144},{32,160},{48,176},{64,192},{80,208},{96,224},{112... | collective-permute-start | bytes 4718600 | tf_op jit(solution)/shard_map/ppermute | solution.py:484
  158.1 7.4 %shard_map.109 = f32[8,768]{1,0:T(8,128)S(1)} custom-call(s32[32,768]{1,0:T(8,128)S(1)} %get-tuple-element.31.pos_ref, s32[8,768]{1,0:T(8,128)S(1)} %bitcast.47, bf16[32,240,256]{2,1,0:T(8,128)(2,1)} %get-tuple-element.35.q_ref, bf16[32,240,256]{2,1,0:T(8,128)(2,1)} %all-to-all-done.1.p_ref), custom_call_target="tpu_custom_call" | custom-call | bytes 31500000 | tf_op jit(solution)/shard_map/pallas_call | solution.py:265
  165.5 19.1 %all-gather.1 = f32[128,896]{1,0:T(8,128)S(1)} all-gather(f32[8,896]{1,0:T(8,128)S(1)} %select_maximum_fusion), channel_id=3, replica_groups=mesh['dp'=32,'group'=16] {'group'}, dimensions={0}, use_global_device_ids=true | all-gather | bytes 487424 | tf_op jit(solution)/shard_map/all_gather | solution.py:552
  185.1 3.0 %shard_map.111.table_ref = f32[240,32]{1,0:T(8,128)S(1)} custom-call(s32[32,768]{1,0:T(8,128)S(1)} %get-tuple-element.31.pos_ref, f32[32,768]{1,0:T(8,128)S(1)} %get-tuple-element.41.hard_ref), custom_call_target="tpu_custom_call" | custom-call | bytes 17500000 | tf_op jit(solution)/shard_map/pallas_call | solution.py:342
  188.1 0.7 fusion.27
  188.8 0.7 maximum_bitcast_fusion
  189.6 8.2 %shard_map.112 = (f32[256,768]{1,0:T(8,128)S(1)}, f32[1,256]{1,0:T(1,128)S(1)}) custom-call(s32[32,768]{1,0:T(8,128)S(1)} %get-tuple-element.31.pos_ref, f32[32,768]{1,0:T(8,128)S(1)} %get-tuple-element.41.hard_ref, f32[240,32]{1,0:T(8,128)S(1)} %shard_map.111.table_ref, bf16[32,240,256]{2,1,0:T(8,128)(2,1)} %get-tuple-element.35.q_ref, ...), custom_call_target="tpu_custom_call" | custom-call | bytes 42000000 | tf_op jit(solution)/shard_map/pallas_call | solution.py:376
  197.7 0.9 copy-done.5
  198.6 2.4 select_reduce_fusion
  202.4 3.7 %fusion.16 = (f32[256]{0:T(256)S(1)}, f32[768,256]{0,1:T(8,128)}) fusion(bf16[768,256]{0,1:T(8,128)(2,1)} %copy-done.7, f32[768]{0:T(1024)S(1)} %get-tuple-element.69, bf16[768,256]{0,1:T(8,128)(2,1)} %copy-done.14, f32[768,768]{1,0:T(8,128)} %all-gather.10.cloned.1.call-done, f32[768]{0:T(1024)S(1)} %copy-done.25), kind=kOutput, calls=%fused_computation.26 | convolution fusion | flops 305921792 | bytes 3939328 | tf_op jit(solution)/shard_map/dot_general | solution.py:24
  206.1 1.7 fusion.9
  207.9 0.7 all_to_all.23
  208.6 12.5 %all-to-all-start.2 = ((f32[32,1,896]{2,1,0:T(1,128)}), f32[32,1,896]{2,1,0:T(1,128)S(1)}, u32[]{:S(2)}, u32[]{:S(2)}) async-start(f32[32,1,896]{2,1,0:T(1,128)} %all_to_all.23), calls=%async_computation.3 | async-start | bytes 229376 | tf_op jit(solution)/shard_map/all_to_all | solution.py:467
  221.3 8.2 %shard_map.113.refs_2_ = bf16[16,240,256]{2,1,0:T(8,128)(2,1)} custom-call(s32[8]{0:T(128)S(1)} %fusion.26.base_ref, f32[32,768]{1,0:T(8,128)S(1)} %bitcast.45, bf16[3072,256]{1,0:T(8,128)(2,1)S(1)} %collective-permute-done.2.refs_0_, bf16[3072,256]{1,0:T(8,128)(2,1)} %collective-permute-done.3.refs_1_, bf16[3072,256]{1,0:T(8,128)(2,1)} %collective-permute-done.4.refs_2_, ...), custom_call_target="tpu_custom_call" | custom-call | bytes 16800000 | tf_op jit(solution)/shard_map/pallas_call | solution.py:224
  229.5 0.8 all-to-all-done.2
  230.8 12.8 %shard_map.114 = f32[256,768]{1,0:T(8,128)S(1)} custom-call(s32[8]{0:T(128)S(1)} %fusion.26.base_ref, f32[240,128]{1,0:T(8,128)S(1)} %pad_maximum_fusion.table_ref, f32[1,256]{1,0:T(1,128)S(1)} %bitcast.51, bf16[8,960,768]{2,1,0:T(8,128)(2,1)} %shard_map.104.match_ref, bf16[8,240,256]{2,1,0:T(8,128)(2,1)S(1)} %shard_map.105.refs_0_, ...), custom_call_target="tpu_custom_call" | custom-call | bytes 35000000 | tf_op jit(solution)/shard_map/pallas_call | solution.py:446
  244.0 17.4 %all-gather.4 = f32[16,1,1920]{2,1,0:T(1,128)S(1)} all-gather(f32[1,1,1920]{2,1,0:T(1,128)S(1)} %reshape.41), channel_id=4, replica_groups=mesh['dp'=32,'group'=16] {'group'}, dimensions={0}, use_global_device_ids=true | all-gather | bytes 130560 | tf_op jit(solution)/shard_map/all_gather | solution.py:588
  261.4 0.5 slice.70
  262.4 0.9 copy.43
  263.3 0.9 copy.44
  264.2 0.6 copy.49
  (109 shorter events, 3.8 us)
Async XLA Ops:
  8.0 59.4 %all-gather.8.cloned.1.call-start = ((), (), s32[]{:S(2)}) async-start(), calls=%async_computation.5 | async-start | bytes 3538944 | tf_op jit(solution)/shard_map/all_gather | solution.py:487
  8.7 0.7 copy-start.2
  9.5 0.7 copy-start.4
  11.3 36.5 %all-to-all-start = ((f32[32,1,768]{2,1,0:T(1,128)}), f32[32,1,768]{2,1,0:T(1,128)S(1)}, u32[]{:S(2)}, u32[]{:S(2)}) async-start(f32[32,1,768]{2,1,0:T(1,128)} %copy.33), calls=%async_computation | async-start | bytes 196608 | tf_op jit(solution)/shard_map/all_to_all | solution.py:467
  25.0 85.3 %reduce-scatter.2.cloned.1.call-start = ((), (), s32[]{:S(2)}) async-start(), calls=%async_computation.4 | async-start | bytes 2506752 | tf_op jit(solution)/shard_map/reduce_scatter | solution.py:532
  26.2 23.8 %copy-start.9 = (bf16[768,256]{0,1:T(8,128)(2,1)}, bf16[768,256]{0,1:T(8,128)(2,1)S(1)}, u32[]{:S(2)}) copy-start(bf16[768,256]{0,1:T(8,128)(2,1)S(1)} %copy.31) | copy-start | bytes 1179652
  27.5 22.5 %copy-start.7 = (bf16[768,256]{0,1:T(8,128)(2,1)}, bf16[768,256]{0,1:T(8,128)(2,1)S(1)}, u32[]{:S(2)}) copy-start(bf16[768,256]{0,1:T(8,128)(2,1)S(1)} %copy.32) | copy-start | bytes 1179652
  47.8 2.2 copy-start.20
  48.1 2.0 copy-start.12
  48.1 29.7 %copy-start.14 = (bf16[768,256]{0,1:T(8,128)(2,1)}, bf16[768,256]{0,1:T(8,128)(2,1)S(1)}, u32[]{:S(2)}) copy-start(bf16[768,256]{0,1:T(8,128)(2,1)S(1)} %get-tuple-element.81) | copy-start | bytes 1179652
  57.7 100.2 %all-to-all-start.1 = ((bf16[32,240,256]{2,1,0:T(8,128)(2,1)}), bf16[32,240,256]{2,1,0:T(8,128)(2,1)}, u32[]{:S(2)}, u32[]{:S(2)}) async-start(bf16[32,240,256]{2,1,0:T(8,128)(2,1)} %shard_map.106), calls=%async_computation.2 | async-start | bytes 7864320 | tf_op jit(solution)/shard_map/all_to_all | solution.py:467
  67.3 10.4 %copy-start.26 = (s32[8]{0:T(128)S(1)}, s32[8]{0:T(128)}, u32[]{:S(2)}) copy-start(s32[8]{0:T(128)} %constant.77) | copy-start | bytes 100
  67.4 10.4 %copy-start.27 = (s32[8]{0:T(128)S(1)}, s32[8]{0:T(128)}, u32[]{:S(2)}) copy-start(s32[8]{0:T(128)} %constant.71.clone) | copy-start | bytes 100
  67.4 131.2 %all-gather.10.cloned.1.call-start = ((), (), s32[]{:S(2)}) async-start(), calls=%async_computation.6 | async-start | bytes 2506752 | tf_op jit(solution)/shard_map/all_gather | solution.py:542
  71.2 67.8 %collective-permute-start = (bf16[3072,256]{1,0:T(8,128)(2,1)}, bf16[3072,256]{1,0:T(8,128)(2,1)S(1)}, u32[]{:S(2)}, u32[]{:S(2)}) collective-permute-start(bf16[3072,256]{1,0:T(8,128)(2,1)} %get-tuple-element.48), channel_id=1, source_target_pairs={{0,128},{16,144},{32,160},{48,176},{64,192},{80,208},{96,224},{112... | collective-permute-start | bytes 4718600 | tf_op jit(solution)/shard_map/ppermute | solution.py:484
  74.3 64.7 %collective-permute-start.1 = (bf16[3072,256]{1,0:T(8,128)(2,1)}, bf16[3072,256]{1,0:T(8,128)(2,1)}, u32[]{:S(2)}, u32[]{:S(2)}) collective-permute-start(bf16[3072,256]{1,0:T(8,128)(2,1)} %get-tuple-element.49), channel_id=1, source_target_pairs={{0,384},{16,400},{32,416},{48,432},{64,448},{80,464},{96,480},{112... | collective-permute-start | bytes 4718600 | tf_op jit(solution)/shard_map/ppermute | solution.py:484
  139.0 1.1 copy-start.17
  140.1 17.9 %copy-start.3 = (s32[768,8]{0,1:T(8,128)S(1)}, s32[768,8]{0,1:T(8,128)}, u32[]{:S(2)}) copy-start(s32[768,8]{0,1:T(8,128)} %param.9) | copy-start | bytes 73732
  140.3 0.9 copy-start.1
  141.4 79.8 %collective-permute-start.4 = (bf16[3072,256]{1,0:T(8,128)(2,1)}, bf16[3072,256]{1,0:T(8,128)(2,1)}, u32[]{:S(2)}, u32[]{:S(2)}) collective-permute-start(bf16[3072,256]{1,0:T(8,128)(2,1)} %copy-done.17), channel_id=1, source_target_pairs={{0,128},{16,144},{32,160},{48,176},{64,192},{80,208},{96,224},{112... | collective-permute-start | bytes 4718600 | tf_op jit(solution)/shard_map/ppermute | solution.py:484
  148.2 1.0 copy-start
  149.1 72.2 %collective-permute-start.5 = (bf16[3072,256]{1,0:T(8,128)(2,1)}, bf16[3072,256]{1,0:T(8,128)(2,1)}, u32[]{:S(2)}, u32[]{:S(2)}) collective-permute-start(bf16[3072,256]{1,0:T(8,128)(2,1)} %collective-permute-done.1.refs_1_), channel_id=1, source_target_pairs={{0,384},{16,400},{32,416},{48,432},{64,448},{80,464},{96,480},{112... | collective-permute-start | bytes 4718600 | tf_op jit(solution)/shard_map/ppermute | solution.py:484
  152.6 68.7 %collective-permute-start.2 = (bf16[3072,256]{1,0:T(8,128)(2,1)}, bf16[3072,256]{1,0:T(8,128)(2,1)S(1)}, u32[]{:S(2)}, u32[]{:S(2)}) collective-permute-start(bf16[3072,256]{1,0:T(8,128)(2,1)} %get-tuple-element.48), channel_id=1, source_target_pairs={{0,384},{16,400},{32,416},{48,432},{64,448},{80,464},{96,480},{112... | collective-permute-start | bytes 4718600 | tf_op jit(solution)/shard_map/ppermute | solution.py:484
  154.6 66.6 %collective-permute-start.3 = (bf16[3072,256]{1,0:T(8,128)(2,1)}, bf16[3072,256]{1,0:T(8,128)(2,1)}, u32[]{:S(2)}, u32[]{:S(2)}) collective-permute-start(bf16[3072,256]{1,0:T(8,128)(2,1)} %get-tuple-element.49), channel_id=1, source_target_pairs={{0,128},{16,144},{32,160},{48,176},{64,192},{80,208},{96,224},{112... | collective-permute-start | bytes 4718600 | tf_op jit(solution)/shard_map/ppermute | solution.py:484
  197.7 0.9 copy-start.5
  198.6 3.8 %copy-start.25 = (f32[768]{0:T(1024)S(1)}, f32[768]{0:T(1024)}, u32[]{:S(2)}) copy-start(f32[768]{0:T(1024)} %get-tuple-element.71) | copy-start | bytes 9220
  201.0 5.1 %copy-start.6 = (f32[256,768]{1,0:T(8,128)S(1)}, f32[256,768]{1,0:T(8,128)}, u32[]{:S(2)}) copy-start(f32[256,768]{1,0:T(8,128)} %copy-done.5) | copy-start | bytes 2359300
  201.0 5.1 %copy-start.21 = (f32[768]{0:T(1024)S(1)}, f32[768]{0:T(1024)}, u32[]{:S(2)}) copy-start(f32[768]{0:T(1024)} %copy-done.20) | copy-start | bytes 9220
  201.0 5.1 %copy-start.23 = (f32[256]{0:T(256)S(1)}, f32[256]{0:T(256)}, u32[]{:S(2)}) copy-start(f32[256]{0:T(256)} %get-tuple-element.72) | copy-start | bytes 3076
  202.4 3.7 %copy-start.10 = (bf16[768,256]{0,1:T(8,128)(2,1)S(1)}, bf16[768,256]{0,1:T(8,128)(2,1)}, u32[]{:S(2)}) copy-start(bf16[768,256]{0,1:T(8,128)(2,1)} %copy-done.9) | copy-start | bytes 1179652
  202.4 3.7 %copy-start.13 = (bf16[768,256]{0,1:T(8,128)(2,1)S(1)}, bf16[768,256]{0,1:T(8,128)(2,1)}, u32[]{:S(2)}) copy-start(bf16[768,256]{0,1:T(8,128)(2,1)} %copy-done.12) | copy-start | bytes 1179652
  202.4 3.7 %copy-start.16 = (f32[768,768]{1,0:T(8,128)S(1)}, f32[768,768]{1,0:T(8,128)}, u32[]{:S(2)}) copy-start(f32[768,768]{1,0:T(8,128)} %all-gather.10.cloned.1.call-done) | copy-start | bytes 7077892
  206.1 1.8 copy-start.19
  208.6 21.6 %all-to-all-start.2 = ((f32[32,1,896]{2,1,0:T(1,128)}), f32[32,1,896]{2,1,0:T(1,128)S(1)}, u32[]{:S(2)}, u32[]{:S(2)}) async-start(f32[32,1,896]{2,1,0:T(1,128)} %all_to_all.23), calls=%async_computation.3 | async-start | bytes 229376 | tf_op jit(solution)/shard_map/all_to_all | solution.py:467
  230.8 12.9 %copy-start.8 = (bf16[768,256]{0,1:T(8,128)(2,1)S(1)}, bf16[768,256]{0,1:T(8,128)(2,1)}, u32[]{:S(2)}) copy-start(bf16[768,256]{0,1:T(8,128)(2,1)} %copy-done.7) | copy-start | bytes 1179652
  230.8 12.9 %copy-start.15 = (f32[768,256]{0,1:T(8,128)S(1)}, f32[768,256]{0,1:T(8,128)}, u32[]{:S(2)}) copy-start(f32[768,256]{0,1:T(8,128)} %get-tuple-element.85) | copy-start | bytes 2359300
  243.7 18.3 %copy-start.11 = (bf16[768,256]{0,1:T(8,128)(2,1)S(1)}, bf16[768,256]{0,1:T(8,128)(2,1)}, u32[]{:S(2)}) copy-start(bf16[768,256]{0,1:T(8,128)(2,1)} %copy-done.9) | copy-start | bytes 1179652
  243.7 18.2 %copy-start.18 = (f32[768,256]{0,1:T(8,128)S(1)}, f32[768,256]{0,1:T(8,128)}, u32[]{:S(2)}) copy-start(f32[768,256]{0,1:T(8,128)} %get-tuple-element.83) | copy-start | bytes 2359300
  243.7 18.2 %copy-start.22 = (f32[768]{0:T(1024)S(1)}, f32[768]{0:T(1024)}, u32[]{:S(2)}) copy-start(f32[768]{0:T(1024)} %copy-done.20) | copy-start | bytes 9220
  243.7 18.2 %copy-start.24 = (f32[256]{0:T(256)S(1)}, f32[256]{0:T(256)}, u32[]{:S(2)}) copy-start(f32[256]{0:T(256)} %get-tuple-element.72) | copy-start | bytes 3076
Sparse Core Ops, SparseCore 0:
  10.9 53.8 all-gather.7
Sparse Core Ops, SparseCore 1:
  50.1 60.1 reduce-scatter.1
  140.3 45.4 all-gather.9

commit v4 on v3

--- a/solution.py
+++ b/solution.py
@@ -211,7 +211,7 @@
 def collect(base, first, code, cap, parts):
     n_data, rows = code.shape
     piece = parts[0].shape[1]
-    many = 2
+    many = MANY
     counts = [part.shape[0] // (rows * many) for part in parts]
     starts = [sum(counts[:i]) for i in range(len(counts))]
 
@@ -262,10 +262,11 @@
 def near_scores(scale, pos, owner_t, q_slots, p_slots):
     n_data, cap, piece = q_slots.shape
     negs, rows = owner_t.shape
+    many = 2 * MANY
     return call(
         functools.partial(near_kernel, scale),
-        n_data // MANY,
-        [whole((n_data, rows)), whole((negs, rows)), slab(cap, piece, MANY), slab(cap, piece, MANY)],
+        n_data // many,
+        [whole((n_data, rows)), whole((negs, rows)), slab(cap, piece, many), slab(cap, piece, many)],
         whole((negs, rows)),
         jax.ShapeDtypeStruct((negs, rows), F32),
         9,
@@ -390,10 +391,11 @@
     )(pos, hard, table, q_slots, p_slots)
 
 
-def pair_kernel(scale, spans, base_ref, table_ref, gain_ref, match_ref, *refs):
+def pair_kernel(scale, spans, base_ref, table_ref, gain_ref, match_ref, other_ref, *refs):
     q_refs, (total_ref, pairs_ref, split_ref) = refs[: len(spans)], refs[len(spans) :]
     step = pl.program_id(0)
     many, cap, piece = q_refs[0].shape
+    deep = match_ref.shape[1]
     wide = table_ref.shape[1]
     n_data = wide // 4
 
@@ -409,7 +411,9 @@
         split_ref[...] = split.astype(BF16)
 
     lane = iota((wide, many * 128), 0)
-    wanted = base_ref[step] + iota((wide, many * 128), 1) // 128
+    place = iota((wide, many * 128), 1) // 128
+    half = many // 2
+    wanted = jnp.where(place < half, base_ref[2 * step] + place, base_ref[2 * step + 1] + place - half)
     weights = contract(split_ref[...], one_hot(lane == wanted), 1, 0) * scale
     spread = (lane >= n_data) & (lane % n_data == wanted)
     inverses = contract(split_ref[...], one_hot(spread), 1, 0)
@@ -426,14 +430,16 @@
 
     for place, (low, high) in enumerate(spans):
         pl.when((step >= low) & (step < high))(functools.partial(fill, q_refs[place]))
-    total_ref[...] += contract(pairs_ref[...], match_ref[0], 0, 0)
+    total = contract(pairs_ref[:deep, :], match_ref[0], 0, 0)
+    total_ref[...] += total + contract(pairs_ref[deep:, :], other_ref[0], 0, 0)
 
 
 def pair_grad(scale, base, table, gain, match, parts):
     cap, wide = table.shape
-    steps, deep, rows = match.shape
+    groups, deep, rows = match.shape
     piece = parts[0].shape[2]
-    many = wide // 4 // steps
+    steps, each = groups // 2, wide // 4 // groups
+    many = 2 * each
     ends = [sum(part.shape[0] for part in parts[: i + 1]) // many for i in range(len(parts))]
     spans = list(zip([0] + ends[:-1], ends))
 
@@ -451,16 +457,17 @@
             in_specs=[
                 pl.BlockSpec((cap, wide), lambda i, base_ref: (0, 0)),
                 pl.BlockSpec((1, piece), lambda i, base_ref: (0, 0)),
-                pl.BlockSpec((1, deep, rows), lambda i, base_ref: (base_ref[i] // many, 0, 0)),
+                pl.BlockSpec((1, deep, rows), lambda i, base_ref: (base_ref[2 * i] // each, 0, 0)),
+                pl.BlockSpec((1, deep, rows), lambda i, base_ref: (base_ref[2 * i + 1] // each, 0, 0)),
                 *[part_spec(span) for span in spans],
             ],
             out_specs=pl.BlockSpec((piece, rows), lambda i, base_ref: (0, 0)),
-            scratch_shapes=[pltpu.VMEM((deep, piece), BF16), pltpu.VMEM((cap, wide), BF16)],
+            scratch_shapes=[pltpu.VMEM((2 * deep, piece), BF16), pltpu.VMEM((cap, wide), BF16)],
         ),
         out_shape=jax.ShapeDtypeStruct((piece, rows), F32),
         compiler_params=pltpu.CompilerParams(vmem_limit_bytes=VMEM_LIMIT),
         cost_estimate=cost(10),
-    )(base, table, gain, match, *parts)
+    )(base, table, gain, match, match, *parts)
 
 
 def swap(x, axis):
@@ -511,15 +518,16 @@
     half = q_zero.shape[0] // 2
 
     pos, code = make_tables(owner_t, neg_row.T, n_data)
-    code_got = swap(code, "dp")
 
     q_values = queries.astype(F32)
     p_values = passages.astype(F32)
     squares = jnp.stack(
         [jnp.sum(q_values * q_values, axis=1), jnp.sum(p_values * p_values, axis=1)]
     )
-    squares = jnp.sum(lax.all_gather(squares, "group", axis=0), axis=0)
-    squares, code_got = tied(squares, code_got)
+    squares = swap(jnp.broadcast_to(squares.reshape(1, -1), (n_members, 2 * rows)), "group")
+    squares = jnp.sum(squares, axis=0).reshape(2, rows)
+    squares, code = tied(squares, code)
+    code_got = swap(code, "dp")
     inverses = lax.rsqrt(squares / width + EPSILON)
     q_inverse, p_inverse = inverses[0][:, None], inverses[1][:, None]
     q_normed = q_values * q_inverse
@@ -585,7 +593,7 @@
     final = jnp.concatenate(
         [jnp.sum(q_inner * q_normed, axis=1), jnp.sum(p_inner * p_normed, axis=1), last]
     )
-    final = lax.all_gather(final, "group", axis=0)
+    final = swap(jnp.broadcast_to(final[None, :], (n_members, final.shape[0])), "group")
     means = jnp.sum(final[:, : 2 * rows], axis=0) / width
     q_mean, p_mean = means[:rows, None], means[rows:, None]
     grad_queries = (q_inverse * (q_inner - q_normed * q_mean)).astype(BF16)

time: 278 us -> 272 us (0.978); the launches traced: 274 us -> 271 us
  waiting for transfers between devices: 44 us -> 65.9 us
  blocking collectives: 55.1 us -> 40.4 us
  Pallas kernels: 70.2 us -> 62.9 us
    all_gather x2 -> x0, blocking collectives: 36 us -> none  [the longest x1 18.6 us: local(): squares = jnp.sum(lax.all_gather(squares, 'group', axis=0), axis=0)]
    all_to_all x3 -> x4, waiting for transfers between devices: 0.79 us -> 23.2 us  [swap(): return lax.all_to_all(x, axis, split_axis=0, concat_axis=0, tiled=True)]
    all_to_all x0 -> x1, blocking collectives: none -> 17.7 us  [swap(): return lax.all_to_all(x, axis, split_axis=0, concat_axis=0, tiled=True)]
    reduce_scatter x1, waiting for transfers between devices: 13.6 us -> 0.03 us  [local(): scores = lax.psum_scatter(scores, 'group', scatter_dimension=0, tiled=True)]
    ppermute x6, waiting for transfers between devices: 28.8 us -> 41.9 us  [shift(): return lax.ppermute(value, 'dp', pairs)]
    pallas_call x3, Pallas kernels: 15.4 us -> 11.3 us  [collect(): call(functools.partial(collect_kernel, first, counts), steps, [pl.BlockSp...]
    all_gather x1, blocking collectives: 19.1 us -> 22.8 us  [local(): lax.all_gather(jnp.concatenate([near, stats], axis=1), 'group', axis=0)]
    all_to_all x3 -> x4, starting transfers between devices: 35.8 us -> 33.9 us  [swap(): return lax.all_to_all(x, axis, split_axis=0, concat_axis=0, tiled=True)]
  transfers between devices with their start and end apart: 12 -> 13, of which waited for: 4 -> 5; matrix products, arithmetic and copies ran while one was open for 8% -> 8% of each run, Pallas kernels for 21% -> 19%
where the time goes in v4:
time: 272 us; the launch traced here: 271 us
  waiting for transfers between devices  65.9 us (24%)
  Pallas kernels  62.9 us (23%)
  starting transfers between devices  52.3 us (19%)
  blocking collectives  40.4 us (15%)
  between operations  19.1 us (7%)
  local copies, waits for them, and re-layouts  16.6 us (6%)
  matrix products  8.58 us (3%)
  other arithmetic  5.48 us (2%)
    ppermute x6, waiting for transfers between devices, shift(): return lax.ppermute(value, 'dp', pairs)  41.9 us
    all_to_all x4, starting transfers between devices, swap(): return lax.all_to_all(x, axis, split_axis=0, concat_axis=0, tiled=True)  33.9 us
    all_to_all x4, waiting for transfers between devices, swap(): return lax.all_to_all(x, axis, split_axis=0, concat_axis=0, tiled=True)  23.2 us
    all_gather x1, blocking collectives, local(): lax.all_gather(jnp.concatenate([near, stats], axis=1), 'group', axis=0)  22.8 us
    ppermute x6, starting transfers between devices, shift(): return lax.ppermute(value, 'dp', pairs)  18.2 us
    all_to_all x1, blocking collectives, swap(): return lax.all_to_all(x, axis, split_axis=0, concat_axis=0, tiled=True)  17.7 us
    pallas_call x3, Pallas kernels, collect(): call(functools.partial(collect_kernel, first, counts), steps, [pl.BlockSp...  11.3 us
    pallas_call x1, Pallas kernels, pair_grad(): pl.pallas_call(functools.partial(pair_kernel, scale, spans), grid_spec=pl...  11 us
  transfers between devices with their start and end apart: 13, of which 5 were waited for; matrix products, arithmetic and copies ran while one was open for 8% of the time, Pallas kernels for 19%

profile of v4, /device:TPU:1, one launch (start us, length us, event | category | flops | bytes accessed | tf_op | source)
XLA Modules:
  0.0 271.3 jit_solution(9063120779386949031)
XLA Ops:
  8.1 0.7 all-gather.4.cloned.1.call-update
  8.8 1.2 copy.59
  9.9 1.3 copy.60
  11.5 0.7 broadcast_in_dim.17
  12.2 10.2 %all-to-all-start = ((f32[16,1,1536]{2,1,0:T(1,128)}), f32[16,1,1536]{2,1,0:T(1,128)S(1)}, u32[]{:S(2)}, u32[]{:S(2)}) async-start(f32[16,1,1536]{2,1,0:T(1,128)} %broadcast_in_dim.17), calls=%async_computation | async-start | bytes 196608 | tf_op jit(solution)/shard_map/all_to_all | solution.py:474
  22.8 0.8 broadcast_multiply_fusion.1
  23.5 7.4 %all-to-all-done = f32[16,1,1536]{2,1,0:T(1,128)S(1)} async-done(((f32[16,1,1536]{2,1,0:T(1,128)}), f32[16,1,1536]{2,1,0:T(1,128)S(1)}, u32[]{:S(2)}, u32[]{:S(2)}) %all-to-all-start) | async-done | bytes 98336 | tf_op jit(solution)/shard_map/all_to_all | solution.py:474
  31.3 1.9 convolution_multiply_fusion
  33.2 0.8 copy.63
  34.0 11.3 %all-to-all-start.1 = ((f32[32,1,768]{2,1,0:T(1,128)}), f32[32,1,768]{2,1,0:T(1,128)S(1)}, u32[]{:S(2)}, u32[]{:S(2)}) async-start(f32[32,1,768]{2,1,0:T(1,128)} %copy.63), calls=%async_computation.2 | async-start | bytes 196608 | tf_op jit(solution)/shard_map/all_to_all | solution.py:474
  45.5 9.8 %all-to-all-done.1 = f32[32,1,768]{2,1,0:T(1,128)S(1)} async-done(((f32[32,1,768]{2,1,0:T(1,128)}), f32[32,1,768]{2,1,0:T(1,128)S(1)}, u32[]{:S(2)}, u32[]{:S(2)}) %all-to-all-start.1) | async-done | bytes 98336 | tf_op jit(solution)/shard_map/all_to_all | solution.py:474
  55.3 7.5 %shard_map.106 = bf16[32,240,256]{2,1,0:T(8,128)(2,1)} custom-call(f32[32,768]{1,0:T(8,128)S(1)} %bitcast.39, bf16[768,256]{1,0:T(8,128)(2,1)S(1)} %copy.64.p_ref), custom_call_target="tpu_custom_call" | custom-call | bytes 28000000 | tf_op jit(solution)/shard_map/pallas_call | solution.py:123
  62.7 4.8 %all-to-all-start.2 = ((bf16[32,240,256]{2,1,0:T(8,128)(2,1)}), bf16[32,240,256]{2,1,0:T(8,128)(2,1)}, u32[]{:S(2)}, u32[]{:S(2)}) async-start(bf16[32,240,256]{2,1,0:T(8,128)(2,1)} %shard_map.106), calls=%async_computation.3 | async-start | bytes 7864320 | tf_op jit(solution)/shard_map/all_to_all | solution.py:474
  67.7 3.8 %fusion.28 = (bf16[3072,256]{1,0:T(8,128)(2,1)}, bf16[3072,256]{1,0:T(8,128)(2,1)}) fusion(bf16[6144,256]{1,0:T(8,128)(2,1)} %all-gather.4.cloned.1.call-done.refs_0_), kind=kLoop, calls=%fused_computation.62 | loop fusion | bytes 6291456 | tf_op jit(solution)/shard_map/slice | solution.py:543
  71.5 3.0 %collective-permute-start = (bf16[3072,256]{1,0:T(8,128)(2,1)}, bf16[3072,256]{1,0:T(8,128)(2,1)S(1)}, u32[]{:S(2)}, u32[]{:S(2)}) collective-permute-start(bf16[3072,256]{1,0:T(8,128)(2,1)} %get-tuple-element.48), channel_id=1, source_target_pairs={{0,128},{16,144},{32,160},{48,176},{64,192},{80,208},{96,224},{112... | collective-permute-start | bytes 4718600 | tf_op jit(solution)/shard_map/ppermute | solution.py:491
  74.4 3.5 %collective-permute-start.1 = (bf16[3072,256]{1,0:T(8,128)(2,1)}, bf16[3072,256]{1,0:T(8,128)(2,1)}, u32[]{:S(2)}, u32[]{:S(2)}) collective-permute-start(bf16[3072,256]{1,0:T(8,128)(2,1)} %get-tuple-element.49), channel_id=1, source_target_pairs={{0,384},{16,400},{32,416},{48,432},{64,448},{80,464},{96,480},{112... | collective-permute-start | bytes 4718600 | tf_op jit(solution)/shard_map/ppermute | solution.py:491
  78.2 7.6 %shard_map.103 = (bf16[32,240,256]{2,1,0:T(8,128)(2,1)}, f32[240,32]{1,0:T(8,128)S(1)}) custom-call(s32[32,768]{1,0:T(8,128)S(1)} %get-tuple-element.31.pos_ref, bf16[768,256]{1,0:T(8,128)(2,1)S(1)} %copy.62.q_ref, f32[1,768]{1,0:T(1,128)S(1)} %get-tuple-element.88.inverse_ref), custom_call_target="tpu_custom_call" | custom-call | bytes 31500000 | tf_op jit(solution)/shard_map/pallas_call | solution.py:175
  85.7 7.6 %shard_map.104.match_ref.other_ref = bf16[8,960,768]{2,1,0:T(8,128)(2,1)} custom-call(f32[32,768]{1,0:T(8,128)S(1)} %bitcast.40), custom_call_target="tpu_custom_call" | custom-call | bytes 28000000 | tf_op jit(solution)/shard_map/pallas_call | solution.py:146
  93.3 2.6 shard_map.105.refs_0_
  95.9 41.9 %collective-permute-done.refs_0_ = bf16[3072,256]{1,0:T(8,128)(2,1)S(1)} collective-permute-done((bf16[3072,256]{1,0:T(8,128)(2,1)}, bf16[3072,256]{1,0:T(8,128)(2,1)S(1)}, u32[]{:S(2)}, u32[]{:S(2)}) %collective-permute-start) | collective-permute-done | bytes 1572896 | tf_op jit(solution)/shard_map/ppermute | solution.py:491
  138.0 1.0 copy-done.13
  139.0 0.9 copy-done.1
  140.1 1.9 collective-permute-start.4
  142.1 3.0 %shard_map.108.refs_1_ = bf16[8,240,256]{2,1,0:T(8,128)(2,1)S(1)} custom-call(s32[8]{0:T(128)S(1)} %fusion.26.base_ref, f32[32,768]{1,0:T(8,128)S(1)} %bitcast.42, bf16[3072,256]{1,0:T(8,128)(2,1)} %copy-done.13, bf16[3072,256]{1,0:T(8,128)(2,1)} %collective-permute-done.1.refs_1_), custom_call_target="tpu_custom_call" | custom-call | bytes 8400000 | tf_op jit(solution)/shard_map/pallas_call | solution.py:224
  145.1 1.0 copy-done
  146.1 4.6 %collective-permute-start.5 = (bf16[3072,256]{1,0:T(8,128)(2,1)}, bf16[3072,256]{1,0:T(8,128)(2,1)}, u32[]{:S(2)}, u32[]{:S(2)}) collective-permute-start(bf16[3072,256]{1,0:T(8,128)(2,1)} %collective-permute-done.1.refs_1_), channel_id=1, source_target_pairs={{0,384},{16,400},{32,416},{48,432},{64,448},{80,464},{96,480},{112... | collective-permute-start | bytes 4718600 | tf_op jit(solution)/shard_map/ppermute | solution.py:491
  150.7 1.9 collective-permute-start.2
  152.6 3.4 %collective-permute-start.3 = (bf16[3072,256]{1,0:T(8,128)(2,1)}, bf16[3072,256]{1,0:T(8,128)(2,1)}, u32[]{:S(2)}, u32[]{:S(2)}) collective-permute-start(bf16[3072,256]{1,0:T(8,128)(2,1)} %get-tuple-element.49), channel_id=1, source_target_pairs={{0,128},{16,144},{32,160},{48,176},{64,192},{80,208},{96,224},{112... | collective-permute-start | bytes 4718600 | tf_op jit(solution)/shard_map/ppermute | solution.py:491
  156.0 2.7 %all-to-all-done.2.p_ref = bf16[32,240,256]{2,1,0:T(8,128)(2,1)} async-done(((bf16[32,240,256]{2,1,0:T(8,128)(2,1)}), bf16[32,240,256]{2,1,0:T(8,128)(2,1)}, u32[]{:S(2)}, u32[]{:S(2)}) %all-to-all-start.2) | async-done | bytes 3932192 | tf_op jit(solution)/shard_map/all_to_all | solution.py:474
  158.9 6.0 %shard_map.109 = f32[8,768]{1,0:T(8,128)S(1)} custom-call(s32[32,768]{1,0:T(8,128)S(1)} %get-tuple-element.31.pos_ref, s32[8,768]{1,0:T(8,128)S(1)} %bitcast.45, bf16[32,240,256]{2,1,0:T(8,128)(2,1)} %get-tuple-element.35.q_ref, bf16[32,240,256]{2,1,0:T(8,128)(2,1)} %all-to-all-done.2.p_ref), custom_call_target="tpu_custom_call" | custom-call | bytes 31500000 | tf_op jit(solution)/shard_map/pallas_call | solution.py:266
  164.9 22.8 %all-gather = f32[128,896]{1,0:T(8,128)S(1)} all-gather(f32[8,896]{1,0:T(8,128)S(1)} %select_maximum_fusion), channel_id=2, replica_groups=mesh['dp'=32,'group'=16] {'group'}, dimensions={0}, use_global_device_ids=true | all-gather | bytes 487424 | tf_op jit(solution)/shard_map/all_gather | solution.py:560
  188.1 3.0 %shard_map.111.table_ref = f32[240,32]{1,0:T(8,128)S(1)} custom-call(s32[32,768]{1,0:T(8,128)S(1)} %get-tuple-element.31.pos_ref, f32[32,768]{1,0:T(8,128)S(1)} %get-tuple-element.41.hard_ref), custom_call_target="tpu_custom_call" | custom-call | bytes 17500000 | tf_op jit(solution)/shard_map/pallas_call | solution.py:343
  191.2 0.6 fusion.27
  191.9 8.2 %shard_map.112 = (f32[256,768]{1,0:T(8,128)S(1)}, f32[1,256]{1,0:T(1,128)S(1)}) custom-call(s32[32,768]{1,0:T(8,128)S(1)} %get-tuple-element.31.pos_ref, f32[32,768]{1,0:T(8,128)S(1)} %get-tuple-element.41.hard_ref, f32[240,32]{1,0:T(8,128)S(1)} %shard_map.111.table_ref, bf16[32,240,256]{2,1,0:T(8,128)(2,1)} %get-tuple-element.35.q_ref, ...), custom_call_target="tpu_custom_call" | custom-call | bytes 42000000 | tf_op jit(solution)/shard_map/pallas_call | solution.py:377
  200.1 0.9 copy-done.4
  201.0 2.4 select_reduce_fusion
  204.8 3.6 %fusion.16 = (f32[256]{0:T(256)S(1)}, f32[768,256]{0,1:T(8,128)}) fusion(bf16[768,256]{0,1:T(8,128)(2,1)S(1)} %copy-done.6, f32[768]{0:T(1024)S(1)} %get-tuple-element.77, bf16[768,256]{0,1:T(8,128)(2,1)} %copy-done.10, f32[768,768]{1,0:T(8,128)} %all-gather.6.cloned.1.call-done, f32[768]{0:T(1024)S(1)} %get-tuple-element.79), kind=kOutput, calls=%fused_computation.26 | convolution fusion | flops 305921792 | bytes 3939328 | tf_op jit(solution)/shard_map/dot_general | solution.py:24
  208.4 3.1 %fusion.9 = (f32[768]{0:T(1024)S(1)}, f32[256]{0:T(256)S(1)}, f32[768,256]{0,1:T(8,128)}) fusion(bf16[768,256]{0,1:T(8,128)(2,1)} %copy-done.7, f32[256]{0:T(256)S(1)} %get-tuple-element.80, f32[768]{0:T(1024)S(1)} %get-tuple-element.76, f32[256,768]{1,0:T(8,128)} %copy-done.4, bf16[768,256]{0,1:T(8,128)(2,1)} %copy-done.9, f32[768,768]{1,0:T(8,128)S(1)} %copy-done.12, ...), kind=kOutput, calls=%fused_computation.19 | convolution fusion | flops 306707456 | bytes 4729856 | tf_op jit(solution)/shard_map/dot_general | solution.py:24
  211.5 0.7 all_to_all.33
  212.2 7.6 %all-to-all-start.3 = ((f32[32,1,896]{2,1,0:T(1,128)}), f32[32,1,896]{2,1,0:T(1,128)S(1)}, u32[]{:S(2)}, u32[]{:S(2)}) async-start(f32[32,1,896]{2,1,0:T(1,128)} %all_to_all.33), calls=%async_computation.4 | async-start | bytes 229376 | tf_op jit(solution)/shard_map/all_to_all | solution.py:474
  219.9 5.7 %shard_map.113.refs_2_ = bf16[16,240,256]{2,1,0:T(8,128)(2,1)} custom-call(s32[8]{0:T(128)S(1)} %fusion.26.base_ref, f32[32,768]{1,0:T(8,128)S(1)} %bitcast.43, bf16[3072,256]{1,0:T(8,128)(2,1)S(1)} %collective-permute-done.2.refs_0_, bf16[3072,256]{1,0:T(8,128)(2,1)} %collective-permute-done.3.refs_1_, bf16[3072,256]{1,0:T(8,128)(2,1)} %collective-permute-done.4.refs_2_, ...), custom_call_target="tpu_custom_call" | custom-call | bytes 16800000 | tf_op jit(solution)/shard_map/pallas_call | solution.py:224
  225.6 3.3 %all-to-all-done.3 = f32[32,1,896]{2,1,0:T(1,128)S(1)} async-done(((f32[32,1,896]{2,1,0:T(1,128)}), f32[32,1,896]{2,1,0:T(1,128)S(1)}, u32[]{:S(2)}, u32[]{:S(2)}) %all-to-all-start.3) | async-done | bytes 114720 | tf_op jit(solution)/shard_map/all_to_all | solution.py:474
  229.5 11.0 %shard_map.114 = f32[256,768]{1,0:T(8,128)S(1)} custom-call(s32[8]{0:T(128)S(1)} %fusion.26.base_ref, f32[240,128]{1,0:T(8,128)S(1)} %pad_maximum_fusion.table_ref, f32[1,256]{1,0:T(1,128)S(1)} %bitcast.49, bf16[8,960,768]{2,1,0:T(8,128)(2,1)} %shard_map.104.match_ref.other_ref, bf16[8,960,768]{2,1,0:T(8,128)(2,1)} %shard_map.104.match_ref.other_ref, ...), custom_call_target="tpu_custom_call" | custom-call | bytes 35000000 | tf_op jit(solution)/shard_map/pallas_call | solution.py:452
  240.9 17.7 %all_to_all.43 = f32[16,1,1920]{2,1,0:T(1,128)S(1)} all-to-all(f32[16,1,1920]{2,1,0:T(1,128)S(1)} %broadcast_in_dim.42), channel_id=1, replica_groups=mesh['dp'=32,'group'=16] {'group'}, dimensions={0} | all-to-all | bytes 245760 | tf_op jit(solution)/shard_map/all_to_all | solution.py:474
  258.6 0.5 slice.70
  259.6 0.9 copy.72
  260.5 0.9 copy.73
  261.4 0.6 copy.79
  (91 shorter events, 3.9 us)
Async XLA Ops:
  8.0 14.4 %copy-start.2 = (s32[768,8]{0,1:T(8,128)S(1)}, s32[768,8]{0,1:T(8,128)}, u32[]{:S(2)}) copy-start(s32[768,8]{0,1:T(8,128)} %param.9) | copy-start | bytes 73732
  8.0 14.4 %copy-start.3 = (s32[768,8]{0,1:T(8,128)S(1)}, s32[768,8]{0,1:T(8,128)}, u32[]{:S(2)}) copy-start(s32[768,8]{0,1:T(8,128)} %param.10) | copy-start | bytes 73732
  8.0 59.6 %all-gather.4.cloned.1.call-start = ((), (), s32[]{:S(2)}) async-start(), calls=%async_computation.7 | async-start | bytes 3538944 | tf_op jit(solution)/shard_map/all_gather | solution.py:494
  9.9 52.8 %copy-start.7 = (bf16[768,256]{0,1:T(8,128)(2,1)}, bf16[768,256]{0,1:T(8,128)(2,1)S(1)}, u32[]{:S(2)}) copy-start(bf16[768,256]{0,1:T(8,128)(2,1)S(1)} %copy.59) | copy-start | bytes 1179652
  11.3 21.9 %copy-start.5 = (bf16[768,256]{0,1:T(8,128)(2,1)}, bf16[768,256]{0,1:T(8,128)(2,1)S(1)}, u32[]{:S(2)}) copy-start(bf16[768,256]{0,1:T(8,128)(2,1)S(1)} %copy.60) | copy-start | bytes 1179652
  12.2 18.7 %all-to-all-start = ((f32[16,1,1536]{2,1,0:T(1,128)}), f32[16,1,1536]{2,1,0:T(1,128)S(1)}, u32[]{:S(2)}, u32[]{:S(2)}) async-start(f32[16,1,1536]{2,1,0:T(1,128)} %broadcast_in_dim.17), calls=%async_computation | async-start | bytes 196608 | tf_op jit(solution)/shard_map/all_to_all | solution.py:474
  22.4 73.5 %reduce-scatter.2.cloned.1.call-start = ((), (), s32[]{:S(2)}) async-start(), calls=%async_computation.6 | async-start | bytes 2506752 | tf_op jit(solution)/shard_map/reduce_scatter | solution.py:540
  31.3 14.0 %copy-start.9 = (bf16[768,256]{0,1:T(8,128)(2,1)}, bf16[768,256]{0,1:T(8,128)(2,1)S(1)}, u32[]{:S(2)}) copy-start(bf16[768,256]{0,1:T(8,128)(2,1)S(1)} %get-tuple-element.90) | copy-start | bytes 1179652
  31.3 46.7 %copy-start.10 = (bf16[768,256]{0,1:T(8,128)(2,1)}, bf16[768,256]{0,1:T(8,128)(2,1)S(1)}, u32[]{:S(2)}) copy-start(bf16[768,256]{0,1:T(8,128)(2,1)S(1)} %get-tuple-element.89) | copy-start | bytes 1179652
  34.0 21.3 %all-to-all-start.1 = ((f32[32,1,768]{2,1,0:T(1,128)}), f32[32,1,768]{2,1,0:T(1,128)S(1)}, u32[]{:S(2)}, u32[]{:S(2)}) async-start(f32[32,1,768]{2,1,0:T(1,128)} %copy.63), calls=%async_computation.2 | async-start | bytes 196608 | tf_op jit(solution)/shard_map/all_to_all | solution.py:474
  62.7 96.0 %all-to-all-start.2 = ((bf16[32,240,256]{2,1,0:T(8,128)(2,1)}), bf16[32,240,256]{2,1,0:T(8,128)(2,1)}, u32[]{:S(2)}, u32[]{:S(2)}) async-start(bf16[32,240,256]{2,1,0:T(8,128)(2,1)} %shard_map.106), calls=%async_computation.3 | async-start | bytes 7864320 | tf_op jit(solution)/shard_map/all_to_all | solution.py:474
  67.6 10.4 %copy-start.15 = (s32[8]{0:T(128)S(1)}, s32[8]{0:T(128)}, u32[]{:S(2)}) copy-start(s32[8]{0:T(128)} %constant.77) | copy-start | bytes 100
  67.6 10.4 %copy-start.16 = (s32[8]{0:T(128)S(1)}, s32[8]{0:T(128)}, u32[]{:S(2)}) copy-start(s32[8]{0:T(128)} %constant.71.clone) | copy-start | bytes 100
  67.6 133.4 %all-gather.6.cloned.1.call-start = ((), (), s32[]{:S(2)}) async-start(), calls=%async_computation.8 | async-start | bytes 2506752 | tf_op jit(solution)/shard_map/all_gather | solution.py:550
  71.5 66.4 %collective-permute-start = (bf16[3072,256]{1,0:T(8,128)(2,1)}, bf16[3072,256]{1,0:T(8,128)(2,1)S(1)}, u32[]{:S(2)}, u32[]{:S(2)}) collective-permute-start(bf16[3072,256]{1,0:T(8,128)(2,1)} %get-tuple-element.48), channel_id=1, source_target_pairs={{0,128},{16,144},{32,160},{48,176},{64,192},{80,208},{96,224},{112... | collective-permute-start | bytes 4718600 | tf_op jit(solution)/shard_map/ppermute | solution.py:491
  74.4 63.4 %collective-permute-start.1 = (bf16[3072,256]{1,0:T(8,128)(2,1)}, bf16[3072,256]{1,0:T(8,128)(2,1)}, u32[]{:S(2)}, u32[]{:S(2)}) collective-permute-start(bf16[3072,256]{1,0:T(8,128)(2,1)} %get-tuple-element.49), channel_id=1, source_target_pairs={{0,384},{16,400},{32,416},{48,432},{64,448},{80,464},{96,480},{112... | collective-permute-start | bytes 4718600 | tf_op jit(solution)/shard_map/ppermute | solution.py:491
  137.8 1.1 copy-start.13
  139.0 0.9 copy-start.1
  140.1 79.7 %collective-permute-start.4 = (bf16[3072,256]{1,0:T(8,128)(2,1)}, bf16[3072,256]{1,0:T(8,128)(2,1)}, u32[]{:S(2)}, u32[]{:S(2)}) collective-permute-start(bf16[3072,256]{1,0:T(8,128)(2,1)} %copy-done.13), channel_id=1, source_target_pairs={{0,128},{16,144},{32,160},{48,176},{64,192},{80,208},{96,224},{112... | collective-permute-start | bytes 4718600 | tf_op jit(solution)/shard_map/ppermute | solution.py:491
  145.1 1.0 copy-start
  146.1 73.8 %collective-permute-start.5 = (bf16[3072,256]{1,0:T(8,128)(2,1)}, bf16[3072,256]{1,0:T(8,128)(2,1)}, u32[]{:S(2)}, u32[]{:S(2)}) collective-permute-start(bf16[3072,256]{1,0:T(8,128)(2,1)} %collective-permute-done.1.refs_1_), channel_id=1, source_target_pairs={{0,384},{16,400},{32,416},{48,432},{64,448},{80,464},{96,480},{112... | collective-permute-start | bytes 4718600 | tf_op jit(solution)/shard_map/ppermute | solution.py:491
  150.7 69.2 %collective-permute-start.2 = (bf16[3072,256]{1,0:T(8,128)(2,1)}, bf16[3072,256]{1,0:T(8,128)(2,1)S(1)}, u32[]{:S(2)}, u32[]{:S(2)}) collective-permute-start(bf16[3072,256]{1,0:T(8,128)(2,1)} %get-tuple-element.48), channel_id=1, source_target_pairs={{0,384},{16,400},{32,416},{48,432},{64,448},{80,464},{96,480},{112... | collective-permute-start | bytes 4718600 | tf_op jit(solution)/shard_map/ppermute | solution.py:491
  152.6 67.3 %collective-permute-start.3 = (bf16[3072,256]{1,0:T(8,128)(2,1)}, bf16[3072,256]{1,0:T(8,128)(2,1)}, u32[]{:S(2)}, u32[]{:S(2)}) collective-permute-start(bf16[3072,256]{1,0:T(8,128)(2,1)} %get-tuple-element.49), channel_id=1, source_target_pairs={{0,128},{16,144},{32,160},{48,176},{64,192},{80,208},{96,224},{112... | collective-permute-start | bytes 4718600 | tf_op jit(solution)/shard_map/ppermute | solution.py:491
  200.1 0.9 copy-start.4
  201.0 3.7 %copy-start.6 = (bf16[768,256]{0,1:T(8,128)(2,1)S(1)}, bf16[768,256]{0,1:T(8,128)(2,1)}, u32[]{:S(2)}) copy-start(bf16[768,256]{0,1:T(8,128)(2,1)} %copy-done.5) | copy-start | bytes 1179652
  204.7 3.6 %copy-start.12 = (f32[768,768]{1,0:T(8,128)S(1)}, f32[768,768]{1,0:T(8,128)}, u32[]{:S(2)}) copy-start(f32[768,768]{1,0:T(8,128)} %all-gather.6.cloned.1.call-done) | copy-start | bytes 7077892
  212.2 16.7 %all-to-all-start.3 = ((f32[32,1,896]{2,1,0:T(1,128)}), f32[32,1,896]{2,1,0:T(1,128)S(1)}, u32[]{:S(2)}, u32[]{:S(2)}) async-start(f32[32,1,896]{2,1,0:T(1,128)} %all_to_all.33), calls=%async_computation.4 | async-start | bytes 229376 | tf_op jit(solution)/shard_map/all_to_all | solution.py:474
  229.5 11.1 %copy-start.11 = (f32[768,256]{0,1:T(8,128)S(1)}, f32[768,256]{0,1:T(8,128)}, u32[]{:S(2)}) copy-start(f32[768,256]{0,1:T(8,128)} %get-tuple-element.93) | copy-start | bytes 2359300
  240.6 18.6 %copy-start.8 = (bf16[768,256]{0,1:T(8,128)(2,1)S(1)}, bf16[768,256]{0,1:T(8,128)(2,1)}, u32[]{:S(2)}) copy-start(bf16[768,256]{0,1:T(8,128)(2,1)} %copy-done.7) | copy-start | bytes 1179652
  240.6 18.6 %copy-start.14 = (f32[768,256]{0,1:T(8,128)S(1)}, f32[768,256]{0,1:T(8,128)}, u32[]{:S(2)}) copy-start(f32[768,256]{0,1:T(8,128)} %get-tuple-element.91) | copy-start | bytes 2359300
Sparse Core Ops, SparseCore 0:
  10.9 56.0 all-gather.3
Sparse Core Ops, SparseCore 1:
  33.3 59.9 reduce-scatter.1
  137.9 49.6 all-gather.5

commit v5 on v4

--- a/solution.py
+++ b/solution.py
@@ -518,16 +518,15 @@
     half = q_zero.shape[0] // 2
 
     pos, code = make_tables(owner_t, neg_row.T, n_data)
+    code_got = swap(code, "dp")
 
     q_values = queries.astype(F32)
     p_values = passages.astype(F32)
     squares = jnp.stack(
         [jnp.sum(q_values * q_values, axis=1), jnp.sum(p_values * p_values, axis=1)]
     )
-    squares = swap(jnp.broadcast_to(squares.reshape(1, -1), (n_members, 2 * rows)), "group")
-    squares = jnp.sum(squares, axis=0).reshape(2, rows)
-    squares, code = tied(squares, code)
-    code_got = swap(code, "dp")
+    squares = jnp.sum(lax.all_gather(squares, "group", axis=0), axis=0)
+    squares, code_got = tied(squares, code_got)
     inverses = lax.rsqrt(squares / width + EPSILON)
     q_inverse, p_inverse = inverses[0][:, None], inverses[1][:, None]
     q_normed = q_values * q_inverse
@@ -550,8 +549,7 @@
     scores = lax.all_gather(scores, "group", axis=0, tiled=True)
     q_one_low, q_three_high = torus.shift(q_lower, -1), torus.shift(q_upper, 1)
     q_low, q_high = torus.shift(q_three_low, 1), torus.shift(q_one_high, -1)
-    part_first = collect(base, 2, code_got, cap, [q_three_low, q_one_high])
-    p_slots, stats, part_first = tied(p_slots, stats, part_first)
+    p_slots, stats = tied(p_slots, stats)
 
     near = near_scores(scale, pos, owner_t, q_slots, p_slots)
     share = rows // n_members
@@ -576,7 +574,9 @@
         + pair_gain[0] / my_gain
     )
     last = jnp.concatenate([gain_part, jnp.broadcast_to(losses, (128,))])
-    _, q_one_low, q_three_high, q_low, q_high = tied(last, q_one_low, q_three_high, q_low, q_high)
+    _, q_three_low, q_one_high, q_one_low, q_three_high = tied(
+        last, q_three_low, q_one_high, q_one_low, q_three_high
+    )
     sent = jnp.concatenate([table, inverse, jnp.zeros((-2 * cap % 128, n_data), F32)], axis=0).T
     edge = sent.shape[1]
     sent = jnp.concatenate([sent, jnp.broadcast_to(last[None, :], (n_data, piece + 128))], axis=1)
@@ -585,15 +585,19 @@
     got_weights, got_inverses = got[:, :cap].T, got[:, cap : 2 * cap].T
     table = jnp.concatenate([got_weights] + [got_inverses] * 3, axis=1)
 
-    part_last = collect(base, 4, code_got, cap, [q_one_low, q_three_high, q_low, q_high])
-    parts = [part_zero, part_first, part_last]
+    part_next = collect(
+        base, 2, code_got, cap, [q_three_low, q_one_high, q_one_low, q_three_high]
+    )
+    part_next, q_low, q_high = tied(part_next, q_low, q_high)
+    part_last = collect(base, 6, code_got, cap, [q_low, q_high])
+    parts = [part_zero, part_next, part_last]
     grad_p = batch_grad + pair_grad(scale, base, table, gain_row, match, parts).T
     q_inner = grad_q * my_gain
     p_inner = grad_p * my_gain
     final = jnp.concatenate(
         [jnp.sum(q_inner * q_normed, axis=1), jnp.sum(p_inner * p_normed, axis=1), last]
     )
-    final = swap(jnp.broadcast_to(final[None, :], (n_members, final.shape[0])), "group")
+    final = lax.all_gather(final, "group", axis=0)
     means = jnp.sum(final[:, : 2 * rows], axis=0) / width
     q_mean, p_mean = means[:rows, None], means[rows:, None]
     grad_queries = (q_inverse * (q_inner - q_normed * q_mean)).astype(BF16)

time: 272 us -> 270 us (level)
  waiting for transfers between devices: 65.9 us -> 46.5 us
  blocking collectives: 40.4 us -> 57.7 us
    all_gather x0 -> x2, blocking collectives: none -> 34.8 us  [the longest x1 18.6 us: local(): squares = jnp.sum(lax.all_gather(squares, 'group', axis=0), axis=0)]
    all_to_all x4 -> x3, waiting for transfers between devices: 23.2 us -> 0.29 us  [swap(): return lax.all_to_all(x, axis, split_axis=0, concat_axis=0, tiled=True)]
    all_to_all x1 -> x0, blocking collectives: 17.7 us -> none  [swap(): return lax.all_to_all(x, axis, split_axis=0, concat_axis=0, tiled=True)]
    reduce_scatter x1, waiting for transfers between devices: 0.03 us -> 14.8 us  [local(): scores = lax.psum_scatter(scores, 'group', scatter_dimension=0, tiled=True)]
    ppermute x6, waiting for transfers between devices: 41.9 us -> 30.7 us  [shift(): return lax.ppermute(value, 'dp', pairs)]
    all_to_all x4 -> x3, starting transfers between devices: 33.9 us -> 31.5 us  [swap(): return lax.all_to_all(x, axis, split_axis=0, concat_axis=0, tiled=True)]
    unnamed x41 -> x64, local copies, waits for them, and re-layouts: 8.82 us -> 9.29 us
  transfers between devices with their start and end apart: 13 -> 12, of which waited for: 5 -> 4; matrix products, arithmetic and copies ran while one was open for 8% -> 8% of each run, Pallas kernels for 19% -> 19%
where the time goes in v5:
time: 270 us; the launch traced here: 269 us
  Pallas kernels  62.9 us (23%)
  blocking collectives  57.7 us (21%)
  starting transfers between devices  51.5 us (19%)
  waiting for transfers between devices  46.5 us (17%)
  between operations  19.3 us (7%)
  local copies, waits for them, and re-layouts  16.2 us (6%)
  matrix products  7.9 us (3%)
  other arithmetic  6.63 us (2%)
    all_to_all x3, starting transfers between devices, swap(): return lax.all_to_all(x, axis, split_axis=0, concat_axis=0, tiled=True)  31.5 us
    ppermute x6, waiting for transfers between devices, shift(): return lax.ppermute(value, 'dp', pairs)  30.7 us
    all_gather x1, blocking collectives, local(): lax.all_gather(jnp.concatenate([near, stats], axis=1), 'group', axis=0)  23 us
    ppermute x6, starting transfers between devices, shift(): return lax.ppermute(value, 'dp', pairs)  19.9 us
    all_gather x1, blocking collectives, local(): squares = jnp.sum(lax.all_gather(squares, 'group', axis=0), axis=0)  18.6 us
    all_gather x1, blocking collectives, local(): final = lax.all_gather(final, 'group', axis=0)  16.2 us
    reduce_scatter x1, waiting for transfers between devices, local(): scores = lax.psum_scatter(scores, 'group', scatter_dimension=0, tiled=True)  14.8 us
    pallas_call x3, Pallas kernels, collect(): call(functools.partial(collect_kernel, first, counts), steps, [pl.BlockSp...  11.4 us
  transfers between devices with their start and end apart: 12, of which 4 were waited for; matrix products, arithmetic and copies ran while one was open for 8% of the time, Pallas kernels for 19%

profile of v5, /device:TPU:1, one launch (start us, length us, event | category | flops | bytes accessed | tf_op | source)
XLA Modules:
  0.0 268.7 jit_solution(14308379898617938611)
XLA Ops:
  8.0 0.7 all-gather.8.cloned.1.call-update
  8.7 0.7 copy-done.2
  9.5 0.7 copy-done.4
  10.5 0.7 copy.33
  11.3 13.7 %all-to-all-start = ((f32[32,1,768]{2,1,0:T(1,128)}), f32[32,1,768]{2,1,0:T(1,128)S(1)}, u32[]{:S(2)}, u32[]{:S(2)}) async-start(f32[32,1,768]{2,1,0:T(1,128)} %copy.33), calls=%async_computation | async-start | bytes 196608 | tf_op jit(solution)/shard_map/all_to_all | solution.py:474
  25.0 1.2 copy.31
  26.2 1.3 copy.32
  27.8 18.6 %all-gather.3 = f32[16,2,768]{2,1,0:T(2,128)S(1)} all-gather(f32[1,2,768]{2,1,0:T(2,128)S(1)} %maximum_bitcast_fusion.1), channel_id=2, replica_groups=mesh['dp'=32,'group'=16] {'group'}, dimensions={0}, use_global_device_ids=true | all-gather | bytes 104448 | tf_op jit(solution)/shard_map/all_gather | solution.py:528
  46.5 1.3 broadcast_multiply_fusion.1
  48.1 1.9 convolution_multiply_fusion
  50.2 7.5 %shard_map.106 = bf16[32,240,256]{2,1,0:T(8,128)(2,1)} custom-call(f32[32,768]{1,0:T(8,128)S(1)} %bitcast.41, bf16[768,256]{1,0:T(8,128)(2,1)S(1)} %copy.35.p_ref), custom_call_target="tpu_custom_call" | custom-call | bytes 28000000 | tf_op jit(solution)/shard_map/pallas_call | solution.py:123
  57.7 9.6 %all-to-all-start.1 = ((bf16[32,240,256]{2,1,0:T(8,128)(2,1)}), bf16[32,240,256]{2,1,0:T(8,128)(2,1)}, u32[]{:S(2)}, u32[]{:S(2)}) async-start(bf16[32,240,256]{2,1,0:T(8,128)(2,1)} %shard_map.106), calls=%async_computation.2 | async-start | bytes 7864320 | tf_op jit(solution)/shard_map/all_to_all | solution.py:474
  67.4 3.8 %fusion.28 = (bf16[3072,256]{1,0:T(8,128)(2,1)}, bf16[3072,256]{1,0:T(8,128)(2,1)}) fusion(bf16[6144,256]{1,0:T(8,128)(2,1)} %all-gather.8.cloned.1.call-done.refs_0_), kind=kLoop, calls=%fused_computation.62 | loop fusion | bytes 6291456 | tf_op jit(solution)/shard_map/slice | solution.py:542
  71.2 4.3 %collective-permute-start.1 = (bf16[3072,256]{1,0:T(8,128)(2,1)}, bf16[3072,256]{1,0:T(8,128)(2,1)}, u32[]{:S(2)}, u32[]{:S(2)}) collective-permute-start(bf16[3072,256]{1,0:T(8,128)(2,1)} %get-tuple-element.50), channel_id=1, source_target_pairs={{0,384},{16,400},{32,416},{48,432},{64,448},{80,464},{96,480},{112... | collective-permute-start | bytes 4718600 | tf_op jit(solution)/shard_map/ppermute | solution.py:491
  75.5 1.9 collective-permute-start
  77.7 7.6 %shard_map.104.match_ref.other_ref = bf16[8,960,768]{2,1,0:T(8,128)(2,1)} custom-call(f32[32,768]{1,0:T(8,128)S(1)} %bitcast.42), custom_call_target="tpu_custom_call" | custom-call | bytes 28000000 | tf_op jit(solution)/shard_map/pallas_call | solution.py:146
  85.3 7.5 %shard_map.103 = (bf16[32,240,256]{2,1,0:T(8,128)(2,1)}, f32[240,32]{1,0:T(8,128)S(1)}) custom-call(s32[32,768]{1,0:T(8,128)S(1)} %get-tuple-element.33.pos_ref, bf16[768,256]{1,0:T(8,128)(2,1)S(1)} %copy.34.q_ref, f32[1,768]{1,0:T(1,128)S(1)} %get-tuple-element.84.inverse_ref), custom_call_target="tpu_custom_call" | custom-call | bytes 31500000 | tf_op jit(solution)/shard_map/pallas_call | solution.py:175
  92.8 2.6 shard_map.105.refs_0_
  95.4 14.8 %reduce-scatter.2.cloned.1.call-done.scores_ref = f32[48,768]{1,0:T(8,128)} async-done(((f32[768,768]{1,0:T(8,128)}), f32[48,768]{1,0:T(8,128)}) %reduce-scatter.2.cloned.1.call-update) | async-done | bytes 147472 | tf_op jit(solution)/shard_map/reduce_scatter | solution.py:539
  110.2 24.5 %collective-permute-done.1.refs_1_ = bf16[3072,256]{1,0:T(8,128)(2,1)} collective-permute-done((bf16[3072,256]{1,0:T(8,128)(2,1)}, bf16[3072,256]{1,0:T(8,128)(2,1)}, u32[]{:S(2)}, u32[]{:S(2)}) %collective-permute-start.1) | collective-permute-done | bytes 1572896 | tf_op jit(solution)/shard_map/ppermute | solution.py:491
  134.7 6.2 %collective-permute-done.refs_0_ = bf16[3072,256]{1,0:T(8,128)(2,1)S(1)} collective-permute-done((bf16[3072,256]{1,0:T(8,128)(2,1)}, bf16[3072,256]{1,0:T(8,128)(2,1)S(1)}, u32[]{:S(2)}, u32[]{:S(2)}) %collective-permute-start) | collective-permute-done | bytes 1572896 | tf_op jit(solution)/shard_map/ppermute | solution.py:491
  141.1 0.9 copy-done.1
  142.2 1.9 collective-permute-start.2
  144.1 5.2 %collective-permute-start.3 = (bf16[3072,256]{1,0:T(8,128)(2,1)}, bf16[3072,256]{1,0:T(8,128)(2,1)}, u32[]{:S(2)}, u32[]{:S(2)}) collective-permute-start(bf16[3072,256]{1,0:T(8,128)(2,1)} %get-tuple-element.50), channel_id=1, source_target_pairs={{0,128},{16,144},{32,160},{48,176},{64,192},{80,208},{96,224},{112... | collective-permute-start | bytes 4718600 | tf_op jit(solution)/shard_map/ppermute | solution.py:491
  149.3 3.4 %collective-permute-start.4 = (bf16[3072,256]{1,0:T(8,128)(2,1)S(1)}, bf16[3072,256]{1,0:T(8,128)(2,1)}, u32[]{:S(2)}, u32[]{:S(2)}) collective-permute-start(bf16[3072,256]{1,0:T(8,128)(2,1)S(1)} %collective-permute-done.refs_0_), channel_id=1, source_target_pairs={{0,128},{16,144},{32,160},{48,176},{64,192},{80,208},{96,224},{112... | collective-permute-start | bytes 4718600 | tf_op jit(solution)/shard_map/ppermute | solution.py:491
  152.7 3.1 %collective-permute-start.5 = (bf16[3072,256]{1,0:T(8,128)(2,1)}, bf16[3072,256]{1,0:T(8,128)(2,1)}, u32[]{:S(2)}, u32[]{:S(2)}) collective-permute-start(bf16[3072,256]{1,0:T(8,128)(2,1)} %collective-permute-done.1.refs_1_), channel_id=1, source_target_pairs={{0,384},{16,400},{32,416},{48,432},{64,448},{80,464},{96,480},{112... | collective-permute-start | bytes 4718600 | tf_op jit(solution)/shard_map/ppermute | solution.py:491
  156.3 6.0 %shard_map.108 = f32[8,768]{1,0:T(8,128)S(1)} custom-call(s32[32,768]{1,0:T(8,128)S(1)} %get-tuple-element.33.pos_ref, s32[8,768]{1,0:T(8,128)S(1)} %bitcast.47, bf16[32,240,256]{2,1,0:T(8,128)(2,1)} %get-tuple-element.37.q_ref, bf16[32,240,256]{2,1,0:T(8,128)(2,1)} %all-to-all-done.1.p_ref), custom_call_target="tpu_custom_call" | custom-call | bytes 31500000 | tf_op jit(solution)/shard_map/pallas_call | solution.py:266
  162.3 23.0 %all-gather.1 = f32[128,896]{1,0:T(8,128)S(1)} all-gather(f32[8,896]{1,0:T(8,128)S(1)} %select_maximum_fusion), channel_id=3, replica_groups=mesh['dp'=32,'group'=16] {'group'}, dimensions={0}, use_global_device_ids=true | all-gather | bytes 487424 | tf_op jit(solution)/shard_map/all_gather | solution.py:558
  185.7 3.0 %shard_map.110.table_ref = f32[240,32]{1,0:T(8,128)S(1)} custom-call(s32[32,768]{1,0:T(8,128)S(1)} %get-tuple-element.33.pos_ref, f32[32,768]{1,0:T(8,128)S(1)} %get-tuple-element.41.hard_ref), custom_call_target="tpu_custom_call" | custom-call | bytes 17500000 | tf_op jit(solution)/shard_map/pallas_call | solution.py:343
  188.8 0.7 maximum_bitcast_fusion
  189.5 0.7 fusion.27
  190.2 8.2 %shard_map.111 = (f32[256,768]{1,0:T(8,128)S(1)}, f32[1,256]{1,0:T(1,128)S(1)}) custom-call(s32[32,768]{1,0:T(8,128)S(1)} %get-tuple-element.33.pos_ref, f32[32,768]{1,0:T(8,128)S(1)} %get-tuple-element.41.hard_ref, f32[240,32]{1,0:T(8,128)S(1)} %shard_map.110.table_ref, bf16[32,240,256]{2,1,0:T(8,128)(2,1)} %get-tuple-element.37.q_ref, ...), custom_call_target="tpu_custom_call" | custom-call | bytes 42000000 | tf_op jit(solution)/shard_map/pallas_call | solution.py:377
  198.4 0.9 copy-done.5
  199.3 2.4 select_reduce_fusion
  203.1 3.7 %fusion.16 = (f32[256]{0:T(256)S(1)}, f32[768,256]{0,1:T(8,128)}) fusion(bf16[768,256]{0,1:T(8,128)(2,1)} %copy-done.7, f32[768]{0:T(1024)S(1)} %get-tuple-element.73, bf16[768,256]{0,1:T(8,128)(2,1)} %copy-done.14, f32[768,768]{1,0:T(8,128)} %all-gather.10.cloned.1.call-done, f32[768]{0:T(1024)S(1)} %copy-done.24), kind=kOutput, calls=%fused_computation.26 | convolution fusion | flops 305921792 | bytes 3939328 | tf_op jit(solution)/shard_map/dot_general | solution.py:24
  206.8 2.3 fusion.9
  209.2 0.7 all_to_all.23
  209.9 8.1 %all-to-all-start.2 = ((f32[32,1,896]{2,1,0:T(1,128)}), f32[32,1,896]{2,1,0:T(1,128)S(1)}, u32[]{:S(2)}, u32[]{:S(2)}) async-start(f32[32,1,896]{2,1,0:T(1,128)} %all_to_all.23), calls=%async_computation.3 | async-start | bytes 229376 | tf_op jit(solution)/shard_map/all_to_all | solution.py:474
  218.1 5.7 %shard_map.112.refs_1_ = bf16[16,240,256]{2,1,0:T(8,128)(2,1)} custom-call(s32[8]{0:T(128)S(1)} %fusion.26.base_ref, f32[32,768]{1,0:T(8,128)S(1)} %bitcast.44, bf16[3072,256]{1,0:T(8,128)(2,1)S(1)} %collective-permute-done.refs_0_, bf16[3072,256]{1,0:T(8,128)(2,1)} %collective-permute-done.1.refs_1_, bf16[3072,256]{1,0:T(8,128)(2,1)} %collective-permute-done.2.refs_2_, ...), custom_call_target="tpu_custom_call" | custom-call | bytes 16800000 | tf_op jit(solution)/shard_map/pallas_call | solution.py:224
  223.8 3.0 %shard_map.113.refs_2_ = bf16[8,240,256]{2,1,0:T(8,128)(2,1)S(1)} custom-call(s32[8]{0:T(128)S(1)} %fusion.26.base_ref, f32[32,768]{1,0:T(8,128)S(1)} %bitcast.45, bf16[3072,256]{1,0:T(8,128)(2,1)} %collective-permute-done.4.refs_0_, bf16[3072,256]{1,0:T(8,128)(2,1)} %collective-permute-done.5.refs_1_), custom_call_target="tpu_custom_call" | custom-call | bytes 8400000 | tf_op jit(solution)/shard_map/pallas_call | solution.py:224
  226.9 1.0 copy-done
  228.4 11.1 %shard_map.114 = f32[256,768]{1,0:T(8,128)S(1)} custom-call(s32[8]{0:T(128)S(1)} %fusion.26.base_ref, f32[240,128]{1,0:T(8,128)S(1)} %pad_maximum_fusion.table_ref, f32[1,256]{1,0:T(1,128)S(1)} %bitcast.51, bf16[8,960,768]{2,1,0:T(8,128)(2,1)} %shard_map.104.match_ref.other_ref, bf16[8,960,768]{2,1,0:T(8,128)(2,1)} %shard_map.104.match_ref.other_ref, ...), custom_call_target="tpu_custom_call" | custom-call | bytes 35000000 | tf_op jit(solution)/shard_map/pallas_call | solution.py:452
  239.9 16.2 %all-gather.4 = f32[16,1,1920]{2,1,0:T(1,128)S(1)} all-gather(f32[1,1,1920]{2,1,0:T(1,128)S(1)} %reshape.41), channel_id=4, replica_groups=mesh['dp'=32,'group'=16] {'group'}, dimensions={0}, use_global_device_ids=true | all-gather | bytes 130560 | tf_op jit(solution)/shard_map/all_gather | solution.py:600
  256.0 0.5 slice.70
  256.6 0.6 copy.49
  257.2 0.4 fusion.13
  257.7 0.9 copy.43
  258.6 0.9 copy.44
  (109 shorter events, 3.6 us)
Async XLA Ops:
  8.0 59.4 %all-gather.8.cloned.1.call-start = ((), (), s32[]{:S(2)}) async-start(), calls=%async_computation.5 | async-start | bytes 3538944 | tf_op jit(solution)/shard_map/all_gather | solution.py:494
  8.7 0.7 copy-start.2
  9.5 0.7 copy-start.4
  11.3 36.5 %all-to-all-start = ((f32[32,1,768]{2,1,0:T(1,128)}), f32[32,1,768]{2,1,0:T(1,128)S(1)}, u32[]{:S(2)}, u32[]{:S(2)}) async-start(f32[32,1,768]{2,1,0:T(1,128)} %copy.33), calls=%async_computation | async-start | bytes 196608 | tf_op jit(solution)/shard_map/all_to_all | solution.py:474
  25.0 85.2 %reduce-scatter.2.cloned.1.call-start = ((), (), s32[]{:S(2)}) async-start(), calls=%async_computation.4 | async-start | bytes 2506752 | tf_op jit(solution)/shard_map/reduce_scatter | solution.py:539
  26.2 23.8 %copy-start.9 = (bf16[768,256]{0,1:T(8,128)(2,1)}, bf16[768,256]{0,1:T(8,128)(2,1)S(1)}, u32[]{:S(2)}) copy-start(bf16[768,256]{0,1:T(8,128)(2,1)S(1)} %copy.31) | copy-start | bytes 1179652
  27.5 22.5 %copy-start.7 = (bf16[768,256]{0,1:T(8,128)(2,1)}, bf16[768,256]{0,1:T(8,128)(2,1)S(1)}, u32[]{:S(2)}) copy-start(bf16[768,256]{0,1:T(8,128)(2,1)S(1)} %copy.32) | copy-start | bytes 1179652
  47.8 2.2 copy-start.19
  48.1 2.0 copy-start.12
  48.1 29.4 %copy-start.14 = (bf16[768,256]{0,1:T(8,128)(2,1)}, bf16[768,256]{0,1:T(8,128)(2,1)S(1)}, u32[]{:S(2)}) copy-start(bf16[768,256]{0,1:T(8,128)(2,1)S(1)} %get-tuple-element.85) | copy-start | bytes 1179652
  57.7 98.4 %all-to-all-start.1 = ((bf16[32,240,256]{2,1,0:T(8,128)(2,1)}), bf16[32,240,256]{2,1,0:T(8,128)(2,1)}, u32[]{:S(2)}, u32[]{:S(2)}) async-start(bf16[32,240,256]{2,1,0:T(8,128)(2,1)} %shard_map.106), calls=%async_computation.2 | async-start | bytes 7864320 | tf_op jit(solution)/shard_map/all_to_all | solution.py:474
  67.3 10.2 %copy-start.26 = (s32[8]{0:T(128)S(1)}, s32[8]{0:T(128)}, u32[]{:S(2)}) copy-start(s32[8]{0:T(128)} %constant.77) | copy-start | bytes 100
  67.3 10.2 %copy-start.27 = (s32[8]{0:T(128)S(1)}, s32[8]{0:T(128)}, u32[]{:S(2)}) copy-start(s32[8]{0:T(128)} %constant.71.clone) | copy-start | bytes 100
  67.4 131.9 %all-gather.10.cloned.1.call-start = ((), (), s32[]{:S(2)}) async-start(), calls=%async_computation.6 | async-start | bytes 2506752 | tf_op jit(solution)/shard_map/all_gather | solution.py:549
  71.2 63.5 %collective-permute-start.1 = (bf16[3072,256]{1,0:T(8,128)(2,1)}, bf16[3072,256]{1,0:T(8,128)(2,1)}, u32[]{:S(2)}, u32[]{:S(2)}) collective-permute-start(bf16[3072,256]{1,0:T(8,128)(2,1)} %get-tuple-element.50), channel_id=1, source_target_pairs={{0,384},{16,400},{32,416},{48,432},{64,448},{80,464},{96,480},{112... | collective-permute-start | bytes 4718600 | tf_op jit(solution)/shard_map/ppermute | solution.py:491
  75.5 65.3 %collective-permute-start = (bf16[3072,256]{1,0:T(8,128)(2,1)}, bf16[3072,256]{1,0:T(8,128)(2,1)S(1)}, u32[]{:S(2)}, u32[]{:S(2)}) collective-permute-start(bf16[3072,256]{1,0:T(8,128)(2,1)} %get-tuple-element.49), channel_id=1, source_target_pairs={{0,128},{16,144},{32,160},{48,176},{64,192},{80,208},{96,224},{112... | collective-permute-start | bytes 4718600 | tf_op jit(solution)/shard_map/ppermute | solution.py:491
  92.8 63.5 %copy-start.3 = (s32[768,8]{0,1:T(8,128)S(1)}, s32[768,8]{0,1:T(8,128)}, u32[]{:S(2)}) copy-start(s32[768,8]{0,1:T(8,128)} %param.9) | copy-start | bytes 73732
  141.1 0.9 copy-start.1
  142.2 75.9 %collective-permute-start.2 = (bf16[3072,256]{1,0:T(8,128)(2,1)}, bf16[3072,256]{1,0:T(8,128)(2,1)}, u32[]{:S(2)}, u32[]{:S(2)}) collective-permute-start(bf16[3072,256]{1,0:T(8,128)(2,1)} %get-tuple-element.49), channel_id=1, source_target_pairs={{0,384},{16,400},{32,416},{48,432},{64,448},{80,464},{96,480},{112... | collective-permute-start | bytes 4718600 | tf_op jit(solution)/shard_map/ppermute | solution.py:491
  144.1 74.0 %collective-permute-start.3 = (bf16[3072,256]{1,0:T(8,128)(2,1)}, bf16[3072,256]{1,0:T(8,128)(2,1)}, u32[]{:S(2)}, u32[]{:S(2)}) collective-permute-start(bf16[3072,256]{1,0:T(8,128)(2,1)} %get-tuple-element.50), channel_id=1, source_target_pairs={{0,128},{16,144},{32,160},{48,176},{64,192},{80,208},{96,224},{112... | collective-permute-start | bytes 4718600 | tf_op jit(solution)/shard_map/ppermute | solution.py:491
  149.3 74.5 %collective-permute-start.4 = (bf16[3072,256]{1,0:T(8,128)(2,1)S(1)}, bf16[3072,256]{1,0:T(8,128)(2,1)}, u32[]{:S(2)}, u32[]{:S(2)}) collective-permute-start(bf16[3072,256]{1,0:T(8,128)(2,1)S(1)} %collective-permute-done.refs_0_), channel_id=1, source_target_pairs={{0,128},{16,144},{32,160},{48,176},{64,192},{80,208},{96,224},{112... | collective-permute-start | bytes 4718600 | tf_op jit(solution)/shard_map/ppermute | solution.py:491
  152.7 71.1 %collective-permute-start.5 = (bf16[3072,256]{1,0:T(8,128)(2,1)}, bf16[3072,256]{1,0:T(8,128)(2,1)}, u32[]{:S(2)}, u32[]{:S(2)}) collective-permute-start(bf16[3072,256]{1,0:T(8,128)(2,1)} %collective-permute-done.1.refs_1_), channel_id=1, source_target_pairs={{0,384},{16,400},{32,416},{48,432},{64,448},{80,464},{96,480},{112... | collective-permute-start | bytes 4718600 | tf_op jit(solution)/shard_map/ppermute | solution.py:491
  198.4 0.9 copy-start.5
  199.3 3.8 %copy-start.24 = (f32[768]{0:T(1024)S(1)}, f32[768]{0:T(1024)}, u32[]{:S(2)}) copy-start(f32[768]{0:T(1024)} %get-tuple-element.75) | copy-start | bytes 9220
  201.7 5.1 %copy-start.6 = (f32[256,768]{1,0:T(8,128)S(1)}, f32[256,768]{1,0:T(8,128)}, u32[]{:S(2)}) copy-start(f32[256,768]{1,0:T(8,128)} %copy-done.5) | copy-start | bytes 2359300
  201.7 5.1 %copy-start.20 = (f32[768]{0:T(1024)S(1)}, f32[768]{0:T(1024)}, u32[]{:S(2)}) copy-start(f32[768]{0:T(1024)} %copy-done.19) | copy-start | bytes 9220
  201.7 5.1 %copy-start.22 = (f32[256]{0:T(256)S(1)}, f32[256]{0:T(256)}, u32[]{:S(2)}) copy-start(f32[256]{0:T(256)} %get-tuple-element.76) | copy-start | bytes 3076
  203.0 3.7 %copy-start.10 = (bf16[768,256]{0,1:T(8,128)(2,1)S(1)}, bf16[768,256]{0,1:T(8,128)(2,1)}, u32[]{:S(2)}) copy-start(bf16[768,256]{0,1:T(8,128)(2,1)} %copy-done.9) | copy-start | bytes 1179652
  203.0 3.7 %copy-start.13 = (bf16[768,256]{0,1:T(8,128)(2,1)S(1)}, bf16[768,256]{0,1:T(8,128)(2,1)}, u32[]{:S(2)}) copy-start(bf16[768,256]{0,1:T(8,128)(2,1)} %copy-done.12) | copy-start | bytes 1179652
  203.0 3.7 %copy-start.16 = (f32[768,768]{1,0:T(8,128)S(1)}, f32[768,768]{1,0:T(8,128)}, u32[]{:S(2)}) copy-start(f32[768,768]{1,0:T(8,128)} %all-gather.10.cloned.1.call-done) | copy-start | bytes 7077892
  206.8 2.4 copy-start.18
  209.9 17.9 %all-to-all-start.2 = ((f32[32,1,896]{2,1,0:T(1,128)}), f32[32,1,896]{2,1,0:T(1,128)S(1)}, u32[]{:S(2)}, u32[]{:S(2)}) async-start(f32[32,1,896]{2,1,0:T(1,128)} %all_to_all.23), calls=%async_computation.3 | async-start | bytes 229376 | tf_op jit(solution)/shard_map/all_to_all | solution.py:474
  226.9 1.0 copy-start
  228.4 11.2 %copy-start.8 = (bf16[768,256]{0,1:T(8,128)(2,1)S(1)}, bf16[768,256]{0,1:T(8,128)(2,1)}, u32[]{:S(2)}) copy-start(bf16[768,256]{0,1:T(8,128)(2,1)} %copy-done.7) | copy-start | bytes 1179652
  228.4 11.2 %copy-start.15 = (f32[768,256]{0,1:T(8,128)S(1)}, f32[768,256]{0,1:T(8,128)}, u32[]{:S(2)}) copy-start(f32[768,256]{0,1:T(8,128)} %get-tuple-element.89) | copy-start | bytes 2359300
  228.4 11.4 %copy-start.25 = (f32[768]{0:T(1024)S(1)}, f32[768]{0:T(1024)}, u32[]{:S(2)}) copy-start(f32[768]{0:T(1024)} %get-tuple-element.70) | copy-start | bytes 9220
  239.5 17.7 %copy-start.11 = (bf16[768,256]{0,1:T(8,128)(2,1)S(1)}, bf16[768,256]{0,1:T(8,128)(2,1)}, u32[]{:S(2)}) copy-start(bf16[768,256]{0,1:T(8,128)(2,1)} %copy-done.9) | copy-start | bytes 1179652
  239.5 17.7 %copy-start.17 = (f32[768,256]{0,1:T(8,128)S(1)}, f32[768,256]{0,1:T(8,128)}, u32[]{:S(2)}) copy-start(f32[768,256]{0,1:T(8,128)} %get-tuple-element.87) | copy-start | bytes 2359300
  239.5 17.7 %copy-start.21 = (f32[768]{0:T(1024)S(1)}, f32[768]{0:T(1024)}, u32[]{:S(2)}) copy-start(f32[768]{0:T(1024)} %copy-done.19) | copy-start | bytes 9220
  239.5 17.7 %copy-start.23 = (f32[256]{0:T(256)S(1)}, f32[256]{0:T(256)}, u32[]{:S(2)}) copy-start(f32[256]{0:T(256)} %get-tuple-element.76) | copy-start | bytes 3076
Sparse Core Ops, SparseCore 0:
  10.9 53.8 all-gather.7
Sparse Core Ops, SparseCore 1:
  50.1 60.1 reduce-scatter.1
  141.0 46.0 all-gather.9
